TPU v7x, 32 devices: a whole 2x2x4 slice. The times are simulated.
32 devices in a mesh: tile: 16 (over z, x, core), tm: 2 (over y).
Axes of the slice: x: 2, y: 2, z: 4, core: 2. Of those that a mesh axis runs over, the one named last changes fastest.
Arguments:
- controls: float32 [4, 128, 8, 512], P('tm', 'tile'), may hold values from -6 to 6
- perturbations: bfloat16 [2, 4, 4, 128, 8, 512], P('tm', None, None, 'tile'), may hold values from -6 to 6
- owner: int32 [4], replicated, may hold values from 0 to 3, each once
- land_mask: int32 [128, 512], P('tile'), may hold values 0 or 1
- diffusivity: float32 [2, 8], replicated, may hold values from 0.2 to 0.24
Outputs:
- increment: float32 [2, 4, 128, 8, 512], P('tm', None, 'tile')
Inputs may be any that keep to these rules, and one draw needn't show every extreme that they name: owner names every member exactly once.
All inputs are finite; a program needn't handle non-finite values. No bound on the sum of `land_mask` on one device may be relied on, other than what follows from the above.
Results may differ from a plain program's by a relative error of at most 0.0029.
Values may be sent and summed in bfloat16 or wider, within the bound.
No kernel may reach another device: no remote copies, remote signals or barrier semaphores. Data moves between devices by JAX's collectives and lax.ppermute only.
A program may use at most 64 MiB of HBM per device.

v0:
```python
import math

import jax
import jax.numpy as jnp
from jax import lax
from jax.sharding import PartitionSpec as P

SWEEPS = 4


def with_halo(cells, sides, width):
    for axis, dim in sides:
        count = lax.axis_size(axis)
        ends = count - 1
        head = lax.slice_in_dim(cells, 0, width, axis=dim)
        tail = lax.slice_in_dim(cells, cells.shape[dim] - width, cells.shape[dim], axis=dim)
        cells = jnp.concatenate(
            [
                lax.ppermute(tail, axis, [(i, (i + 1) % count) for i in range(ends)]),
                cells,
                lax.ppermute(head, axis, [((i + 1) % count, i) for i in range(ends)]),
            ],
            axis=dim,
        )
    return cells


def spread(value, axis, source):
    kept = jnp.where(lax.axis_index(axis) == source, value, 0).astype(value.dtype)
    return lax.psum(kept, axis)


def weight_sweep(field, coef):
    padded = jnp.pad(field, ((0, 0), (1, 1), (0, 0), (1, 1)))
    coef_pad = jnp.pad(coef, ((1, 1), (0, 0), (1, 1)))
    flux = 0.5 * (coef + coef_pad[:-2, :, 1:-1]) * (padded[:, :-2, :, 1:-1] - field)
    flux = flux + 0.5 * (coef + coef_pad[2:, :, 1:-1]) * (padded[:, 2:, :, 1:-1] - field)
    flux = flux + 0.5 * (coef + coef_pad[1:-1, :, :-2]) * (padded[:, 1:-1, :, :-2] - field)
    flux = flux + 0.5 * (coef + coef_pad[1:-1, :, 2:]) * (padded[:, 1:-1, :, 2:] - field)
    return field + flux


def on_device(controls, perturbations, owner, land_mask, diffusivity):
    diffuse_coef = jnp.where(
        land_mask[:, None, :] == 1, diffusivity[1][None, :, None], diffusivity[0][None, :, None]
    )
    rim_rows = 1
    coef_wide = with_halo(diffuse_coef, (("tile", 0),), rim_rows)
    smooth = controls
    for sweep_index in range(SWEEPS):
        extended = with_halo(smooth, (("tile", 1),), 1)
        smooth = weight_sweep(extended, coef_wide)[:, 1:-1]
    weights = smooth.astype(jnp.bfloat16)
    member_count = owner.shape[0]
    pert_here = perturbations[0]
    factor = 1.0 / math.sqrt(member_count - 1)
    pair_count = controls.shape[0]
    summed = jnp.zeros(pert_here.shape[1:], jnp.float32)
    for root_index in range(lax.axis_size("tm")):
        arrived = spread(weights, "tm", root_index)
        chosen = lax.dynamic_slice_in_dim(owner, root_index * pair_count, pair_count)
        selected = jnp.take(pert_here, chosen, axis=0)
        summed = summed + jnp.einsum(
            "pvxly,pxly->vxly", selected, arrived, preferred_element_type=jnp.float32
        )
    return (summed * factor)[None]


def solution(mesh):
    return jax.shard_map(
        on_device,
        mesh=mesh,
        in_specs=(
            P("tm", "tile", None, None),
            P("tm", None, None, "tile", None, None),
            P(),
            P("tile", None),
            P(),
        ),
        out_specs=P("tm", None, "tile", None, None),
        check_vma=False,
    )
```

profile of v0, /device:TPU:0, one launch (start us, length us, event | category | flops | bytes accessed | tf_op | source)
XLA Modules:
  0.0 86.1 jit_solution(7496322621619128020)
XLA Ops:
  6.5 0.8 slice_bitcast_fusion.1
  7.3 0.7 broadcast_compare_fusion
  8.1 2.4 %collective-permute-start.2 = (f32[1,8,512]{2,1,0:T(8,128)S(1)}, f32[1,8,512]{2,1,0:T(8,128)S(1)}, u32[]{:S(2)}, u32[]{:S(2)}) collective-permute-start(f32[1,8,512]{2,1,0:T(8,128)S(1)} %get-tuple-element.30), channel_id=1, source_target_pairs={{0,2},{2,4},{4,6},{6,8},{8,10},{10,12},{12,14},{14,16},{16,18},{18... | collective-permute-start | bytes 49160 | tf_op jit(solution)/shard_map/ppermute | solution.py:19
  10.5 1.3 %collective-permute-start.3 = (f32[1,8,512]{2,1,0:T(8,128)S(1)}, f32[1,8,512]{2,1,0:T(8,128)S(1)}, u32[]{:S(2)}, u32[]{:S(2)}) collective-permute-start(f32[1,8,512]{2,1,0:T(8,128)S(1)} %get-tuple-element.31), channel_id=1, source_target_pairs={{2,0},{4,2},{6,4},{8,6},{10,8},{12,10},{14,12},{16,14},{18,16},{20... | collective-permute-start | bytes 49160 | tf_op jit(solution)/shard_map/ppermute | solution.py:21
  11.8 0.8 fusion.57
  12.6 5.1 %collective-permute-start = (f32[2,1,8,512]{3,2,1,0:T(8,128)S(1)}, f32[2,1,8,512]{3,2,1,0:T(8,128)S(1)}, u32[]{:S(2)}, u32[]{:S(2)}) collective-permute-start(f32[2,1,8,512]{3,2,1,0:T(8,128)S(1)} %get-tuple-element.25), channel_id=1, source_target_pairs={{0,2},{2,4},{4,6},{6,8},{8,10},{10,12},{12,14},{14,16},{16,18},{18... | collective-permute-start | bytes 98312 | tf_op jit(solution)/shard_map/ppermute | solution.py:19
  17.7 1.3 %collective-permute-start.1 = (f32[2,1,8,512]{3,2,1,0:T(8,128)S(1)}, f32[2,1,8,512]{3,2,1,0:T(8,128)S(1)}, u32[]{:S(2)}, u32[]{:S(2)}) collective-permute-start(f32[2,1,8,512]{3,2,1,0:T(8,128)S(1)} %get-tuple-element.24), channel_id=1, source_target_pairs={{2,0},{4,2},{6,4},{8,6},{10,8},{12,10},{14,12},{16,14},{18,16},{20... | collective-permute-start | bytes 98312 | tf_op jit(solution)/shard_map/ppermute | solution.py:21
  19.3 0.8 copy-done.1
  20.0 2.0 %collective-permute-done.1 = f32[2,1,8,512]{3,2,1,0:T(8,128)S(1)} collective-permute-done((f32[2,1,8,512]{3,2,1,0:T(8,128)S(1)}, f32[2,1,8,512]{3,2,1,0:T(8,128)S(1)}, u32[]{:S(2)}, u32[]{:S(2)}) %collective-permute-start.1) | collective-permute-done | bytes 32800 | tf_op jit(solution)/shard_map/ppermute | solution.py:21
  22.4 4.5 %collective-permute-start.4 = (f32[2,1,8,512]{3,2,1,0:T(8,128)S(1)}, f32[2,1,8,512]{3,2,1,0:T(8,128)S(1)}, u32[]{:S(2)}, u32[]{:S(2)}) collective-permute-start(f32[2,1,8,512]{3,2,1,0:T(8,128)S(1)} %get-tuple-element.22), channel_id=1, source_target_pairs={{0,2},{2,4},{4,6},{6,8},{8,10},{10,12},{12,14},{14,16},{16,18},{18... | collective-permute-start | bytes 98312 | tf_op jit(solution)/shard_map/ppermute | solution.py:19
  26.9 1.3 %collective-permute-start.5 = (f32[2,1,8,512]{3,2,1,0:T(8,128)S(1)}, f32[2,1,8,512]{3,2,1,0:T(8,128)S(1)}, u32[]{:S(2)}, u32[]{:S(2)}) collective-permute-start(f32[2,1,8,512]{3,2,1,0:T(8,128)S(1)} %get-tuple-element.23), channel_id=1, source_target_pairs={{2,0},{4,2},{6,4},{8,6},{10,8},{12,10},{14,12},{16,14},{18,16},{20... | collective-permute-start | bytes 98312 | tf_op jit(solution)/shard_map/ppermute | solution.py:21
  28.2 1.8 %collective-permute-done.5 = f32[2,1,8,512]{3,2,1,0:T(8,128)S(1)} collective-permute-done((f32[2,1,8,512]{3,2,1,0:T(8,128)S(1)}, f32[2,1,8,512]{3,2,1,0:T(8,128)S(1)}, u32[]{:S(2)}, u32[]{:S(2)}) %collective-permute-start.5) | collective-permute-done | bytes 32800 | tf_op jit(solution)/shard_map/ppermute | solution.py:21
  30.3 5.8 %collective-permute-start.6 = (f32[2,1,8,512]{3,2,1,0:T(8,128)S(1)}, f32[2,1,8,512]{3,2,1,0:T(8,128)S(1)}, u32[]{:S(2)}, u32[]{:S(2)}) collective-permute-start(f32[2,1,8,512]{3,2,1,0:T(8,128)S(1)} %get-tuple-element.20), channel_id=1, source_target_pairs={{0,2},{2,4},{4,6},{6,8},{8,10},{10,12},{12,14},{14,16},{16,18},{18... | collective-permute-start | bytes 98312 | tf_op jit(solution)/shard_map/ppermute | solution.py:19
  36.1 1.3 %collective-permute-start.7 = (f32[2,1,8,512]{3,2,1,0:T(8,128)S(1)}, f32[2,1,8,512]{3,2,1,0:T(8,128)S(1)}, u32[]{:S(2)}, u32[]{:S(2)}) collective-permute-start(f32[2,1,8,512]{3,2,1,0:T(8,128)S(1)} %get-tuple-element.21), channel_id=1, source_target_pairs={{2,0},{4,2},{6,4},{8,6},{10,8},{12,10},{14,12},{16,14},{18,16},{20... | collective-permute-start | bytes 98312 | tf_op jit(solution)/shard_map/ppermute | solution.py:21
  37.4 1.8 %collective-permute-done.7 = f32[2,1,8,512]{3,2,1,0:T(8,128)S(1)} collective-permute-done((f32[2,1,8,512]{3,2,1,0:T(8,128)S(1)}, f32[2,1,8,512]{3,2,1,0:T(8,128)S(1)}, u32[]{:S(2)}, u32[]{:S(2)}) %collective-permute-start.7) | collective-permute-done | bytes 32800 | tf_op jit(solution)/shard_map/ppermute | solution.py:21
  39.5 5.0 %collective-permute-start.8 = (f32[2,1,8,512]{3,2,1,0:T(8,128)S(1)}, f32[2,1,8,512]{3,2,1,0:T(8,128)S(1)}, u32[]{:S(2)}, u32[]{:S(2)}) collective-permute-start(f32[2,1,8,512]{3,2,1,0:T(8,128)S(1)} %get-tuple-element.18), channel_id=1, source_target_pairs={{0,2},{2,4},{4,6},{6,8},{8,10},{10,12},{12,14},{14,16},{16,18},{18... | collective-permute-start | bytes 98312 | tf_op jit(solution)/shard_map/ppermute | solution.py:19
  44.5 1.3 %collective-permute-start.9 = (f32[2,1,8,512]{3,2,1,0:T(8,128)S(1)}, f32[2,1,8,512]{3,2,1,0:T(8,128)S(1)}, u32[]{:S(2)}, u32[]{:S(2)}) collective-permute-start(f32[2,1,8,512]{3,2,1,0:T(8,128)S(1)} %get-tuple-element.19), channel_id=1, source_target_pairs={{2,0},{4,2},{6,4},{8,6},{10,8},{12,10},{14,12},{16,14},{18,16},{20... | collective-permute-start | bytes 98312 | tf_op jit(solution)/shard_map/ppermute | solution.py:21
  45.9 1.7 %collective-permute-done.9 = f32[2,1,8,512]{3,2,1,0:T(8,128)S(1)} collective-permute-done((f32[2,1,8,512]{3,2,1,0:T(8,128)S(1)}, f32[2,1,8,512]{3,2,1,0:T(8,128)S(1)}, u32[]{:S(2)}, u32[]{:S(2)}) %collective-permute-start.9) | collective-permute-done | bytes 32800 | tf_op jit(solution)/shard_map/ppermute | solution.py:21
  47.9 0.9 %broadcast_select_fusion = (bf16[2,8,8,512]{3,2,1,0:T(8,128)(2,1)}, bf16[2,8,8,512]{3,2,1,0:T(8,128)(2,1)S(1)}) fusion(pred[]{:T(512)S(6)} %eq.16, f32[2,10,8,512]{3,2,1,0:T(8,128)S(1)} %get-tuple-element.15, f32[8,8,512]{2,1,0:T(8,128)S(1)} %slice.186, f32[2,10,8,512]{3,2,1,0:T(8,128)S(1)} %get-tuple-element.17, f32[8,8,512]{2,1,0:T(8,128)S(1)} %slice.184, ...), kind=kLoop, calls=%fused_computation.88 | loop fusion | flops 786432 | bytes 2097153 | tf_op jit(solution)/shard_map/jit(_where)/select_n | solution.py:29
  48.7 0.7 broadcast_select_fusion.1
  49.4 0.6 copy-done.2
  51.3 25.6 %all-reduce.8.cloned.1.call-done = (bf16[2,8,8,512]{3,2,1,0:T(8,128)(2,1)}, bf16[2,8,8,512]{3,2,1,0:T(8,128)(2,1)}) async-done(((bf16[2,8,8,512]{3,2,1,0:T(8,128)(2,1)}, bf16[2,8,8,512]{3,2,1,0:T(8,128)(2,1)}), (bf16[2,8,8,512]{3,2,1,0:T(8,128)(2,1)}, bf16[2,8,8,512]{3,2,1,0:T(8,128)(2,1)})) %all-reduce.8.cloned.1.call-update) | async-done | bytes 262160 | tf_op jit(solution)/shard_map/psum | solution.py:30
  76.9 1.0 %bitcast_convert_fusion = (f32[8,8,512,2]{2,1,0,3:T(8,128)S(1)}, f32[8,8,512,2]{2,1,0,3:T(8,128)S(1)}) fusion(bf16[2,8,8,512]{3,2,1,0:T(8,128)(2,1)} %get-tuple-element.7, bf16[2,8,8,512]{3,2,1,0:T(8,128)(2,1)} %get-tuple-element.6), kind=kLoop, calls=%fused_computation.86 | loop fusion | flops 131072 | bytes 786432
  78.4 0.9 %multiply_bitcast_fusion = f32[1,4,8,8,512]{4,3,2,1,0:T(8,128)} fusion(f32[8,8,512,4]{2,1,0,3:T(8,128)S(1)} %multiply_reduce_fusion.1, f32[8,8,512,4]{2,1,0,3:T(8,128)S(1)} %multiply_reduce_fusion), kind=kLoop, calls=%fused_computation.20 | loop fusion | flops 262144 | bytes 1572864 | tf_op jit(solution)/shard_map/broadcast_in_dim | solution.py:66
  (42 shorter events, 3.3 us)
Async XLA Ops:
  6.5 43.6 %copy-start = (bf16[1,4,4,8,8,512]{5,4,3,2,1,0:T(8,128)(2,1)S(1)}, bf16[1,4,4,8,8,512]{5,4,3,2,1,0:T(8,128)(2,1)}, u32[]{:S(2)}) copy-start(bf16[1,4,4,8,8,512]{5,4,3,2,1,0:T(8,128)(2,1)} %param.8) | copy-start | bytes 3145732
  6.5 70.3 %all-reduce.8.cloned.1.call-start = ((), (), s32[]{:S(2)}) async-start(), calls=%async_computation | async-start | bytes 524288 | tf_op jit(solution)/shard_map/psum | solution.py:30
  8.1 10.9 %collective-permute-start.2 = (f32[1,8,512]{2,1,0:T(8,128)S(1)}, f32[1,8,512]{2,1,0:T(8,128)S(1)}, u32[]{:S(2)}, u32[]{:S(2)}) collective-permute-start(f32[1,8,512]{2,1,0:T(8,128)S(1)} %get-tuple-element.30), channel_id=1, source_target_pairs={{0,2},{2,4},{4,6},{6,8},{8,10},{10,12},{12,14},{14,16},{16,18},{18... | collective-permute-start | bytes 49160 | tf_op jit(solution)/shard_map/ppermute | solution.py:19
  10.5 8.5 %collective-permute-start.3 = (f32[1,8,512]{2,1,0:T(8,128)S(1)}, f32[1,8,512]{2,1,0:T(8,128)S(1)}, u32[]{:S(2)}, u32[]{:S(2)}) collective-permute-start(f32[1,8,512]{2,1,0:T(8,128)S(1)} %get-tuple-element.31), channel_id=1, source_target_pairs={{2,0},{4,2},{6,4},{8,6},{10,8},{12,10},{14,12},{16,14},{18,16},{20... | collective-permute-start | bytes 49160 | tf_op jit(solution)/shard_map/ppermute | solution.py:21
  12.6 6.7 %collective-permute-start = (f32[2,1,8,512]{3,2,1,0:T(8,128)S(1)}, f32[2,1,8,512]{3,2,1,0:T(8,128)S(1)}, u32[]{:S(2)}, u32[]{:S(2)}) collective-permute-start(f32[2,1,8,512]{3,2,1,0:T(8,128)S(1)} %get-tuple-element.25), channel_id=1, source_target_pairs={{0,2},{2,4},{4,6},{6,8},{8,10},{10,12},{12,14},{14,16},{16,18},{18... | collective-permute-start | bytes 98312 | tf_op jit(solution)/shard_map/ppermute | solution.py:19
  17.7 4.3 %collective-permute-start.1 = (f32[2,1,8,512]{3,2,1,0:T(8,128)S(1)}, f32[2,1,8,512]{3,2,1,0:T(8,128)S(1)}, u32[]{:S(2)}, u32[]{:S(2)}) collective-permute-start(f32[2,1,8,512]{3,2,1,0:T(8,128)S(1)} %get-tuple-element.24), channel_id=1, source_target_pairs={{2,0},{4,2},{6,4},{8,6},{10,8},{12,10},{14,12},{16,14},{18,16},{20... | collective-permute-start | bytes 98312 | tf_op jit(solution)/shard_map/ppermute | solution.py:21
  19.1 1.0 %copy-start.1 = (f32[2,8,8,512]{3,2,1,0:T(8,128)S(1)}, f32[2,8,8,512]{3,2,1,0:T(8,128)}, u32[]{:S(2)}) copy-start(f32[2,8,8,512]{3,2,1,0:T(8,128)} %param.7) | copy-start | bytes 786436
  22.4 5.9 %collective-permute-start.4 = (f32[2,1,8,512]{3,2,1,0:T(8,128)S(1)}, f32[2,1,8,512]{3,2,1,0:T(8,128)S(1)}, u32[]{:S(2)}, u32[]{:S(2)}) collective-permute-start(f32[2,1,8,512]{3,2,1,0:T(8,128)S(1)} %get-tuple-element.22), channel_id=1, source_target_pairs={{0,2},{2,4},{4,6},{6,8},{8,10},{10,12},{12,14},{14,16},{16,18},{18... | collective-permute-start | bytes 98312 | tf_op jit(solution)/shard_map/ppermute | solution.py:19
  26.9 3.1 %collective-permute-start.5 = (f32[2,1,8,512]{3,2,1,0:T(8,128)S(1)}, f32[2,1,8,512]{3,2,1,0:T(8,128)S(1)}, u32[]{:S(2)}, u32[]{:S(2)}) collective-permute-start(f32[2,1,8,512]{3,2,1,0:T(8,128)S(1)} %get-tuple-element.23), channel_id=1, source_target_pairs={{2,0},{4,2},{6,4},{8,6},{10,8},{12,10},{14,12},{16,14},{18,16},{20... | collective-permute-start | bytes 98312 | tf_op jit(solution)/shard_map/ppermute | solution.py:21
  30.3 7.1 %collective-permute-start.6 = (f32[2,1,8,512]{3,2,1,0:T(8,128)S(1)}, f32[2,1,8,512]{3,2,1,0:T(8,128)S(1)}, u32[]{:S(2)}, u32[]{:S(2)}) collective-permute-start(f32[2,1,8,512]{3,2,1,0:T(8,128)S(1)} %get-tuple-element.20), channel_id=1, source_target_pairs={{0,2},{2,4},{4,6},{6,8},{8,10},{10,12},{12,14},{14,16},{16,18},{18... | collective-permute-start | bytes 98312 | tf_op jit(solution)/shard_map/ppermute | solution.py:19
  36.1 3.1 %collective-permute-start.7 = (f32[2,1,8,512]{3,2,1,0:T(8,128)S(1)}, f32[2,1,8,512]{3,2,1,0:T(8,128)S(1)}, u32[]{:S(2)}, u32[]{:S(2)}) collective-permute-start(f32[2,1,8,512]{3,2,1,0:T(8,128)S(1)} %get-tuple-element.21), channel_id=1, source_target_pairs={{2,0},{4,2},{6,4},{8,6},{10,8},{12,10},{14,12},{16,14},{18,16},{20... | collective-permute-start | bytes 98312 | tf_op jit(solution)/shard_map/ppermute | solution.py:21
  39.5 6.4 %collective-permute-start.8 = (f32[2,1,8,512]{3,2,1,0:T(8,128)S(1)}, f32[2,1,8,512]{3,2,1,0:T(8,128)S(1)}, u32[]{:S(2)}, u32[]{:S(2)}) collective-permute-start(f32[2,1,8,512]{3,2,1,0:T(8,128)S(1)} %get-tuple-element.18), channel_id=1, source_target_pairs={{0,2},{2,4},{4,6},{6,8},{8,10},{10,12},{12,14},{14,16},{16,18},{18... | collective-permute-start | bytes 98312 | tf_op jit(solution)/shard_map/ppermute | solution.py:19
  44.5 3.1 %collective-permute-start.9 = (f32[2,1,8,512]{3,2,1,0:T(8,128)S(1)}, f32[2,1,8,512]{3,2,1,0:T(8,128)S(1)}, u32[]{:S(2)}, u32[]{:S(2)}) collective-permute-start(f32[2,1,8,512]{3,2,1,0:T(8,128)S(1)} %get-tuple-element.19), channel_id=1, source_target_pairs={{2,0},{4,2},{6,4},{8,6},{10,8},{12,10},{14,12},{16,14},{18,16},{20... | collective-permute-start | bytes 98312 | tf_op jit(solution)/shard_map/ppermute | solution.py:21
  49.4 0.7 copy-start.2
Sparse Core Ops, SparseCore 0:
  49.5 27.2 all-reduce.7
where the time goes:
time: 86.6 us; the launch traced here: 86.1 us
  waiting for transfers between devices  32.8 us (38%)
  starting transfers between devices  29.2 us (34%)
  between operations  13.7 us (16%)
  other arithmetic  6.08 us (7%)
  local copies, waits for them, and re-layouts  4.28 us (5%)
    psum x1, waiting for transfers between devices, spread(): return lax.psum(kept, axis)  25.6 us
    ppermute x5, starting transfers between devices, with_halo(): lax.ppermute(tail, axis, [(i, (i + 1) % count) for i in range(ends)])  22.7 us
    ppermute x5, waiting for transfers between devices, with_halo(): lax.ppermute(head, axis, [((i + 1) % count, i) for i in range(ends)])  7.24 us
    ppermute x5, starting transfers between devices, with_halo(): lax.ppermute(head, axis, [((i + 1) % count, i) for i in range(ends)])  6.46 us
  transfers between devices with their start and end apart: 11, of which 5 were waited for; matrix products, arithmetic and copies ran while one was open for 3% of the time, Pallas kernels for 0%

commit v1 on v0

v1 whole, which is shorter than its diff:
```python
import math

import jax
import jax.numpy as jnp
from jax import lax
from jax.sharding import PartitionSpec as P

SWEEPS = 4


def swap(value, axis, first):
    count = lax.axis_size(axis)
    pairs = [(i, i + 1) for i in range(first, count - 1, 2)]
    return lax.ppermute(value, axis, pairs + [(b, a) for a, b in pairs])


def packed(controls, code, start):
    slots, _, levels, columns = controls.shape
    rows = lax.dynamic_slice_in_dim(controls, start, SWEEPS, axis=1)
    marks = lax.dynamic_slice_in_dim(code, start, SWEEPS, axis=0)
    marks = jnp.pad(marks, ((0, levels - SWEEPS), (0, 0)))
    return jnp.concatenate([rows.reshape(slots * SWEEPS, levels, columns), marks[None]], axis=0)


def unpacked(packet, slots):
    _, levels, columns = packet.shape
    rows = packet[: slots * SWEEPS].reshape(slots, SWEEPS, levels, columns)
    return rows, packet[slots * SWEEPS, :SWEEPS]


def on_device(controls, perturbations, owner, land_mask, diffusivity):
    slots, height, levels, columns = controls.shape
    odd = lax.axis_index("tile") % 2
    code = land_mask.astype(jnp.float32) + 1.0
    tail = height - SWEEPS
    across = swap(packed(controls, code, tail * odd), "tile", 1)
    within = swap(packed(controls, code, tail * (1 - odd)), "tile", 0)
    low, low_code = unpacked(jnp.where(odd == 1, within, across), slots)
    high, high_code = unpacked(jnp.where(odd == 1, across, within), slots)
    field = jnp.concatenate([low, controls, high], axis=1)
    code = jnp.concatenate([low_code, code, high_code], axis=0)[:, None, :]
    kappa = jnp.where(code == 2.0, diffusivity[1][None, :, None], diffusivity[0][None, :, None])
    inside = code > 0.0
    kappa = jnp.where(inside, kappa, 0.0)

    east = 0.5 * (kappa + jnp.pad(kappa, ((0, 0), (0, 0), (0, 1)))[:, :, 1:])
    west = 0.5 * (kappa + jnp.pad(kappa, ((0, 0), (0, 0), (1, 0)))[:, :, :-1])
    south = 0.5 * (kappa[:-1] + kappa[1:])
    for _ in range(SWEEPS):
        wide = jnp.pad(field, ((0, 0), (0, 0), (0, 0), (1, 1)))[:, 1:-1]
        here = field[:, 1:-1]
        flux = south[:-1] * (field[:, :-2] - here) + south[1:] * (field[:, 2:] - here)
        flux = flux + west[1:-1] * (wide[..., :-2] - here) + east[1:-1] * (wide[..., 2:] - here)
        field = jnp.where(inside[1:-1], here + flux, 0.0)
        east, west, south, inside = east[1:-1], west[1:-1], south[1:-1], inside[1:-1]
    weights = field.astype(jnp.bfloat16)

    factor = 1.0 / math.sqrt(owner.shape[0] - 1)
    count = lax.axis_size("tm")
    here = lax.axis_index("tm")
    summed = None
    for step in range(count):
        if step == 0:
            arrived = weights
        else:
            arrived = lax.ppermute(weights, "tm", [(i, (i + step) % count) for i in range(count)])
        chosen = lax.dynamic_slice_in_dim(owner, (here - step) % count * slots, slots)
        for slot in range(slots):
            pert = lax.dynamic_index_in_dim(perturbations[0], chosen[slot], 0, keepdims=False)
            term = pert.astype(jnp.float32) * arrived[slot].astype(jnp.float32)[None]
            summed = term if summed is None else summed + term
    return (summed * factor)[None]


def solution(mesh):
    return jax.shard_map(
        on_device,
        mesh=mesh,
        in_specs=(
            P("tm", "tile", None, None),
            P("tm", None, None, "tile", None, None),
            P(),
            P("tile", None),
            P(),
        ),
        out_specs=P("tm", None, "tile", None, None),
        check_vma=False,
    )
```

time: 86.6 us -> 26 us (0.30)
  waiting for transfers between devices: 32.8 us -> 3.91 us
  starting transfers between devices: 29.2 us -> 6.61 us
  between operations: 13.7 us -> 8.09 us
  other arithmetic: 6.08 us -> 2.66 us
    psum x1 -> x0, waiting for transfers between devices: 25.6 us -> none  [spread(): return lax.psum(kept, axis)]
    ppermute x10 -> x3, starting transfers between devices: 29.2 us -> 6.61 us  [the longest x2 5.03 us: swap(): return lax.ppermute(value, axis, pairs + [(b, a) for a, b in pairs])]
    ppermute x10 -> x3, waiting for transfers between devices: 7.25 us -> 3.91 us  [the longest x1 3.9 us: on_device(): lax.ppermute(weights, 'tm', [(i, (i + step) % count) for i in range(count)])]
    gather x2 -> x0, local copies, waits for them, and re-layouts: 1.16 us -> none  [on_device(): selected = jnp.take(pert_here, chosen, axis=0)]
    mul x1 -> x5, other arithmetic: 0.15 us -> 1.28 us  [the longest x1 1.01 us: on_device(): return (summed * factor)[None]]
    dynamic_slice x0 -> x3, local copies, waits for them, and re-layouts: none -> 1.07 us  [the longest x1 0.99 us: packed(): rows = lax.dynamic_slice_in_dim(controls, start, SWEEPS, axis=1)]
    unnamed x1 -> x0, other arithmetic: 1.02 us -> none
    unnamed x8 -> x10, local copies, waits for them, and re-layouts: 1.42 us -> 2.33 us
  transfers between devices with their start and end apart: 11 -> 3, of which waited for: 5 -> 1; matrix products, arithmetic and copies ran while one was open for 3% -> 3% of each run, Pallas kernels for 0% -> 0%
where the time goes in v1:
time: 26 us; the launch traced here: 25.6 us
  between operations  8.09 us (31%)
  starting transfers between devices  6.61 us (25%)
  local copies, waits for them, and re-layouts  4.37 us (17%)
  waiting for transfers between devices  3.91 us (15%)
  other arithmetic  2.66 us (10%)
    ppermute x2, starting transfers between devices, swap(): return lax.ppermute(value, axis, pairs + [(b, a) for a, b in pairs])  5.03 us
    ppermute x1, waiting for transfers between devices, on_device(): lax.ppermute(weights, 'tm', [(i, (i + step) % count) for i in range(count)])  3.9 us
    unnamed x10, local copies, waits for them, and re-layouts  2.33 us
    ppermute x1, starting transfers between devices, on_device(): lax.ppermute(weights, 'tm', [(i, (i + step) % count) for i in range(count)])  1.58 us
    mul x1, other arithmetic, on_device(): return (summed * factor)[None]  1.01 us
    dynamic_slice x1, local copies, waits for them, and re-layouts, packed(): rows = lax.dynamic_slice_in_dim(controls, start, SWEEPS, axis=1)  0.99 us
    select_n x3, other arithmetic, on_device(): field = jnp.where(inside[1:-1], here + flux, 0.0)  0.91 us
    slice x1, local copies, waits for them, and re-layouts, on_device(): chosen[slot]  0.65 us
  transfers between devices with their start and end apart: 3, of which 1 were waited for; matrix products, arithmetic and copies ran while one was open for 3% of the time, Pallas kernels for 0%

profile of v1, /device:TPU:0, one launch (start us, length us, event | category | flops | bytes accessed | tf_op | source)
XLA Modules:
  0.0 25.6 jit_solution(15605360949957006541)
XLA Ops:
  0.0 0.7 %copy-done.2 = s32[8,512]{1,0:T(8,128)S(1)} copy-done((s32[8,512]{1,0:T(8,128)S(1)}, s32[8,512]{1,0:T(8,128)}, u32[]{:S(2)}) %copy-start.2) | copy-done | bytes 16408
  0.7 1.0 %constant_dynamic-slice_fusion.3 = (f32[2,4,8,512]{3,2,1,0:T(8,128)S(1)}, f32[2,4,8,512]{3,2,1,0:T(8,128)S(1)}) fusion(f32[2,8,8,512]{3,2,1,0:T(8,128)} %param.5, s32[]{:T(128)S(6)} %select_n.83, s32[]{:T(128)S(6)} %select_n.84), kind=kLoop, calls=%fused_computation.109 | loop fusion | bytes 524296 | tf_op jit(solution)/shard_map/dynamic_slice | solution.py:19
  1.8 0.7 %collective-permute-start.1 = (f32[9,8,512]{2,1,0:T(8,128)S(1)}, f32[9,8,512]{2,1,0:T(8,128)S(1)}, u32[]{:S(2)}, u32[]{:S(2)}) collective-permute-start(f32[9,8,512]{2,1,0:T(8,128)S(1)} %pad_maximum_fusion.2), channel_id=1, source_target_pairs={{2,4},{6,8},{10,12},{14,16},{18,20},{22,24},{26,28},{4,2},{8,6},{1... | collective-permute-start | bytes 442376 | tf_op jit(solution)/shard_map/ppermute | solution.py:14
  2.5 4.4 %collective-permute-start = (f32[9,8,512]{2,1,0:T(8,128)S(1)}, f32[9,8,512]{2,1,0:T(8,128)S(1)}, u32[]{:S(2)}, u32[]{:S(2)}) collective-permute-start(f32[9,8,512]{2,1,0:T(8,128)S(1)} %pad_maximum_fusion.1), channel_id=1, source_target_pairs={{0,2},{4,6},{8,10},{12,14},{16,18},{20,22},{24,26},{28,30},{2,0},{... | collective-permute-start | bytes 442376 | tf_op jit(solution)/shard_map/ppermute | solution.py:14
  6.8 0.7 %copy-done.3 = s32[4]{0:T(128)S(1)} copy-done((s32[4]{0:T(128)S(1)}, s32[4]{0:T(128)}, u32[]{:S(2)}) %copy-start.3) | copy-done | bytes 40
  7.5 0.1 fusion.66
  7.6 0.7 %fusion.65 = (s32[1]{0:T(128)}, s32[1]{0:T(128)}, s32[1]{0:T(128)}, s32[1]{0:T(128)}) fusion(s32[2]{0:T(128)S(1)} %get-tuple-element.37, s32[2]{0:T(128)S(1)} %get-tuple-element.38), kind=kLoop, calls=%fused_computation.117 | loop fusion | bytes 32 | tf_op jit(solution)/shard_map/slice | solution.py:69
  15.3 0.0 copy-start.4
  16.0 0.0 copy-done.4
  16.0 0.0 collective-permute-done.1
  16.0 0.0 collective-permute-done
  16.1 0.1 select_select_fusion
  16.2 0.2 fusion.38
  16.9 0.0 copy-start.1
  16.9 0.9 %copy-done.1 = f32[2,8,8,512]{3,2,1,0:T(8,128)S(1)} copy-done((f32[2,8,8,512]{3,2,1,0:T(8,128)S(1)}, f32[2,8,8,512]{3,2,1,0:T(8,128)}, u32[]{:S(2)}) %copy-start.1) | copy-done | bytes 262168
  17.9 0.3 %fusion.9 = f32[2,14,8,512]{3,2,1,0:T(8,128)S(1)} fusion(f32[2,16,8,512]{3,2,1,0:T(8,128)S(1)} %pad_maximum_fusion, f32[14,8,512]{2,1,0:T(8,128)S(1)} %slice.301, f32[14,8,512]{2,1,0:T(8,128)S(1)} %slice.300, f32[14,8,512]{2,1,0:T(8,128)S(1)} %get-tuple-element.18, f32[14,8,512]{2,1,0:T(8,128)S(1)} %get-tuple-element.17, ...), kind=kLoop, calls=%fused_computation.20 | loop fusion | flops 1490944 | bytes 3284992 | tf_op jit(solution)/shard_map/jit(_where)/select_n | solution.py:54
  18.2 0.3 %fusion.20 = f32[2,12,8,512]{3,2,1,0:T(8,128)S(1)} fusion(f32[2,14,8,512]{3,2,1,0:T(8,128)S(1)} %fusion.9, f32[12,8,512]{2,1,0:T(8,128)S(1)} %slice.308, f32[12,8,512]{2,1,0:T(8,128)S(1)} %slice.307, f32[12,8,512]{2,1,0:T(8,128)S(1)} %get-tuple-element.16, f32[12,8,512]{2,1,0:T(8,128)S(1)} %get-tuple-element.15, pred[12,512]{1,0:T(8,128)(4,1)S(1)} %slice_bitcast_fusion.5), kind=kLoop, calls=%fused_computation.35 | loop fusion | flops 1277952 | bytes 2826240 | tf_op jit(solution)/shard_map/jit(_where)/select_n | solution.py:54
  18.6 0.3 %fusion.31 = f32[2,10,8,512]{3,2,1,0:T(8,128)S(1)} fusion(f32[2,12,8,512]{3,2,1,0:T(8,128)S(1)} %fusion.20, f32[10,8,512]{2,1,0:T(8,128)S(1)} %slice.315, f32[10,8,512]{2,1,0:T(8,128)S(1)} %slice.314, f32[10,8,512]{2,1,0:T(8,128)S(1)} %get-tuple-element.14, f32[10,8,512]{2,1,0:T(8,128)S(1)} %get-tuple-element.13, pred[10,512]{1,0:T(8,128)(4,1)S(1)} %slice_bitcast_fusion.6), kind=kLoop, calls=%fused_computation.48 | loop fusion | flops 1064960 | bytes 2367488 | tf_op jit(solution)/shard_map/jit(_where)/select_n | solution.py:54
  18.8 0.0 copy-start
  18.8 0.2 fusion.47
  19.1 1.6 %collective-permute-start.2 = (bf16[2,8,8,512]{3,2,1,0:T(8,128)(2,1)S(1)}, bf16[2,8,8,512]{3,2,1,0:T(8,128)(2,1)S(1)}, u32[]{:S(2)}, u32[]{:S(2)}) collective-permute-start(bf16[2,8,8,512]{3,2,1,0:T(8,128)(2,1)S(1)} %fusion.47), channel_id=1, source_target_pairs={{0,1},{1,0},{2,3},{3,2},{4,5},{5,4},{6,7},{7,6},{8,9},{9,8},{10,11... | collective-permute-start | bytes 393224 | tf_op jit(solution)/shard_map/ppermute | solution.py:66
  20.7 3.9 %collective-permute-done.2 = bf16[2,8,8,512]{3,2,1,0:T(8,128)(2,1)S(1)} collective-permute-done((bf16[2,8,8,512]{3,2,1,0:T(8,128)(2,1)S(1)}, bf16[2,8,8,512]{3,2,1,0:T(8,128)(2,1)S(1)}, u32[]{:S(2)}, u32[]{:S(2)}) %collective-permute-start.2) | collective-permute-done | bytes 131104 | tf_op jit(solution)/shard_map/ppermute | solution.py:66
  24.6 0.0 copy-done
  24.6 1.0 %fusion.1 = f32[1,4,8,8,512]{4,3,2,1,0:T(8,128)} fusion(f32[8,8,512]{2,1,0:T(8,128)S(1)} %get-tuple-element.26, bf16[1,4,4,8,8,512]{5,4,3,2,1,0:T(8,128)(2,1)S(1)} %copy-done, s32[]{:T(128)S(6)} %select_n.97, f32[8,8,512]{2,1,0:T(8,128)S(1)} %get-tuple-element.25, s32[]{:T(128)S(6)} %select_n.96, f32[8,8,512]{2,1,0:T(8,128)S(1)} %get-tuple-element.24, ...), kind=kLoop, calls=%fused_computation.7 | loop fusion | flops 1572864 | bytes 2097168 | tf_op jit(solution)/shard_map/mul | solution.py:72
  (35 shorter events, 0.5 us)
Async XLA Ops:
  0.0 0.7 %copy-start.2 = (s32[8,512]{1,0:T(8,128)S(1)}, s32[8,512]{1,0:T(8,128)}, u32[]{:S(2)}) copy-start(s32[8,512]{1,0:T(8,128)} %param.8) | copy-start | bytes 49156
  1.8 14.3 %collective-permute-start.1 = (f32[9,8,512]{2,1,0:T(8,128)S(1)}, f32[9,8,512]{2,1,0:T(8,128)S(1)}, u32[]{:S(2)}, u32[]{:S(2)}) collective-permute-start(f32[9,8,512]{2,1,0:T(8,128)S(1)} %pad_maximum_fusion.2), channel_id=1, source_target_pairs={{2,4},{6,8},{10,12},{14,16},{18,20},{22,24},{26,28},{4,2},{8,6},{1... | collective-permute-start | bytes 442376 | tf_op jit(solution)/shard_map/ppermute | solution.py:14
  2.5 13.6 %collective-permute-start = (f32[9,8,512]{2,1,0:T(8,128)S(1)}, f32[9,8,512]{2,1,0:T(8,128)S(1)}, u32[]{:S(2)}, u32[]{:S(2)}) collective-permute-start(f32[9,8,512]{2,1,0:T(8,128)S(1)} %pad_maximum_fusion.1), channel_id=1, source_target_pairs={{0,2},{4,6},{8,10},{12,14},{16,18},{20,22},{24,26},{28,30},{2,0},{... | collective-permute-start | bytes 442376 | tf_op jit(solution)/shard_map/ppermute | solution.py:14
  6.8 0.7 %copy-start.3 = (s32[4]{0:T(128)S(1)}, s32[4]{0:T(128)}, u32[]{:S(2)}) copy-start(s32[4]{0:T(128)} %param.7) | copy-start | bytes 52
  15.3 0.7 %copy-start.4 = (f32[2,8]{1,0:T(2,128)S(1)}, f32[2,8]{1,0:T(2,128)}, u32[]{:S(2)}) copy-start(f32[2,8]{1,0:T(2,128)} %param.9) | copy-start | bytes 196
  16.9 1.0 %copy-start.1 = (f32[2,8,8,512]{3,2,1,0:T(8,128)S(1)}, f32[2,8,8,512]{3,2,1,0:T(8,128)}, u32[]{:S(2)}) copy-start(f32[2,8,8,512]{3,2,1,0:T(8,128)} %param.5) | copy-start | bytes 786436
  18.8 5.8 %copy-start = (bf16[1,4,4,8,8,512]{5,4,3,2,1,0:T(8,128)(2,1)S(1)}, bf16[1,4,4,8,8,512]{5,4,3,2,1,0:T(8,128)(2,1)}, u32[]{:S(2)}) copy-start(bf16[1,4,4,8,8,512]{5,4,3,2,1,0:T(8,128)(2,1)} %param.6) | copy-start | bytes 3145732
  19.1 5.5 %collective-permute-start.2 = (bf16[2,8,8,512]{3,2,1,0:T(8,128)(2,1)S(1)}, bf16[2,8,8,512]{3,2,1,0:T(8,128)(2,1)S(1)}, u32[]{:S(2)}, u32[]{:S(2)}) collective-permute-start(bf16[2,8,8,512]{3,2,1,0:T(8,128)(2,1)S(1)} %fusion.47), channel_id=1, source_target_pairs={{0,1},{1,0},{2,3},{3,2},{4,5},{5,4},{6,7},{7,6},{8,9},{9,8},{10,11... | collective-permute-start | bytes 393224 | tf_op jit(solution)/shard_map/ppermute | solution.py:66

commit v2 on v1

v2 whole, which is shorter than its diff:
```python
import math

import jax
import jax.numpy as jnp
from jax import lax
from jax.experimental import pallas as pl
from jax.experimental.pallas import tpu as pltpu
from jax.sharding import PartitionSpec as P

SWEEPS = 4
VMEM = pl.BlockSpec(memory_space=pltpu.VMEM)
SMEM = pl.BlockSpec(memory_space=pltpu.SMEM)
ANY = pl.BlockSpec(memory_space=pl.ANY)
PARAMS = pltpu.CompilerParams(vmem_limit_bytes=16 * 1024 * 1024)


def parity():
    return lax.rem(lax.axis_index("tile"), 2)


def own_row(odd, j):
    return j + odd * (2 * SWEEPS - 1 - 2 * j)


def half_row(odd, j):
    return j % SWEEPS + odd * (SWEEPS - 1 - 2 * (j % SWEEPS))


def outer_start(odd):
    return SWEEPS * odd


def inner_start(odd):
    return SWEEPS * (1 - odd)


def swap(value, axis, first):
    count = lax.axis_size(axis)
    pairs = [(i, i + 1) for i in range(first, count - 1, 2)]
    return lax.ppermute(value, axis, pairs + [(b, a) for a, b in pairs])


def pack_kernel(controls, mask, within, across, rows, sems):
    odd = parity()
    slots = controls.shape[0]
    copies = [pltpu.make_async_copy(mask, rows, sems.at[2 * slots])]
    for slot in range(slots):
        for side, (start, packet) in enumerate(((outer_start(odd), across), (inner_start(odd), within))):
            copies.append(
                pltpu.make_async_copy(
                    controls.at[slot, pl.ds(start, SWEEPS)],
                    packet.at[pl.ds(SWEEPS * slot, SWEEPS)],
                    sems.at[2 * slot + side],
                )
            )
    for copy in copies:
        copy.start()
    copies[0].wait()
    code = rows[...].astype(jnp.float32) + 1.0
    within[SWEEPS * slots] = code
    across[SWEEPS * slots] = code
    for copy in copies[1:]:
        copy.wait()


def by_level(diffusivity, kind, shape):
    level = lax.broadcasted_iota(jnp.int32, shape, 0)
    value = jnp.full(shape, diffusivity[kind, 0], jnp.float32)
    for index in range(1, shape[0]):
        value = jnp.where(level == index, diffusivity[kind, index], value)
    return value


def kappa_of(code, sea, land):
    code = jnp.broadcast_to(code, sea.shape)
    return jnp.where(code == 2.0, land, jnp.where(code == 1.0, sea, 0.0))


def along_row(kappa):
    columns = kappa.shape[1]
    lane = lax.broadcasted_iota(jnp.int32, kappa.shape, 1)
    last = lane == columns - 1
    loss = 0.5 * (kappa + jnp.where(last, 0.0, pltpu.roll(kappa, columns - 1, 1)))
    east = jnp.where(last, 0.0, loss)
    west = pltpu.roll(east, 1, 1)
    return east, west, loss + jnp.where(lane == 0, 0.5 * kappa, west)


def update(centre, east, west, below, above, here, before, after):
    columns = here.shape[1]
    value = centre * here + below * before + above * after
    value = value + east * pltpu.roll(here, columns - 1, 1)
    return value + west * pltpu.roll(here, 1, 1)


FACE, EAST, WEST, CENTRE, KAPPA = 0, 4, 8, 12, 16


def inner_kernel(controls, packet, mask, diffusivity, weights, kept, coef, face, centre, east, west, field):
    odd = parity()
    slots, _, levels, columns = controls.shape
    shape = (levels, columns)
    sea, land = by_level(diffusivity, 0, shape), by_level(diffusivity, 1, shape)
    total = 3 * SWEEPS

    def far_row(k):
        return k + odd * (SWEEPS - 1 - 2 * k)

    def kappa_at(j):
        if j < 2 * SWEEPS:
            code = mask[pl.ds(own_row(odd, j), 1), :].astype(jnp.float32) + 1.0
        else:
            place = far_row(j - 2 * SWEEPS) + SWEEPS * odd
            code = packet[slots * SWEEPS, pl.ds(place, 1), :]
        return kappa_of(code, sea, land)

    previous = kappa_at(0)
    coef[KAPPA] = previous
    e, w, loss = along_row(previous)
    coef[EAST], coef[WEST] = e, w
    lost = loss
    for j in range(1, total):
        kappa = kappa_at(j)
        step = 0.5 * (previous + kappa)
        face[j] = step
        centre[j - 1] = 1.0 - (lost + step)
        if j <= SWEEPS:
            coef[FACE + j - 1] = step
            coef[CENTRE + j - 1] = 1.0 - (lost + step)
        if j < total - 1:
            e, w, loss = along_row(kappa)
            east[j], west[j] = e, w
            if j < SWEEPS:
                coef[EAST + j], coef[WEST + j] = e, w
            lost = loss + step
        previous = kappa

    for slot in range(slots):
        def start(j):
            if j < 2 * SWEEPS:
                return controls[slot, own_row(odd, j)]
            return packet[SWEEPS * slot + far_row(j - 2 * SWEEPS)]

        for sweep in range(1, SWEEPS + 1):
            def read(j):
                return start(j) if sweep == 1 else field[sweep - 2, slot, j]

            low, high = sweep, total - sweep
            before, here = read(low - 1), read(low)
            for j in range(low, high):
                after = read(j + 1)
                value = update(centre[j], east[j], west[j], face[j], face[j + 1], here, before, after)
                if sweep == SWEEPS:
                    weights[slot, half_row(odd, j)] = value.astype(weights.dtype)
                else:
                    field[sweep - 1, slot, j] = value
                    if j - sweep < 2:
                        kept[slot, 2 * (sweep - 1) + j - sweep] = value
                before, here = here, after


def outer_kernel(controls, packet, kept, coef, diffusivity, weights, face, centre, east, west, field):
    odd = parity()
    tile, tiles = lax.axis_index("tile"), lax.axis_size("tile")
    slots, _, levels, columns = controls.shape
    shape = (levels, columns)
    sea, land = by_level(diffusivity, 0, shape), by_level(diffusivity, 1, shape)
    edge = jnp.where(odd == 1, tile == tiles - 1, tile == 0)
    inside = jnp.where(edge, 0.0, 1.0).astype(jnp.float32)

    def far_row(k):
        return SWEEPS - 1 - k + odd * (2 * k - SWEEPS + 1)

    previous = None
    lost = None
    for j in range(-SWEEPS, 1):
        if j < 0:
            place = far_row(-1 - j) + SWEEPS * (1 - odd)
            kappa = kappa_of(packet[slots * SWEEPS, pl.ds(place, 1), :], sea, land)
        else:
            kappa = coef[KAPPA]
        if previous is not None:
            step = 0.5 * (previous + kappa)
            face[j + SWEEPS] = step
            if lost is not None:
                centre[j - 1 + SWEEPS] = 1.0 - (lost + step)
            if j < 0:
                e, w, loss = along_row(kappa)
                east[j + SWEEPS], west[j + SWEEPS] = e, w
                lost = loss + step
            else:
                centre[SWEEPS] = coef[CENTRE] - step
        previous = kappa

    def coefficients(j):
        if j < 0:
            i = j + SWEEPS
            return centre[i], east[i], west[i], face[i], face[i + 1]
        if j == 0:
            return centre[SWEEPS], coef[EAST], coef[WEST], face[SWEEPS], coef[FACE]
        return coef[CENTRE + j], coef[EAST + j], coef[WEST + j], coef[FACE + j - 1], coef[FACE + j]

    for slot in range(slots):
        for sweep in range(1, SWEEPS + 1):
            def read(j):
                if sweep == 1:
                    if j >= 0:
                        return controls[slot, own_row(odd, j)]
                    return packet[SWEEPS * slot + far_row(-1 - j)]
                if j >= sweep - 1:
                    return kept[slot, 2 * (sweep - 2) + j - (sweep - 1)]
                return field[sweep - 2, slot, j + SWEEPS]

            low = sweep - SWEEPS
            before, here = read(low - 1), read(low)
            for j in range(low, sweep):
                after = read(j + 1)
                value = update(*coefficients(j), here, before, after)
                if j < 0:
                    value = value * inside
                if sweep == SWEEPS:
                    weights[slot, half_row(odd, j)] = value.astype(weights.dtype)
                else:
                    field[sweep - 1, slot, j + SWEEPS] = value
                before, here = here, after


def early_kernel(arrivals, factor, *refs):
    pert, owner, inner, outer = refs[:4]
    arrived = refs[4 : 4 + arrivals]
    out, partial, chosen, ready, sems, out_sems = refs[4 + arrivals :]
    odd = parity()
    count, here = lax.axis_size("tm"), lax.axis_index("tm")
    slots = inner.shape[0]
    variables = pert.shape[1]

    def member(step, slot):
        return owner[lax.rem(here - step + count, count) * slots + slot]

    copies = []
    for step in range(1, count):
        for slot in range(slots):
            place = (step - 1) * slots + slot
            copies.append(
                pltpu.make_async_copy(
                    pert.at[member(step, slot), :, pl.ds(outer_start(odd), SWEEPS)],
                    chosen.at[place],
                    sems.at[place],
                )
            )
            copies[-1].start()

    for row in range(SWEEPS):
        total = [None] * variables
        for step in range(count):
            source = inner if step == 0 else arrived[step - 1]
            for slot in range(slots):
                weight = source[slot, row].astype(jnp.float32) * factor
                who = member(step, slot)
                for v in range(variables):
                    term = pert[who, v, inner_start(odd) + row].astype(jnp.float32) * weight
                    total[v] = term if total[v] is None else total[v] + term
        for v in range(variables):
            ready[v, row] = total[v]
    writes = []
    for v in range(variables):
        writes.append(
            pltpu.make_async_copy(ready.at[v], out.at[v, pl.ds(inner_start(odd), SWEEPS)], out_sems.at[v])
        )
        writes[-1].start()
    for row in range(SWEEPS):
        total = [None] * variables
        for slot in range(slots):
            weight = outer[slot, row].astype(jnp.float32) * factor
            who = member(0, slot)
            for v in range(variables):
                term = pert[who, v, outer_start(odd) + row].astype(jnp.float32) * weight
                total[v] = term if total[v] is None else total[v] + term
        for v in range(variables):
            partial[v, row] = total[v]
    for copy in copies + writes:
        copy.wait()


def late_kernel(arrivals, factor, *refs):
    partial, chosen = refs[:2]
    arrived = refs[2 : 2 + arrivals]
    _, out, ready, sems = refs[2 + arrivals :]
    odd = parity()
    variables = partial.shape[0]
    slots = arrived[0].shape[0] if arrivals else 0
    writes = []
    for v in range(variables):
        for row in range(SWEEPS):
            total = partial[v, row]
            for index in range(arrivals):
                for slot in range(slots):
                    weight = arrived[index][slot, row].astype(jnp.float32) * factor
                    total = total + chosen[index * slots + slot, v, row].astype(jnp.float32) * weight
            ready[v, row] = total
        writes.append(
            pltpu.make_async_copy(ready.at[v], out.at[v, pl.ds(outer_start(odd), SWEEPS)], sems.at[v])
        )
        writes[-1].start()
    for copy in writes:
        copy.wait()


def cost(flops, moved):
    return pl.CostEstimate(flops=flops, bytes_accessed=moved, transcendentals=0)


def on_device(controls, perturbations, owner, land_mask, diffusivity):
    slots, height, levels, columns = controls.shape
    members, variables = perturbations.shape[1:3]
    count = lax.axis_size("tm")
    factor = 1.0 / math.sqrt(owner.shape[0] - 1)
    row = (levels, columns)
    f32, bf16 = jnp.float32, jnp.bfloat16
    packet = pltpu.VMEM((slots * SWEEPS + 1, *row), f32)
    half = pltpu.VMEM((slots, SWEEPS, *row), bf16)
    dma = pltpu.SemaphoreType.DMA

    within, across = pl.pallas_call(
        pack_kernel,
        out_shape=(packet, packet),
        in_specs=[ANY, ANY],
        out_specs=(VMEM, VMEM),
        scratch_shapes=[pltpu.VMEM((height, columns), land_mask.dtype), dma((2 * slots + 1,))],
        compiler_params=PARAMS,
        name="pack",
    )(controls, land_mask)
    within = swap(within, "tile", 0)
    across = swap(across, "tile", 1)

    mine = pltpu.with_memory_space_constraint(controls, pltpu.VMEM)
    inner, kept, coef = pl.pallas_call(
        inner_kernel,
        out_shape=(half, pltpu.VMEM((slots, 6, *row), f32), pltpu.VMEM((17, *row), f32)),
        in_specs=[VMEM, VMEM, VMEM, SMEM],
        out_specs=(VMEM, VMEM, VMEM),
        scratch_shapes=[pltpu.VMEM((3 * SWEEPS, *row), f32)] * 4
        + [pltpu.VMEM((SWEEPS - 1, slots, 3 * SWEEPS, *row), f32)],
        compiler_params=PARAMS,
        cost_estimate=cost(4_000_000, 1_000_000),
        name="inner_rows",
    )(mine, pltpu.with_memory_space_constraint(within, pltpu.VMEM), land_mask, diffusivity)

    def shift(value):
        return [
            lax.ppermute(value, "tm", [(i, (i + step) % count) for i in range(count)])
            for step in range(1, count)
        ]

    inner_arrived = shift(inner)
    outer = pl.pallas_call(
        outer_kernel,
        out_shape=half,
        in_specs=[VMEM, VMEM, VMEM, VMEM, SMEM],
        out_specs=VMEM,
        scratch_shapes=[pltpu.VMEM((SWEEPS + 1, *row), f32)] * 4
        + [pltpu.VMEM((SWEEPS - 1, slots, 2 * SWEEPS, *row), f32)],
        compiler_params=PARAMS,
        cost_estimate=cost(2_000_000, 1_000_000),
        name="outer_rows",
    )(mine, pltpu.with_memory_space_constraint(across, pltpu.VMEM), kept, coef, diffusivity)
    outer_arrived = shift(outer)

    def near(value):
        return pltpu.with_memory_space_constraint(value, pltpu.VMEM)

    arrivals = count - 1
    result = jax.ShapeDtypeStruct((variables, height, *row), f32)
    part = pltpu.VMEM((variables, SWEEPS, *row), f32)
    others = max(arrivals, 1) * slots
    out, partial, chosen = pl.pallas_call(
        lambda *refs: early_kernel(arrivals, factor, *refs),
        out_shape=(result, part, pltpu.VMEM((others, variables, SWEEPS, *row), bf16)),
        in_specs=[VMEM, SMEM, VMEM, VMEM] + [VMEM] * arrivals,
        out_specs=(ANY, VMEM, VMEM),
        scratch_shapes=[pltpu.VMEM(part.shape, f32), dma((others,)), dma((variables,))],
        compiler_params=PARAMS,
        cost_estimate=cost(4_000_000, 2_000_000),
        name="early_products",
    )(near(perturbations[0]), owner, inner, outer, *map(near, inner_arrived))
    out = pl.pallas_call(
        lambda *refs: late_kernel(arrivals, factor, *refs),
        out_shape=result,
        in_specs=[VMEM, VMEM] + [VMEM] * arrivals + [ANY],
        out_specs=ANY,
        scratch_shapes=[pltpu.VMEM(part.shape, f32), dma((variables,))],
        input_output_aliases={2 + arrivals: 0},
        compiler_params=PARAMS,
        cost_estimate=cost(1_000_000, 1_000_000),
        name="late_products",
    )(partial, chosen, *map(near, outer_arrived), out)
    return out[None]


def solution(mesh):
    return jax.shard_map(
        on_device,
        mesh=mesh,
        in_specs=(
            P("tm", "tile", None, None),
            P("tm", None, None, "tile", None, None),
            P(),
            P("tile", None),
            P(),
        ),
        out_specs=P("tm", None, "tile", None, None),
        check_vma=False,
    )
```

time: 26 us -> 17 us (0.65)
  the two profiles are of different devices: /device:TPU:0 before, /device:TPU:9 now
where the time goes in v2:
time: 17 us; the launch traced here: 16.7 us
  starting transfers between devices  6.37 us (37%)
  Pallas kernels  5.18 us (30%)
  waiting for transfers between devices  2.72 us (16%)
  local copies, waits for them, and re-layouts  2.35 us (14%)
    ppermute x2, starting transfers between devices, swap(): return lax.ppermute(value, axis, pairs + [(b, a) for a, b in pairs])  3.76 us
    ppermute x2, starting transfers between devices, shift(): lax.ppermute(value, 'tm', [(i, (i + step) % count) for i in range(count)])  2.61 us
    unnamed x10, local copies, waits for them, and re-layouts  2.35 us
    ppermute x2, waiting for transfers between devices, swap(): return lax.ppermute(value, axis, pairs + [(b, a) for a, b in pairs])  1.55 us
    pallas_call x1, Pallas kernels, on_device(): pl.pallas_call(lambda *refs: early_kernel(arrivals, factor, *refs), out_s...  1.51 us
    pallas_call x1, Pallas kernels, on_device(): pl.pallas_call(inner_kernel, out_shape=(half, pltpu.VMEM((slots, 6, *row)...  1.45 us
    ppermute x2, waiting for transfers between devices, shift(): lax.ppermute(value, 'tm', [(i, (i + step) % count) for i in range(count)])  1.17 us
    pallas_call x1, Pallas kernels, on_device(): pl.pallas_call(outer_kernel, out_shape=half, in_specs=[VMEM, VMEM, VMEM,...  1.08 us
  transfers between devices with their start and end apart: 4, of which 2 were waited for; matrix products, arithmetic and copies ran while one was open for 0% of the time, Pallas kernels for 24%

profile of v2, /device:TPU:9, one launch (start us, length us, event | category | flops | bytes accessed | tf_op | source)
XLA Modules:
  0.0 16.7 jit_solution(4390145196185380196)
XLA Ops:
  0.0 0.0 copy-start
  0.0 0.9 %copy-done = f32[2,8,8,512]{3,2,1,0:T(8,128)S(1)} copy-done((f32[2,8,8,512]{3,2,1,0:T(8,128)S(1)}, f32[2,8,8,512]{3,2,1,0:T(8,128)}, u32[]{:S(2)}) %copy-start) | copy-done | bytes 262168
  1.0 0.0 copy-start.2
  1.0 0.7 %copy-done.2 = s32[8,512]{1,0:T(8,128)S(1)} copy-done((s32[8,512]{1,0:T(8,128)S(1)}, s32[8,512]{1,0:T(8,128)}, u32[]{:S(2)}) %copy-start.2) | copy-done | bytes 16408
  1.7 0.0 copy-start.1
  1.7 0.4 %pack.1 = (f32[9,8,512]{2,1,0:T(8,128)S(1)}, f32[9,8,512]{2,1,0:T(8,128)S(1)}) custom-call(f32[2,8,8,512]{3,2,1,0:T(8,128)S(1)} %copy-done, s32[8,512]{1,0:T(8,128)S(1)} %copy-done.2), custom_call_target="tpu_custom_call" | custom-call | tf_op jit(solution)/shard_map/pack/pallas_call | solution.py:324
  2.1 0.7 %collective-permute-start = (f32[9,8,512]{2,1,0:T(8,128)S(1)}, f32[9,8,512]{2,1,0:T(8,128)S(1)}, u32[]{:S(2)}, u32[]{:S(2)}) collective-permute-start(f32[9,8,512]{2,1,0:T(8,128)S(1)} %get-tuple-element.13), channel_id=1, source_target_pairs={{0,2},{4,6},{8,10},{12,14},{16,18},{20,22},{24,26},{28,30},{2,0},{... | collective-permute-start | bytes 442376 | tf_op jit(solution)/shard_map/ppermute | solution.py:40
  2.8 3.0 %collective-permute-start.1 = (f32[9,8,512]{2,1,0:T(8,128)S(1)}, f32[9,8,512]{2,1,0:T(8,128)S(1)}, u32[]{:S(2)}, u32[]{:S(2)}) collective-permute-start(f32[9,8,512]{2,1,0:T(8,128)S(1)} %get-tuple-element.15), channel_id=1, source_target_pairs={{2,4},{6,8},{10,12},{14,16},{18,20},{22,24},{26,28},{4,2},{8,6},{1... | collective-permute-start | bytes 442376 | tf_op jit(solution)/shard_map/ppermute | solution.py:40
  5.8 0.0 collective-permute-done.packet
  5.9 0.0 copy-start.3
  5.9 0.7 %copy-done.3 = f32[2,8]{1,0:T(2,128)S(1)} copy-done((f32[2,8]{1,0:T(2,128)S(1)}, f32[2,8]{1,0:T(2,128)}, u32[]{:S(2)}) %copy-start.3) | copy-done | bytes 88
  6.5 1.5 %inner_rows.1 = (bf16[2,4,8,512]{3,2,1,0:T(8,128)(2,1)S(1)}, f32[2,6,8,512]{3,2,1,0:T(8,128)S(1)}, f32[17,8,512]{2,1,0:T(8,128)S(1)}) custom-call(f32[2,8,8,512]{3,2,1,0:T(8,128)S(1)} %copy-done, f32[9,8,512]{2,1,0:T(8,128)S(1)} %collective-permute-done.packet, s32[8,512]{1,0:T(8,128)S(1)} %copy-done.2, f32[2,8]{1,0:T(2,128)S(1)} %copy-done.3), custom_call_target="tpu_custom_call" | custom-call | flops 4000000 | bytes 1000000 | tf_op jit(solution)/shard_map/inner_rows/pallas_call | solution.py:337
  8.0 1.3 %collective-permute-start.2 = (bf16[2,4,8,512]{3,2,1,0:T(8,128)(2,1)S(1)}, bf16[2,4,8,512]{3,2,1,0:T(8,128)(2,1)S(1)}, u32[]{:S(2)}, u32[]{:S(2)}) collective-permute-start(bf16[2,4,8,512]{3,2,1,0:T(8,128)(2,1)S(1)} %get-tuple-element.14.refs_2_), channel_id=1, source_target_pairs={{0,1},{1,0},{2,3},{3,2},{4,5},{5,4},{6,7},{7,6},{8,9},{9,8},{10,11... | collective-permute-start | bytes 196616 | tf_op jit(solution)/shard_map/ppermute | solution.py:351
  9.3 1.5 %collective-permute-done.1.packet = f32[9,8,512]{2,1,0:T(8,128)S(1)} collective-permute-done((f32[9,8,512]{2,1,0:T(8,128)S(1)}, f32[9,8,512]{2,1,0:T(8,128)S(1)}, u32[]{:S(2)}, u32[]{:S(2)}) %collective-permute-start.1) | collective-permute-done | bytes 147488 | tf_op jit(solution)/shard_map/ppermute | solution.py:40
  10.8 1.1 %outer_rows.1.refs_3_ = bf16[2,4,8,512]{3,2,1,0:T(8,128)(2,1)S(1)} custom-call(f32[2,8,8,512]{3,2,1,0:T(8,128)S(1)} %copy-done, f32[9,8,512]{2,1,0:T(8,128)S(1)} %collective-permute-done.1.packet, f32[2,6,8,512]{3,2,1,0:T(8,128)S(1)} %get-tuple-element.16.kept, f32[17,8,512]{2,1,0:T(8,128)S(1)} %get-tuple-element.17.coef, f32[2,8]{1,0:T(2,128)S(1)} %copy-done.3), custom_call_target="tpu_custom_call" | custom-call | flops 2000000 | bytes 1000000 | tf_op jit(solution)/shard_map/outer_rows/pallas_call | solution.py:356
  11.9 0.0 copy-start.4
  11.9 1.3 %collective-permute-start.3 = (bf16[2,4,8,512]{3,2,1,0:T(8,128)(2,1)S(1)}, bf16[2,4,8,512]{3,2,1,0:T(8,128)(2,1)S(1)}, u32[]{:S(2)}, u32[]{:S(2)}) collective-permute-start(bf16[2,4,8,512]{3,2,1,0:T(8,128)(2,1)S(1)} %outer_rows.1.refs_3_), channel_id=1, source_target_pairs={{0,1},{1,0},{2,3},{3,2},{4,5},{5,4},{6,7},{7,6},{8,9},{9,8},{10,11... | collective-permute-start | bytes 196616 | tf_op jit(solution)/shard_map/ppermute | solution.py:351
  13.2 0.0 collective-permute-done.2.refs_4_
  13.2 0.0 copy-done.1
  13.3 0.0 copy-done.4
  13.3 1.5 %early_products.1 = (f32[4,8,8,512]{3,2,1,0:T(8,128)}, f32[4,4,8,512]{3,2,1,0:T(8,128)S(1)}, bf16[2,4,4,8,512]{4,3,2,1,0:T(8,128)(2,1)S(1)}) custom-call(bf16[4,4,8,8,512]{4,3,2,1,0:T(8,128)(2,1)S(1)} %bitcast.2, s32[4]{0:T(128)S(1)} %copy-done.4, bf16[2,4,8,512]{3,2,1,0:T(8,128)(2,1)S(1)} %get-tuple-element.14.refs_2_, ...), custom_call_target="tpu_custom_call" | custom-call | flops 4000000 | bytes 2000000 | tf_op jit(solution)/shard_map/early_products/pallas_call | solution.py:376
  14.8 1.2 %collective-permute-done.3.refs_2_ = bf16[2,4,8,512]{3,2,1,0:T(8,128)(2,1)S(1)} collective-permute-done((bf16[2,4,8,512]{3,2,1,0:T(8,128)(2,1)S(1)}, bf16[2,4,8,512]{3,2,1,0:T(8,128)(2,1)S(1)}, u32[]{:S(2)}, u32[]{:S(2)}) %collective-permute-start.3) | collective-permute-done | bytes 65568 | tf_op jit(solution)/shard_map/ppermute | solution.py:351
  15.9 0.8 %late_products.1 = f32[4,8,8,512]{3,2,1,0:T(8,128)} custom-call(f32[4,4,8,512]{3,2,1,0:T(8,128)S(1)} %get-tuple-element.18.refs_0_, bf16[2,4,4,8,512]{4,3,2,1,0:T(8,128)(2,1)S(1)} %get-tuple-element.19.refs_1_, bf16[2,4,8,512]{3,2,1,0:T(8,128)(2,1)S(1)} %collective-permute-done.3.refs_2_, ...), custom_call_target="tpu_custom_call", output_to_operand_aliasing={{}: (3, {})} | custom-call | flops 1000000 | bytes 1000000 | tf_op jit(solution)/shard_map/late_products/pallas_call | solution.py:386
Async XLA Ops:
  0.0 0.9 %copy-start = (f32[2,8,8,512]{3,2,1,0:T(8,128)S(1)}, f32[2,8,8,512]{3,2,1,0:T(8,128)}, u32[]{:S(2)}) copy-start(f32[2,8,8,512]{3,2,1,0:T(8,128)} %controls.5) | copy-start | bytes 786436
  1.0 0.7 %copy-start.2 = (s32[8,512]{1,0:T(8,128)S(1)}, s32[8,512]{1,0:T(8,128)}, u32[]{:S(2)}) copy-start(s32[8,512]{1,0:T(8,128)} %mask.3) | copy-start | bytes 49156
  1.7 11.6 %copy-start.1 = (bf16[1,4,4,8,8,512]{5,4,3,2,1,0:T(8,128)(2,1)S(1)}, bf16[1,4,4,8,8,512]{5,4,3,2,1,0:T(8,128)(2,1)}, u32[]{:S(2)}) copy-start(bf16[1,4,4,8,8,512]{5,4,3,2,1,0:T(8,128)(2,1)} %param.6) | copy-start | bytes 3145732
  2.1 3.8 %collective-permute-start = (f32[9,8,512]{2,1,0:T(8,128)S(1)}, f32[9,8,512]{2,1,0:T(8,128)S(1)}, u32[]{:S(2)}, u32[]{:S(2)}) collective-permute-start(f32[9,8,512]{2,1,0:T(8,128)S(1)} %get-tuple-element.13), channel_id=1, source_target_pairs={{0,2},{4,6},{8,10},{12,14},{16,18},{20,22},{24,26},{28,30},{2,0},{... | collective-permute-start | bytes 442376 | tf_op jit(solution)/shard_map/ppermute | solution.py:40
  2.8 8.0 %collective-permute-start.1 = (f32[9,8,512]{2,1,0:T(8,128)S(1)}, f32[9,8,512]{2,1,0:T(8,128)S(1)}, u32[]{:S(2)}, u32[]{:S(2)}) collective-permute-start(f32[9,8,512]{2,1,0:T(8,128)S(1)} %get-tuple-element.15), channel_id=1, source_target_pairs={{2,4},{6,8},{10,12},{14,16},{18,20},{22,24},{26,28},{4,2},{8,6},{1... | collective-permute-start | bytes 442376 | tf_op jit(solution)/shard_map/ppermute | solution.py:40
  5.9 0.7 %copy-start.3 = (f32[2,8]{1,0:T(2,128)S(1)}, f32[2,8]{1,0:T(2,128)}, u32[]{:S(2)}) copy-start(f32[2,8]{1,0:T(2,128)} %diffusivity.3) | copy-start | bytes 196
  8.0 5.3 %collective-permute-start.2 = (bf16[2,4,8,512]{3,2,1,0:T(8,128)(2,1)S(1)}, bf16[2,4,8,512]{3,2,1,0:T(8,128)(2,1)S(1)}, u32[]{:S(2)}, u32[]{:S(2)}) collective-permute-start(bf16[2,4,8,512]{3,2,1,0:T(8,128)(2,1)S(1)} %get-tuple-element.14.refs_2_), channel_id=1, source_target_pairs={{0,1},{1,0},{2,3},{3,2},{4,5},{5,4},{6,7},{7,6},{8,9},{9,8},{10,11... | collective-permute-start | bytes 196616 | tf_op jit(solution)/shard_map/ppermute | solution.py:351
  11.9 1.3 %copy-start.4 = (s32[4]{0:T(128)S(1)}, s32[4]{0:T(128)}, u32[]{:S(2)}) copy-start(s32[4]{0:T(128)} %refs_1_.1) | copy-start | bytes 52
  11.9 4.0 %collective-permute-start.3 = (bf16[2,4,8,512]{3,2,1,0:T(8,128)(2,1)S(1)}, bf16[2,4,8,512]{3,2,1,0:T(8,128)(2,1)S(1)}, u32[]{:S(2)}, u32[]{:S(2)}) collective-permute-start(bf16[2,4,8,512]{3,2,1,0:T(8,128)(2,1)S(1)} %outer_rows.1.refs_3_), channel_id=1, source_target_pairs={{0,1},{1,0},{2,3},{3,2},{4,5},{5,4},{6,7},{7,6},{8,9},{9,8},{10,11... | collective-permute-start | bytes 196616 | tf_op jit(solution)/shard_map/ppermute | solution.py:351

commit v3 on v2

--- a/solution.py
+++ b/solution.py
@@ -40,10 +40,21 @@
     return lax.ppermute(value, axis, pairs + [(b, a) for a, b in pairs])
 
 
-def pack_kernel(controls, mask, within, across, rows, sems):
+def swap_across(value):
+    tiles, times = lax.axis_size("tile"), lax.axis_size("tm")
+    pairs = [((i, t), (i + 1, t)) for i in range(1, tiles - 1, 2) for t in range(times)]
+    pairs += [((i, t), (i, t + 1)) for i in (0, tiles - 1) for t in range(0, times, 2)]
+    flat = [(a * times + t, b * times + u) for (a, t), (b, u) in pairs]
+    return lax.ppermute(value, ("tile", "tm"), flat + [(b, a) for a, b in flat])
+
+
+def pack_kernel(controls, mask, diffusivity, within, across, by_level, rows, scalars, sems):
     odd = parity()
     slots = controls.shape[0]
-    copies = [pltpu.make_async_copy(mask, rows, sems.at[2 * slots])]
+    copies = [
+        pltpu.make_async_copy(mask, rows, sems.at[2 * slots]),
+        pltpu.make_async_copy(diffusivity, scalars, sems.at[2 * slots + 1]),
+    ]
     for slot in range(slots):
         for side, (start, packet) in enumerate(((outer_start(odd), across), (inner_start(odd), within))):
             copies.append(
@@ -59,21 +70,20 @@
     code = rows[...].astype(jnp.float32) + 1.0
     within[SWEEPS * slots] = code
     across[SWEEPS * slots] = code
-    for copy in copies[1:]:
+    copies[1].wait()
+    shape = by_level.shape[1:]
+    level = lax.broadcasted_iota(jnp.int32, shape, 0)
+    for kind in range(2):
+        value = jnp.full(shape, scalars[kind, 0], jnp.float32)
+        for index in range(1, shape[0]):
+            value = jnp.where(level == index, scalars[kind, index], value)
+        by_level[kind] = value
+    for copy in copies[2:]:
         copy.wait()
 
 
-def by_level(diffusivity, kind, shape):
-    level = lax.broadcasted_iota(jnp.int32, shape, 0)
-    value = jnp.full(shape, diffusivity[kind, 0], jnp.float32)
-    for index in range(1, shape[0]):
-        value = jnp.where(level == index, diffusivity[kind, index], value)
-    return value
-
-
 def kappa_of(code, sea, land):
-    code = jnp.broadcast_to(code, sea.shape)
-    return jnp.where(code == 2.0, land, jnp.where(code == 1.0, sea, 0.0))
+    return jnp.where(jnp.broadcast_to(code, sea.shape) == 2.0, land, sea)
 
 
 def along_row(kappa):
@@ -96,11 +106,10 @@
 FACE, EAST, WEST, CENTRE, KAPPA = 0, 4, 8, 12, 16
 
 
-def inner_kernel(controls, packet, mask, diffusivity, weights, kept, coef, face, centre, east, west, field):
+def inner_kernel(controls, packet, mine, by_level, weights, kept, coef, face, centre, east, west, field):
     odd = parity()
     slots, _, levels, columns = controls.shape
-    shape = (levels, columns)
-    sea, land = by_level(diffusivity, 0, shape), by_level(diffusivity, 1, shape)
+    sea, land = by_level[0], by_level[1]
     total = 3 * SWEEPS
 
     def far_row(k):
@@ -108,7 +117,7 @@
 
     def kappa_at(j):
         if j < 2 * SWEEPS:
-            code = mask[pl.ds(own_row(odd, j), 1), :].astype(jnp.float32) + 1.0
+            code = mine[slots * SWEEPS, pl.ds(own_row(odd, j), 1), :]
         else:
             place = far_row(j - 2 * SWEEPS) + SWEEPS * odd
             code = packet[slots * SWEEPS, pl.ds(place, 1), :]
@@ -159,12 +168,11 @@
                 before, here = here, after
 
 
-def outer_kernel(controls, packet, kept, coef, diffusivity, weights, face, centre, east, west, field):
+def outer_kernel(controls, packet, kept, coef, by_level, weights, face, centre, east, west, field):
     odd = parity()
     tile, tiles = lax.axis_index("tile"), lax.axis_size("tile")
     slots, _, levels, columns = controls.shape
-    shape = (levels, columns)
-    sea, land = by_level(diffusivity, 0, shape), by_level(diffusivity, 1, shape)
+    sea, land = by_level[0], by_level[1]
     edge = jnp.where(odd == 1, tile == tiles - 1, tile == 0)
     inside = jnp.where(edge, 0.0, 1.0).astype(jnp.float32)
 
@@ -176,7 +184,7 @@
     for j in range(-SWEEPS, 1):
         if j < 0:
             place = far_row(-1 - j) + SWEEPS * (1 - odd)
-            kappa = kappa_of(packet[slots * SWEEPS, pl.ds(place, 1), :], sea, land)
+            kappa = kappa_of(packet[slots * SWEEPS, pl.ds(place, 1), :], sea, land) * inside
         else:
             kappa = coef[KAPPA]
         if previous is not None:
@@ -206,7 +214,7 @@
                 if sweep == 1:
                     if j >= 0:
                         return controls[slot, own_row(odd, j)]
-                    return packet[SWEEPS * slot + far_row(-1 - j)]
+                    return packet[SWEEPS * slot + far_row(-1 - j)] * inside
                 if j >= sweep - 1:
                     return kept[slot, 2 * (sweep - 2) + j - (sweep - 1)]
                 return field[sweep - 2, slot, j + SWEEPS]
@@ -321,30 +329,40 @@
     half = pltpu.VMEM((slots, SWEEPS, *row), bf16)
     dma = pltpu.SemaphoreType.DMA
 
-    within, across = pl.pallas_call(
+    def near(value):
+        return pltpu.with_memory_space_constraint(value, pltpu.VMEM)
+
+    def far(value):
+        return pltpu.with_memory_space_constraint(value, pltpu.HBM)
+
+    my_within, my_across, by_level = pl.pallas_call(
         pack_kernel,
-        out_shape=(packet, packet),
-        in_specs=[ANY, ANY],
-        out_specs=(VMEM, VMEM),
-        scratch_shapes=[pltpu.VMEM((height, columns), land_mask.dtype), dma((2 * slots + 1,))],
+        out_shape=(packet, packet, pltpu.VMEM((2, *row), f32)),
+        in_specs=[ANY, ANY, ANY],
+        out_specs=(VMEM, VMEM, VMEM),
+        scratch_shapes=[
+            pltpu.VMEM((height, columns), land_mask.dtype),
+            pltpu.SMEM((2, levels), f32),
+            dma((2 * slots + 2,)),
+        ],
         compiler_params=PARAMS,
         name="pack",
-    )(controls, land_mask)
-    within = swap(within, "tile", 0)
-    across = swap(across, "tile", 1)
-
-    mine = pltpu.with_memory_space_constraint(controls, pltpu.VMEM)
+    )(far(controls), far(land_mask), far(diffusivity))
+    across = swap_across(my_across)
+    within = swap(my_within, "tile", 0)
+
+    mine = near(controls)
     inner, kept, coef = pl.pallas_call(
         inner_kernel,
         out_shape=(half, pltpu.VMEM((slots, 6, *row), f32), pltpu.VMEM((17, *row), f32)),
-        in_specs=[VMEM, VMEM, VMEM, SMEM],
+        in_specs=[VMEM, VMEM, VMEM, VMEM],
         out_specs=(VMEM, VMEM, VMEM),
         scratch_shapes=[pltpu.VMEM((3 * SWEEPS, *row), f32)] * 4
         + [pltpu.VMEM((SWEEPS - 1, slots, 3 * SWEEPS, *row), f32)],
         compiler_params=PARAMS,
         cost_estimate=cost(4_000_000, 1_000_000),
         name="inner_rows",
-    )(mine, pltpu.with_memory_space_constraint(within, pltpu.VMEM), land_mask, diffusivity)
+    )(mine, near(within), near(my_within), near(by_level))
 
     def shift(value):
         return [
@@ -356,18 +374,15 @@
     outer = pl.pallas_call(
         outer_kernel,
         out_shape=half,
-        in_specs=[VMEM, VMEM, VMEM, VMEM, SMEM],
+        in_specs=[VMEM, VMEM, VMEM, VMEM, VMEM],
         out_specs=VMEM,
         scratch_shapes=[pltpu.VMEM((SWEEPS + 1, *row), f32)] * 4
         + [pltpu.VMEM((SWEEPS - 1, slots, 2 * SWEEPS, *row), f32)],
         compiler_params=PARAMS,
         cost_estimate=cost(2_000_000, 1_000_000),
         name="outer_rows",
-    )(mine, pltpu.with_memory_space_constraint(across, pltpu.VMEM), kept, coef, diffusivity)
+    )(mine, near(across), near(kept), near(coef), near(by_level))
     outer_arrived = shift(outer)
-
-    def near(value):
-        return pltpu.with_memory_space_constraint(value, pltpu.VMEM)
 
     arrivals = count - 1
     result = jax.ShapeDtypeStruct((variables, height, *row), f32)
@@ -382,7 +397,7 @@
         compiler_params=PARAMS,
         cost_estimate=cost(4_000_000, 2_000_000),
         name="early_products",
-    )(near(perturbations[0]), owner, inner, outer, *map(near, inner_arrived))
+    )(near(perturbations[0]), owner, near(inner), near(outer), *map(near, inner_arrived))
     out = pl.pallas_call(
         lambda *refs: late_kernel(arrivals, factor, *refs),
         out_shape=result,
@@ -393,7 +408,7 @@
         compiler_params=PARAMS,
         cost_estimate=cost(1_000_000, 1_000_000),
         name="late_products",
-    )(partial, chosen, *map(near, outer_arrived), out)
+    )(near(partial), near(chosen), *map(near, outer_arrived), out)
     return out[None]
 
 

time: 17 us -> 13.4 us (0.79)
  local copies, waits for them, and re-layouts: 2.35 us -> 0.01 us
  starting transfers between devices: 6.37 us -> 4.52 us
  waiting for transfers between devices: 2.72 us -> 3.9 us
  Pallas kernels: 5.18 us -> 4.74 us
    ppermute x2 -> x1, starting transfers between devices: 3.76 us -> 0.74 us  [swap(): return lax.ppermute(value, axis, pairs + [(b, a) for a, b in pairs])]
    ppermute x0 -> x1, waiting for transfers between devices: none -> 2.95 us  [swap_across(): return lax.ppermute(value, ('tile', 'tm'), flat + [(b, a) for a, b in flat])]
    unnamed x10 -> x6, local copies, waits for them, and re-layouts: 2.35 us -> 0.01 us
    ppermute x2 -> x1, waiting for transfers between devices: 1.55 us -> 0.01 us  [swap(): return lax.ppermute(value, axis, pairs + [(b, a) for a, b in pairs])]
    ppermute x0 -> x1, starting transfers between devices: none -> 1.17 us  [swap_across(): return lax.ppermute(value, ('tile', 'tm'), flat + [(b, a) for a, b in flat])]
    pallas_call x1, Pallas kernels: 0.39 us -> 1.1 us  [on_device(): pl.pallas_call(pack_kernel, out_shape=(packet, packet, pltpu.VMEM((2, *ro...]
    pallas_call x1, Pallas kernels: 1.45 us -> 0.87 us  [on_device(): pl.pallas_call(inner_kernel, out_shape=(half, pltpu.VMEM((slots, 6, *row)...]
    pallas_call x1, Pallas kernels: 1.08 us -> 0.51 us  [on_device(): pl.pallas_call(outer_kernel, out_shape=half, in_specs=[VMEM, VMEM, VMEM,...]
  transfers between devices with their start and end apart: 4 -> 4, of which waited for: 2 -> 2; matrix products, arithmetic and copies ran while one was open for 0% -> 0% of each run, Pallas kernels for 24% -> 22%
where the time goes in v3:
time: 13.4 us; the launch traced here: 13.2 us
  Pallas kernels  4.74 us (35%)
  starting transfers between devices  4.52 us (34%)
  waiting for transfers between devices  3.9 us (29%)
    ppermute x1, waiting for transfers between devices, swap_across(): return lax.ppermute(value, ('tile', 'tm'), flat + [(b, a) for a, b in flat])  2.95 us
    ppermute x2, starting transfers between devices, shift(): lax.ppermute(value, 'tm', [(i, (i + step) % count) for i in range(count)])  2.61 us
    pallas_call x1, Pallas kernels, on_device(): pl.pallas_call(lambda *refs: early_kernel(arrivals, factor, *refs), out_s...  1.51 us
    ppermute x1, starting transfers between devices, swap_across(): return lax.ppermute(value, ('tile', 'tm'), flat + [(b, a) for a, b in flat])  1.17 us
    pallas_call x1, Pallas kernels, on_device(): pl.pallas_call(pack_kernel, out_shape=(packet, packet, pltpu.VMEM((2, *ro...  1.1 us
    ppermute x2, waiting for transfers between devices, shift(): lax.ppermute(value, 'tm', [(i, (i + step) % count) for i in range(count)])  0.95 us
    pallas_call x1, Pallas kernels, on_device(): pl.pallas_call(inner_kernel, out_shape=(half, pltpu.VMEM((slots, 6, *row)...  0.87 us
    pallas_call x1, Pallas kernels, on_device(): pl.pallas_call(lambda *refs: late_kernel(arrivals, factor, *refs), out_sh...  0.75 us
  transfers between devices with their start and end apart: 4, of which 2 were waited for; matrix products, arithmetic and copies ran while one was open for 0% of the time, Pallas kernels for 22%

profile of v3, /device:TPU:9, one launch (start us, length us, event | category | flops | bytes accessed | tf_op | source)
XLA Modules:
  0.0 13.2 jit_solution(4313100967536919734)
XLA Ops:
  0.0 0.0 copy-start
  0.0 0.0 copy-start.1
  0.0 1.1 %pack.1 = (f32[9,8,512]{2,1,0:T(8,128)S(1)}, f32[9,8,512]{2,1,0:T(8,128)S(1)}, f32[2,8,512]{2,1,0:T(8,128)S(1)}) custom-call(f32[2,8,8,512]{3,2,1,0:T(8,128)} %controls.5, s32[8,512]{1,0:T(8,128)} %mask.1, f32[2,8]{1,0:T(2,128)} %diffusivity.1), custom_call_target="tpu_custom_call" | custom-call | tf_op jit(solution)/shard_map/pack/pallas_call | solution.py:338
  1.1 0.7 %collective-permute-start = (f32[9,8,512]{2,1,0:T(8,128)S(1)}, f32[9,8,512]{2,1,0:T(8,128)S(1)}, u32[]{:S(2)}, u32[]{:S(2)}) collective-permute-start(f32[9,8,512]{2,1,0:T(8,128)S(1)} %get-tuple-element.14.mine), channel_id=1, source_target_pairs={{0,2},{4,6},{8,10},{12,14},{16,18},{20,22},{24,26},{28,30},{2,0},{... | collective-permute-start | bytes 442376 | tf_op jit(solution)/shard_map/ppermute | solution.py:40
  1.9 1.2 %collective-permute-start.1 = (f32[9,8,512]{2,1,0:T(8,128)S(1)}, f32[9,8,512]{2,1,0:T(8,128)S(1)}, u32[]{:S(2)}, u32[]{:S(2)}) collective-permute-start(f32[9,8,512]{2,1,0:T(8,128)S(1)} %get-tuple-element.17), channel_id=1, source_target_pairs={{2,4},{3,5},{6,8},{7,9},{10,12},{11,13},{14,16},{15,17},{18,20},{1... | collective-permute-start | bytes 442376 | tf_op jit(solution)/shard_map/ppermute | solution.py:48
  3.0 0.0 collective-permute-done.packet
  3.0 0.0 copy-done
  3.0 0.9 %inner_rows.1 = (bf16[2,4,8,512]{3,2,1,0:T(8,128)(2,1)S(1)}, f32[2,6,8,512]{3,2,1,0:T(8,128)S(1)}, f32[17,8,512]{2,1,0:T(8,128)S(1)}) custom-call(f32[2,8,8,512]{3,2,1,0:T(8,128)S(1)} %copy-done, f32[9,8,512]{2,1,0:T(8,128)S(1)} %collective-permute-done.packet, f32[9,8,512]{2,1,0:T(8,128)S(1)} %get-tuple-element.14.mine, ...), custom_call_target="tpu_custom_call" | custom-call | flops 4000000 | bytes 1000000 | tf_op jit(solution)/shard_map/inner_rows/pallas_call | solution.py:355
  3.9 1.3 %collective-permute-start.2 = (bf16[2,4,8,512]{3,2,1,0:T(8,128)(2,1)S(1)}, bf16[2,4,8,512]{3,2,1,0:T(8,128)(2,1)S(1)}, u32[]{:S(2)}, u32[]{:S(2)}) collective-permute-start(bf16[2,4,8,512]{3,2,1,0:T(8,128)(2,1)S(1)} %get-tuple-element.16.refs_2_), channel_id=1, source_target_pairs={{0,1},{1,0},{2,3},{3,2},{4,5},{5,4},{6,7},{7,6},{8,9},{9,8},{10,11... | collective-permute-start | bytes 196616 | tf_op jit(solution)/shard_map/ppermute | solution.py:369
  5.2 2.9 %collective-permute-done.1.packet = f32[9,8,512]{2,1,0:T(8,128)S(1)} collective-permute-done((f32[9,8,512]{2,1,0:T(8,128)S(1)}, f32[9,8,512]{2,1,0:T(8,128)S(1)}, u32[]{:S(2)}, u32[]{:S(2)}) %collective-permute-start.1) | collective-permute-done | bytes 147488 | tf_op jit(solution)/shard_map/ppermute | solution.py:48
  8.2 0.5 %outer_rows.1.refs_3_ = bf16[2,4,8,512]{3,2,1,0:T(8,128)(2,1)S(1)} custom-call(f32[2,8,8,512]{3,2,1,0:T(8,128)S(1)} %copy-done, f32[9,8,512]{2,1,0:T(8,128)S(1)} %collective-permute-done.1.packet, f32[2,6,8,512]{3,2,1,0:T(8,128)S(1)} %get-tuple-element.18.kept, f32[17,8,512]{2,1,0:T(8,128)S(1)} %get-tuple-element.19.coef, ...), custom_call_target="tpu_custom_call" | custom-call | flops 2000000 | bytes 1000000 | tf_op jit(solution)/shard_map/outer_rows/pallas_call | solution.py:374
  8.7 0.0 copy-start.2
  8.7 1.3 %collective-permute-start.3 = (bf16[2,4,8,512]{3,2,1,0:T(8,128)(2,1)S(1)}, bf16[2,4,8,512]{3,2,1,0:T(8,128)(2,1)S(1)}, u32[]{:S(2)}, u32[]{:S(2)}) collective-permute-start(bf16[2,4,8,512]{3,2,1,0:T(8,128)(2,1)S(1)} %outer_rows.1.refs_3_), channel_id=1, source_target_pairs={{0,1},{1,0},{2,3},{3,2},{4,5},{5,4},{6,7},{7,6},{8,9},{9,8},{10,11... | collective-permute-start | bytes 196616 | tf_op jit(solution)/shard_map/ppermute | solution.py:369
  10.0 0.0 collective-permute-done.2.refs_4_
  10.0 0.0 copy-done.1
  10.0 0.0 copy-done.2
  10.0 1.5 %early_products.1 = (f32[4,8,8,512]{3,2,1,0:T(8,128)}, f32[4,4,8,512]{3,2,1,0:T(8,128)S(1)}, bf16[2,4,4,8,512]{4,3,2,1,0:T(8,128)(2,1)S(1)}) custom-call(bf16[4,4,8,8,512]{4,3,2,1,0:T(8,128)(2,1)S(1)} %bitcast.2, s32[4]{0:T(128)S(1)} %copy-done.2, bf16[2,4,8,512]{3,2,1,0:T(8,128)(2,1)S(1)} %get-tuple-element.16.refs_2_, ...), custom_call_target="tpu_custom_call" | custom-call | flops 4000000 | bytes 2000000 | tf_op jit(solution)/shard_map/early_products/pallas_call | solution.py:391
  11.5 0.9 %collective-permute-done.3.refs_2_ = bf16[2,4,8,512]{3,2,1,0:T(8,128)(2,1)S(1)} collective-permute-done((bf16[2,4,8,512]{3,2,1,0:T(8,128)(2,1)S(1)}, bf16[2,4,8,512]{3,2,1,0:T(8,128)(2,1)S(1)}, u32[]{:S(2)}, u32[]{:S(2)}) %collective-permute-start.3) | collective-permute-done | bytes 65568 | tf_op jit(solution)/shard_map/ppermute | solution.py:369
  12.5 0.8 %late_products.1 = f32[4,8,8,512]{3,2,1,0:T(8,128)} custom-call(f32[4,4,8,512]{3,2,1,0:T(8,128)S(1)} %get-tuple-element.20.refs_0_, bf16[2,4,4,8,512]{4,3,2,1,0:T(8,128)(2,1)S(1)} %get-tuple-element.21.refs_1_, bf16[2,4,8,512]{3,2,1,0:T(8,128)(2,1)S(1)} %collective-permute-done.3.refs_2_, ...), custom_call_target="tpu_custom_call", output_to_operand_aliasing={{}: (3, {})} | custom-call | flops 1000000 | bytes 1000000 | tf_op jit(solution)/shard_map/late_products/pallas_call | solution.py:401
Async XLA Ops:
  0.0 3.0 %copy-start = (f32[2,8,8,512]{3,2,1,0:T(8,128)S(1)}, f32[2,8,8,512]{3,2,1,0:T(8,128)}, u32[]{:S(2)}) copy-start(f32[2,8,8,512]{3,2,1,0:T(8,128)} %controls.5) | copy-start | bytes 786436
  0.0 10.0 %copy-start.1 = (bf16[1,4,4,8,8,512]{5,4,3,2,1,0:T(8,128)(2,1)S(1)}, bf16[1,4,4,8,8,512]{5,4,3,2,1,0:T(8,128)(2,1)}, u32[]{:S(2)}) copy-start(bf16[1,4,4,8,8,512]{5,4,3,2,1,0:T(8,128)(2,1)} %param.6) | copy-start | bytes 3145732
  1.1 1.9 %collective-permute-start = (f32[9,8,512]{2,1,0:T(8,128)S(1)}, f32[9,8,512]{2,1,0:T(8,128)S(1)}, u32[]{:S(2)}, u32[]{:S(2)}) collective-permute-start(f32[9,8,512]{2,1,0:T(8,128)S(1)} %get-tuple-element.14.mine), channel_id=1, source_target_pairs={{0,2},{4,6},{8,10},{12,14},{16,18},{20,22},{24,26},{28,30},{2,0},{... | collective-permute-start | bytes 442376 | tf_op jit(solution)/shard_map/ppermute | solution.py:40
  1.9 6.3 %collective-permute-start.1 = (f32[9,8,512]{2,1,0:T(8,128)S(1)}, f32[9,8,512]{2,1,0:T(8,128)S(1)}, u32[]{:S(2)}, u32[]{:S(2)}) collective-permute-start(f32[9,8,512]{2,1,0:T(8,128)S(1)} %get-tuple-element.17), channel_id=1, source_target_pairs={{2,4},{3,5},{6,8},{7,9},{10,12},{11,13},{14,16},{15,17},{18,20},{1... | collective-permute-start | bytes 442376 | tf_op jit(solution)/shard_map/ppermute | solution.py:48
  3.9 6.1 %collective-permute-start.2 = (bf16[2,4,8,512]{3,2,1,0:T(8,128)(2,1)S(1)}, bf16[2,4,8,512]{3,2,1,0:T(8,128)(2,1)S(1)}, u32[]{:S(2)}, u32[]{:S(2)}) collective-permute-start(bf16[2,4,8,512]{3,2,1,0:T(8,128)(2,1)S(1)} %get-tuple-element.16.refs_2_), channel_id=1, source_target_pairs={{0,1},{1,0},{2,3},{3,2},{4,5},{5,4},{6,7},{7,6},{8,9},{9,8},{10,11... | collective-permute-start | bytes 196616 | tf_op jit(solution)/shard_map/ppermute | solution.py:369
  8.7 1.3 %copy-start.2 = (s32[4]{0:T(128)S(1)}, s32[4]{0:T(128)}, u32[]{:S(2)}) copy-start(s32[4]{0:T(128)} %refs_1_.1) | copy-start | bytes 52
  8.7 3.8 %collective-permute-start.3 = (bf16[2,4,8,512]{3,2,1,0:T(8,128)(2,1)S(1)}, bf16[2,4,8,512]{3,2,1,0:T(8,128)(2,1)S(1)}, u32[]{:S(2)}, u32[]{:S(2)}) collective-permute-start(bf16[2,4,8,512]{3,2,1,0:T(8,128)(2,1)S(1)} %outer_rows.1.refs_3_), channel_id=1, source_target_pairs={{0,1},{1,0},{2,3},{3,2},{4,5},{5,4},{6,7},{7,6},{8,9},{9,8},{10,11... | collective-permute-start | bytes 196616 | tf_op jit(solution)/shard_map/ppermute | solution.py:369

commit v4 on v0

v4 whole, which is shorter than its diff:
```python
import math

import jax
import jax.numpy as jnp
from jax import lax
from jax.experimental import pallas as pl
from jax.experimental.pallas import tpu as pltpu
from jax.sharding import PartitionSpec as P

SWEEPS = 4
VMEM = pl.BlockSpec(memory_space=pltpu.VMEM)
SMEM = pl.BlockSpec(memory_space=pltpu.SMEM)
ANY = pl.BlockSpec(memory_space=pl.ANY)
PARAMS = pltpu.CompilerParams(vmem_limit_bytes=16 * 1024 * 1024)


def parity():
    return lax.rem(lax.axis_index("tile"), 2)


def own_row(odd, j):
    return j + odd * (2 * SWEEPS - 1 - 2 * j)


def half_row(odd, j):
    return j % SWEEPS + odd * (SWEEPS - 1 - 2 * (j % SWEEPS))


def outer_start(odd):
    return SWEEPS * odd


def inner_start(odd):
    return SWEEPS * (1 - odd)


def swap_within(value):
    pairs = [(i, i + 1) for i in range(0, lax.axis_size("tile"), 2)]
    return lax.ppermute(value, "tile", pairs + [(b, a) for a, b in pairs])


def swap_across(value):
    tiles, times = lax.axis_size("tile"), lax.axis_size("tm")
    pairs = [((i, t), (i + 1, t)) for i in range(1, tiles - 1, 2) for t in range(times)]
    pairs += [((i, t), (i, t + 1)) for i in (0, tiles - 1) for t in range(0, times, 2)]
    flat = [(a * times + t, b * times + u) for (a, t), (b, u) in pairs]
    return lax.ppermute(value, ("tile", "tm"), flat + [(b, a) for a, b in flat])


def half_codes(odd, code):
    half = code.shape[1] // 2
    left, right = code[:, :half], code[:, half:]
    top = lax.broadcasted_iota(jnp.int32, left.shape, 0) < SWEEPS
    even = jnp.where(top, left, pltpu.roll(right, SWEEPS, 0))
    return jnp.where(odd == 1, jnp.where(top, pltpu.roll(left, SWEEPS, 0), right), even)


def pack_kernel(controls, mask, diffusivity, across, codes, table, rows, sems):
    odd = parity()
    slots, columns = controls.shape[0], controls.shape[3]
    half, count = columns // 2, slots * SWEEPS
    copies = [
        pltpu.make_async_copy(mask, rows, sems.at[0]),
        pltpu.make_async_copy(diffusivity, table, sems.at[1]),
    ]
    for slot in range(slots):
        for side in range(2):
            copies.append(
                pltpu.make_async_copy(
                    controls.at[slot, pl.ds(outer_start(odd), SWEEPS), :, pl.ds(side * half, half)],
                    across.at[pl.ds(side * count + slot * SWEEPS, SWEEPS)],
                    sems.at[len(copies)],
                )
            )
    for copy in copies[2:] + copies[:2]:
        copy.start()
    copies[0].wait()
    code = rows[...].astype(jnp.float32) + 1.0
    codes[...] = code
    across[2 * count] = half_codes(odd, code)
    for copy in copies[1:]:
        copy.wait()


def within_kernel(controls, codes, first, second):
    odd = parity()
    for slot, piece in enumerate((first, second)):
        for row in range(SWEEPS):
            piece[row] = controls[slot, inner_start(odd) + row]
    second[SWEEPS] = codes[...]


def by_level(table, kind, shape):
    level = lax.broadcasted_iota(jnp.int32, shape, 0)
    value = jnp.broadcast_to(table[kind : kind + 1, 0:1], shape)
    for index in range(1, shape[0]):
        value = jnp.where(level == index, table[kind : kind + 1, index : index + 1], value)
    return value


def kappa_of(code, sea, land):
    return jnp.where(jnp.broadcast_to(code, sea.shape) == 2.0, land, sea)


def along_row(kappa):
    columns = kappa.shape[1]
    lane = lax.broadcasted_iota(jnp.int32, kappa.shape, 1)
    last = lane == columns - 1
    loss = kappa + jnp.where(last, 0.0, pltpu.roll(kappa, columns - 1, 1))
    east = jnp.where(last, 0.0, loss)
    west = pltpu.roll(east, 1, 1)
    return east, west, loss + jnp.where(lane == 0, kappa, west)


def sideways(centre, east, west, here):
    columns = here.shape[1]
    return centre * here + east * pltpu.roll(here, columns - 1, 1) + west * pltpu.roll(here, 1, 1)


FACE, EAST, WEST, CENTRE, KAPPA, COEFS = 0, 4, 8, 12, 16, 17
PART, VALUE, KEPT = 0, SWEEPS, 2 * SWEEPS - 1
OUTER, INNER = 0, 1


def row_of(side, odd, k):
    return own_row(odd, k if side == OUTER else 2 * SWEEPS - 1 - k)


def middle_kernel(controls, codes, table, kept, coef, halves, face, centre, east, west, field):
    odd = parity()
    slots, _, levels, columns = controls.shape
    shape = (levels, columns)
    total = 2 * SWEEPS
    for kind in range(2):
        halves[kind] = 0.5 * by_level(table, kind, shape)
    sea, land = halves[0], halves[1]

    previous = lost = None
    for j in range(total):
        kappa = kappa_of(codes[pl.ds(own_row(odd, j), 1), :], sea, land)
        e, w, loss = along_row(kappa)
        east[j], west[j] = e, w
        if j:
            face[j] = previous + kappa
            centre[j - 1] = 1.0 - (lost + face[j])
            lost = loss + face[j]
        else:
            lost = loss
        previous = kappa
        for side, k in ((OUTER, j), (INNER, total - 1 - j)):
            if k == 0:
                coef[side, KAPPA] = kappa
            if k < SWEEPS:
                coef[side, EAST + k], coef[side, WEST + k] = e, w
    centre[total - 1] = 1.0 - lost
    for k in range(SWEEPS):
        coef[OUTER, CENTRE + k], coef[INNER, CENTRE + k] = centre[k], centre[total - 1 - k]
        if k:
            coef[OUTER, FACE + k], coef[INNER, FACE + k] = face[k], face[total - k]

    def value(slot, sweep, j):
        return field[sweep - 1, slot, j] if sweep else controls[slot, own_row(odd, j)]

    for sweep in range(1, SWEEPS + 1):
        low, high = sweep - 1, total - sweep
        before = [None] * slots
        here = [value(slot, sweep - 1, low) for slot in range(slots)]
        for j in range(low, high + 1):
            c, e, w = centre[j], east[j], west[j]
            below = face[j] if j > low else None
            above = face[j + 1] if j < high else None
            for slot in range(slots):
                after = None
                result = sideways(c, e, w, here[slot])
                if above is not None:
                    after = value(slot, sweep - 1, j + 1)
                    result = result + above * after
                if below is not None:
                    result = result + below * before[slot]
                if j == low:
                    kept[OUTER, slot, PART + sweep - 1] = result
                elif j == high:
                    kept[INNER, slot, PART + sweep - 1] = result
                else:
                    field[sweep - 1, slot, j] = result
                    if j == low + 1:
                        kept[OUTER, slot, VALUE + sweep - 1] = result
                    if j == high - 1:
                        kept[INNER, slot, VALUE + sweep - 1] = result
                before[slot], here[slot] = here[slot], after


def side_rows(side, odd, controls, far, far_kappa, inside, kept, coef, weights, face, centre, east, west, field):
    slots = controls.shape[0]

    def masked(value):
        return value if inside is None else value * inside

    previous = masked(far_kappa(-SWEEPS))
    lost = None
    for k in range(1 - SWEEPS, 1):
        i = k + SWEEPS
        kappa = masked(far_kappa(k)) if k else coef[side, KAPPA]
        step = previous + kappa
        face[i] = step
        if lost is not None:
            centre[i - 1] = 1.0 - (lost + step)
        if k:
            e, w, loss = along_row(kappa)
            east[i], west[i] = e, w
            lost = loss + step
        else:
            centre[i] = coef[side, CENTRE] - step
        previous = kappa
    first = face[SWEEPS]
    first_inside = masked(first)

    def value(slot, sweep, k):
        if sweep == 0:
            return masked(far(slot, k)) if k < 0 else controls[slot, row_of(side, odd, k)]
        if k == sweep:
            return kept[side, slot, VALUE + sweep - 1]
        return field[sweep - 1, slot, k + SWEEPS]

    for sweep in range(1, SWEEPS + 1):
        low = sweep - SWEEPS
        before = [value(slot, sweep - 1, low - 1) for slot in range(slots)]
        here = [value(slot, sweep - 1, low) for slot in range(slots)]
        for k in range(low, sweep):
            i = k + SWEEPS
            below = face[i] if k < 0 else first if k == 0 else coef[side, FACE + k]
            if k < sweep - 1:
                above = face[i + 1] if k < -1 else first_inside if k == -1 else coef[side, FACE + k + 1]
                c = centre[i] if k <= 0 else coef[side, CENTRE + k]
                e, w = (east[i], west[i]) if k < 0 else (coef[side, EAST + k], coef[side, WEST + k])
            for slot in range(slots):
                after = None
                if k < sweep - 1:
                    after = value(slot, sweep - 1, k + 1)
                    result = sideways(c, e, w, here[slot]) + above * after + below * before[slot]
                elif k == 0:
                    result = kept[side, slot, PART] + below * (before[slot] - here[slot])
                else:
                    result = kept[side, slot, PART + sweep - 1] + below * before[slot]
                if sweep == SWEEPS:
                    place = half_row(odd, k if side == OUTER else 2 * SWEEPS - 1 - k)
                    weights[slot, place] = result.astype(weights.dtype)
                else:
                    field[sweep - 1, slot, i] = result
                before[slot], here[slot] = here[slot], after


def inner_kernel(controls, first, second, kept, coef, halves, weights, *scratch):
    odd = parity()

    def place(k):
        return -1 - k + odd * (SWEEPS + 1 + 2 * k)

    def far(slot, k):
        return (first, second)[slot][place(k)]

    def far_kappa(k):
        return kappa_of(second[SWEEPS, pl.ds(place(k) + SWEEPS * odd, 1), :], halves[0], halves[1])

    side_rows(INNER, odd, controls, far, far_kappa, None, kept, coef, weights, *scratch)


def outer_kernel(controls, packet, kept, coef, halves, weights, *scratch):
    odd = parity()
    tile, tiles = lax.axis_index("tile"), lax.axis_size("tile")
    count = controls.shape[0] * SWEEPS
    edge = jnp.where(odd == 1, tile == tiles - 1, tile == 0)
    inside = jnp.where(edge, 0.0, 1.0).astype(jnp.float32)

    def place(k):
        return SWEEPS + k - odd * (2 * k + SWEEPS + 1)

    def far(slot, k):
        at = SWEEPS * slot + place(k)
        return jnp.concatenate([packet[at], packet[count + at]], axis=1)

    def far_kappa(k):
        left = packet[2 * count, pl.ds(place(k), 1), :]
        right = packet[2 * count, pl.ds(place(k) + SWEEPS, 1), :]
        return kappa_of(jnp.concatenate([left, right], axis=1), halves[0], halves[1])

    side_rows(OUTER, odd, controls, far, far_kappa, inside, kept, coef, weights, *scratch)


def products(pert, weight, total):
    return [
        term if old is None else old + term
        for old, term in zip(total, [p.astype(jnp.float32) * weight for p in pert])
    ]


def own_kernel(factor, pert, owner, inner, outer, near_part, far_part, near_others, far_others, sems):
    odd = parity()
    count, here = lax.axis_size("tm"), lax.axis_index("tm")
    slots, variables = inner.shape[0], pert.shape[1]

    def member(step, slot):
        return owner[lax.rem(here - step + count, count) * slots + slot]

    copies = []
    for step in range(1, count):
        for slot in range(slots):
            place = (step - 1) * slots + slot
            for side, (start, others) in enumerate(
                ((inner_start(odd), near_others), (outer_start(odd), far_others))
            ):
                copies.append(
                    pltpu.make_async_copy(
                        pert.at[member(step, slot), :, pl.ds(start, SWEEPS)],
                        others.at[place],
                        sems.at[2 * place + side],
                    )
                )
    for copy in copies:
        copy.start()
    for start, weights, part in (
        (inner_start(odd), inner, near_part),
        (outer_start(odd), outer, far_part),
    ):
        for row in range(SWEEPS):
            total = [None] * variables
            for slot in range(slots):
                weight = weights[slot, row].astype(jnp.float32) * factor
                who = member(0, slot)
                total = products([pert[who, v, start + row] for v in range(variables)], weight, total)
            for v in range(variables):
                part[v, row] = total[v]
    for copy in copies:
        copy.wait()


def add_others(factor, part, others, arrived, row):
    variables = part.shape[0]
    total = [part[v, row] for v in range(variables)]
    for index, weights in enumerate(arrived):
        slots = weights.shape[0]
        for slot in range(slots):
            weight = weights[slot, row].astype(jnp.float32) * factor
            place = index * slots + slot
            total = products([others[place, v, row] for v in range(variables)], weight, total)
    return total


def add_and_write(factor, start, part, others, arrived, out, ready, sems):
    for row in range(SWEEPS):
        for v, total in enumerate(add_others(factor, part, others, arrived, row)):
            ready[v, row] = total
    writes = [
        pltpu.make_async_copy(ready.at[v], out.at[v, pl.ds(start, SWEEPS)], sems.at[v])
        for v in range(part.shape[0])
    ]
    for copy in writes:
        copy.start()
    for copy in writes:
        copy.wait()


def near_kernel(factor, part, others, *refs):
    *arrived, out, ready, sems = refs
    add_and_write(factor, inner_start(parity()), part, others, arrived, out, ready, sems)


def far_kernel(factor, part, others, *refs):
    *arrived, _, out, ready, sems = refs
    add_and_write(factor, outer_start(parity()), part, others, arrived, out, ready, sems)


def cost(flops, moved):
    return pl.CostEstimate(flops=flops, bytes_accessed=moved, transcendentals=0)


def near(value):
    return pltpu.with_memory_space_constraint(value, pltpu.VMEM)


def far(value):
    return pltpu.with_memory_space_constraint(value, pltpu.HBM)


def on_device(controls, perturbations, owner, land_mask, diffusivity):
    slots, height, levels, columns = controls.shape
    members, variables = perturbations.shape[1:3]
    count = lax.axis_size("tm")
    factor = 1.0 / math.sqrt(owner.shape[0] - 1)
    row = (levels, columns)
    f32, bf16 = jnp.float32, jnp.bfloat16
    dma = pltpu.SemaphoreType.DMA

    packet = pltpu.VMEM((2 * slots * SWEEPS + 1, levels, columns // 2), f32)
    mine = near(controls)
    my_across, codes, table = pl.pallas_call(
        pack_kernel,
        out_shape=(packet, pltpu.VMEM((height, columns), f32), pltpu.VMEM((2, levels), f32)),
        in_specs=[ANY, ANY, ANY],
        out_specs=(VMEM, VMEM, VMEM),
        scratch_shapes=[pltpu.VMEM((height, columns), land_mask.dtype), dma((2 * slots + 2,))],
        compiler_params=PARAMS,
        name="pack",
    )(far(controls), far(land_mask), far(diffusivity))
    across = swap_across(my_across)
    my_within = pl.pallas_call(
        within_kernel,
        out_shape=(pltpu.VMEM((SWEEPS, *row), f32), pltpu.VMEM((SWEEPS + 1, *row), f32)),
        in_specs=[VMEM, VMEM],
        out_specs=(VMEM, VMEM),
        compiler_params=PARAMS,
        cost_estimate=cost(1, 1),
        name="pack_within",
    )(mine, near(codes))
    within = [swap_within(value) for value in my_within]

    kept, coef, halves = pl.pallas_call(
        middle_kernel,
        out_shape=(
            pltpu.VMEM((2, slots, KEPT, *row), f32),
            pltpu.VMEM((2, COEFS, *row), f32),
            pltpu.VMEM((2, *row), f32),
        ),
        in_specs=[VMEM] * 3,
        out_specs=(VMEM,) * 3,
        scratch_shapes=[pltpu.VMEM((height, *row), f32)] * 4
        + [pltpu.VMEM((SWEEPS - 1, slots, height, *row), f32)],
        compiler_params=PARAMS,
        cost_estimate=cost(1, 1),
        name="middle",
    )(mine, near(codes), near(table))
    shared = (near(kept), near(coef), near(halves))

    def side(kernel, arrived, name):
        return pl.pallas_call(
            kernel,
            out_shape=pltpu.VMEM((slots, SWEEPS, *row), bf16),
            in_specs=[VMEM] * (4 + len(arrived)),
            out_specs=VMEM,
            scratch_shapes=[pltpu.VMEM((SWEEPS + 1, *row), f32)] * 4
            + [pltpu.VMEM((SWEEPS - 1, slots, 2 * SWEEPS, *row), f32)],
            compiler_params=PARAMS,
            cost_estimate=cost(1, 1),
            name=name,
        )(mine, *map(near, arrived), *shared)

    inner = side(inner_kernel, within, "inner_rows")

    def shift(value):
        return [
            near(lax.ppermute(value, "tm", [(i, (i + step) % count) for i in range(count)]))
            for step in range(1, count)
        ]

    inner_arrived = shift(inner)
    outer = side(outer_kernel, [across], "outer_rows")
    outer_arrived = shift(outer)

    arrivals = count - 1
    part = pltpu.VMEM((variables, SWEEPS, *row), f32)
    others = pltpu.VMEM((max(arrivals, 1) * slots, variables, SWEEPS, *row), bf16)
    near_part, far_part, near_others, far_others = pl.pallas_call(
        lambda *refs: own_kernel(factor, *refs),
        out_shape=(part, part, others, others),
        in_specs=[VMEM, SMEM, VMEM, VMEM],
        out_specs=(VMEM,) * 4,
        scratch_shapes=[dma((2 * max(arrivals, 1) * slots,))],
        compiler_params=PARAMS,
        cost_estimate=cost(4_000_000, 2_000_000),
        name="own_products",
    )(near(perturbations[0]), owner, near(inner), near(outer))
    result = jax.ShapeDtypeStruct((variables, height, *row), f32)
    scratch = [pltpu.VMEM((variables, SWEEPS, *row), f32), dma((variables,))]
    out = pl.pallas_call(
        lambda *refs: near_kernel(factor, *refs),
        out_shape=result,
        in_specs=[VMEM] * (2 + arrivals),
        out_specs=ANY,
        scratch_shapes=scratch,
        compiler_params=PARAMS,
        cost_estimate=cost(1_000_000, 1_000_000),
        name="near_products",
    )(near(near_part), near(near_others), *inner_arrived)
    out = pl.pallas_call(
        lambda *refs: far_kernel(factor, *refs),
        out_shape=result,
        in_specs=[VMEM] * (2 + arrivals) + [ANY],
        out_specs=ANY,
        scratch_shapes=scratch,
        input_output_aliases={2 + arrivals: 0},
        compiler_params=PARAMS,
        cost_estimate=cost(1_000_000, 1_000_000),
        name="far_products",
    )(near(far_part), near(far_others), *outer_arrived, out)
    return out[None]


def solution(mesh):
    return jax.shard_map(
        on_device,
        mesh=mesh,
        in_specs=(
            P("tm", "tile", None, None),
            P("tm", None, None, "tile", None, None),
            P(),
            P("tile", None),
            P(),
        ),
        out_specs=P("tm", None, "tile", None, None),
        check_vma=False,
    )
```

time: 86.6 us -> 13.1 us (0.15)
  waiting for transfers between devices: 32.8 us -> 1.2 us
  starting transfers between devices: 29.2 us -> 6.82 us
  between operations: 13.7 us -> 0.08 us
  other arithmetic: 6.08 us -> 0 us
  Pallas kernels: 0 us -> 4.78 us
  local copies, waits for them, and re-layouts: 4.28 us -> 0.02 us
    psum x1 -> x0, waiting for transfers between devices: 25.6 us -> none  [spread(): return lax.psum(kept, axis)]
    ppermute x10 -> x5, starting transfers between devices: 29.2 us -> 6.82 us  [the longest x2 3.21 us: shift(): lax.ppermute(value, 'tm', [(i, (i + step) % count) for i in range(count)])]
    ppermute x10 -> x5, waiting for transfers between devices: 7.25 us -> 1.2 us  [the longest x2 0.94 us: shift(): lax.ppermute(value, 'tm', [(i, (i + step) % count) for i in range(count)])]
    pallas_call x0 -> x8, Pallas kernels: none -> 4.78 us  [the longest x1 0.9 us: on_device(): pl.pallas_call(pack_kernel, out_shape=(packet, pltpu.VMEM((height, column...]
    select_n x3 -> x0, other arithmetic: 1.61 us -> none  [the longest x2 1.53 us: spread(): jnp.where(lax.axis_index(axis) == source, value, 0).astype(value.dtype)]
    unnamed x8 -> x6, local copies, waits for them, and re-layouts: 1.42 us -> 0.02 us
    gather x2 -> x0, local copies, waits for them, and re-layouts: 1.16 us -> none  [on_device(): selected = jnp.take(pert_here, chosen, axis=0)]
    unnamed x1 -> x0, other arithmetic: 1.02 us -> none
  transfers between devices with their start and end apart: 11 -> 5, of which waited for: 5 -> 2; matrix products, arithmetic and copies ran while one was open for 3% -> 0% of each run, Pallas kernels for 0% -> 24%
where the time goes in v4:
time: 13.1 us; the launch traced here: 12.9 us
  starting transfers between devices  6.82 us (52%)
  Pallas kernels  4.78 us (36%)
  waiting for transfers between devices  1.2 us (9%)
    ppermute x2, starting transfers between devices, shift(): lax.ppermute(value, 'tm', [(i, (i + step) % count) for i in range(count)])  3.21 us
    ppermute x1, starting transfers between devices, swap_across(): return lax.ppermute(value, ('tile', 'tm'), flat + [(b, a) for a, b in flat])  3.03 us
    ppermute x2, waiting for transfers between devices, shift(): lax.ppermute(value, 'tm', [(i, (i + step) % count) for i in range(count)])  0.94 us
    pallas_call x1, Pallas kernels, on_device(): pl.pallas_call(pack_kernel, out_shape=(packet, pltpu.VMEM((height, column...  0.9 us
    pallas_call x1, Pallas kernels, on_device(): pl.pallas_call(lambda *refs: own_kernel(factor, *refs), out_shape=(part,...  0.87 us
    pallas_call x1, Pallas kernels, on_device(): pl.pallas_call(lambda *refs: near_kernel(factor, *refs), out_shape=result...  0.79 us
    pallas_call x1, Pallas kernels, on_device(): pl.pallas_call(lambda *refs: far_kernel(factor, *refs), out_shape=result,...  0.79 us
    pallas_call x2, Pallas kernels, side(): pl.pallas_call(kernel, out_shape=pltpu.VMEM((slots, SWEEPS, *row), bf16),...  0.77 us
  transfers between devices with their start and end apart: 5, of which 2 were waited for; matrix products, arithmetic and copies ran while one was open for 0% of the time, Pallas kernels for 24%

profile of v4, /device:TPU:0, one launch (start us, length us, event | category | flops | bytes accessed | tf_op | source)
XLA Modules:
  0.0 12.9 jit_solution(130017168845391890)
XLA Ops:
  0.0 0.0 copy-start
  0.0 0.9 %pack.1 = (f32[17,8,256]{2,1,0:T(8,128)S(1)}, f32[8,512]{1,0:T(8,128)S(1)}, f32[2,8]{1,0:T(2,128)S(1)}) custom-call(f32[2,8,8,512]{3,2,1,0:T(8,128)} %controls.9, s32[8,512]{1,0:T(8,128)} %mask.1, f32[2,8]{1,0:T(2,128)} %diffusivity.1), custom_call_target="tpu_custom_call" | custom-call | tf_op jit(solution)/shard_map/pack/pallas_call | solution.py:396
  0.9 3.0 %collective-permute-start.2 = (f32[17,8,256]{2,1,0:T(8,128)S(1)}, f32[17,8,256]{2,1,0:T(8,128)S(1)}, u32[]{:S(2)}, u32[]{:S(2)}) collective-permute-start(f32[17,8,256]{2,1,0:T(8,128)S(1)} %get-tuple-element.24), channel_id=1, source_target_pairs={{2,4},{3,5},{6,8},{7,9},{10,12},{11,13},{14,16},{15,17},{18,20},{1... | collective-permute-start | bytes 417800 | tf_op jit(solution)/shard_map/ppermute | solution.py:47
  3.9 0.0 copy-done
  4.0 0.2 %collective-permute-start.1 = (f32[5,8,512]{2,1,0:T(8,128)S(1)}, f32[5,8,512]{2,1,0:T(8,128)S(1)}, u32[]{:S(2)}, u32[]{:S(2)}) collective-permute-start(f32[5,8,512]{2,1,0:T(8,128)S(1)} %get-tuple-element.19), channel_id=1, source_target_pairs={{0,2},{4,6},{8,10},{12,14},{16,18},{20,22},{24,26},{28,30},{2,0},{... | collective-permute-start | bytes 245768 | tf_op jit(solution)/shard_map/ppermute | solution.py:39
  4.1 0.4 %collective-permute-start = (f32[4,8,512]{2,1,0:T(8,128)S(1)}, f32[4,8,512]{2,1,0:T(8,128)S(1)}, u32[]{:S(2)}, u32[]{:S(2)}) collective-permute-start(f32[4,8,512]{2,1,0:T(8,128)S(1)} %get-tuple-element.18), channel_id=1, source_target_pairs={{0,2},{4,6},{8,10},{12,14},{16,18},{20,22},{24,26},{28,30},{2,0},{... | collective-permute-start | bytes 196616 | tf_op jit(solution)/shard_map/ppermute | solution.py:39
  4.5 0.6 %middle.1 = (f32[2,2,7,8,512]{4,3,2,1,0:T(8,128)S(1)}, f32[2,17,8,512]{3,2,1,0:T(8,128)S(1)}, f32[2,8,512]{2,1,0:T(8,128)S(1)}) custom-call(f32[2,8,8,512]{3,2,1,0:T(8,128)S(1)} %copy-done, f32[8,512]{1,0:T(8,128)S(1)} %get-tuple-element.17.codes, f32[2,8]{1,0:T(2,128)S(1)} %get-tuple-element.20.table), custom_call_target="tpu_custom_call" | custom-call | flops 1 | bytes 1 | tf_op jit(solution)/shard_map/middle/pallas_call | solution.py:417
  5.2 0.3 %collective-permute-done.first = f32[4,8,512]{2,1,0:T(8,128)S(1)} collective-permute-done((f32[4,8,512]{2,1,0:T(8,128)S(1)}, f32[4,8,512]{2,1,0:T(8,128)S(1)}, u32[]{:S(2)}, u32[]{:S(2)}) %collective-permute-start) | collective-permute-done | bytes 65568 | tf_op jit(solution)/shard_map/ppermute | solution.py:39
  5.4 0.0 collective-permute-done.1.second
  5.4 0.4 %inner_rows.1.refs_2_ = bf16[2,4,8,512]{3,2,1,0:T(8,128)(2,1)S(1)} custom-call(f32[2,8,8,512]{3,2,1,0:T(8,128)S(1)} %copy-done, f32[4,8,512]{2,1,0:T(8,128)S(1)} %collective-permute-done.first, f32[5,8,512]{2,1,0:T(8,128)S(1)} %collective-permute-done.1.second, f32[2,2,7,8,512]{4,3,2,1,0:T(8,128)S(1)} %get-tuple-element.21.kept, ...), custom_call_target="tpu_custom_call" | custom-call | flops 1 | bytes 1 | tf_op jit(solution)/shard_map/inner_rows/pallas_call | solution.py:435
  5.8 0.0 copy-start.1
  5.8 1.5 %collective-permute-start.4 = (bf16[2,4,8,512]{3,2,1,0:T(8,128)(2,1)S(1)}, bf16[2,4,8,512]{3,2,1,0:T(8,128)(2,1)S(1)}, u32[]{:S(2)}, u32[]{:S(2)}) collective-permute-start(bf16[2,4,8,512]{3,2,1,0:T(8,128)(2,1)S(1)} %inner_rows.1.refs_2_), channel_id=1, source_target_pairs={{0,1},{1,0},{2,3},{3,2},{4,5},{5,4},{6,7},{7,6},{8,9},{9,8},{10,11... | collective-permute-start | bytes 196616 | tf_op jit(solution)/shard_map/ppermute | solution.py:451
  7.4 0.0 collective-permute-done.2.packet
  7.4 0.4 %outer_rows.1.refs_3_ = bf16[2,4,8,512]{3,2,1,0:T(8,128)(2,1)S(1)} custom-call(f32[2,8,8,512]{3,2,1,0:T(8,128)S(1)} %copy-done, f32[17,8,256]{2,1,0:T(8,128)S(1)} %collective-permute-done.2.packet, f32[2,2,7,8,512]{4,3,2,1,0:T(8,128)S(1)} %get-tuple-element.21.kept, f32[2,17,8,512]{3,2,1,0:T(8,128)S(1)} %get-tuple-element.22.coef, ...), custom_call_target="tpu_custom_call" | custom-call | flops 1 | bytes 1 | tf_op jit(solution)/shard_map/outer_rows/pallas_call | solution.py:435
  7.8 0.0 copy-start.2
  7.8 1.7 %collective-permute-start.3 = (bf16[2,4,8,512]{3,2,1,0:T(8,128)(2,1)S(1)}, bf16[2,4,8,512]{3,2,1,0:T(8,128)(2,1)S(1)}, u32[]{:S(2)}, u32[]{:S(2)}) collective-permute-start(bf16[2,4,8,512]{3,2,1,0:T(8,128)(2,1)S(1)} %outer_rows.1.refs_3_), channel_id=1, source_target_pairs={{0,1},{1,0},{2,3},{3,2},{4,5},{5,4},{6,7},{7,6},{8,9},{9,8},{10,11... | collective-permute-start | bytes 196616 | tf_op jit(solution)/shard_map/ppermute | solution.py:451
  9.5 0.0 copy-done.1
  9.5 0.0 copy-done.2
  9.5 0.9 %own_products.1 = (f32[4,4,8,512]{3,2,1,0:T(8,128)S(1)}, f32[4,4,8,512]{3,2,1,0:T(8,128)S(1)}, bf16[2,4,4,8,512]{4,3,2,1,0:T(8,128)(2,1)S(1)}, bf16[2,4,4,8,512]{4,3,2,1,0:T(8,128)(2,1)S(1)}) custom-call(bf16[4,4,8,8,512]{4,3,2,1,0:T(8,128)(2,1)S(1)} %bitcast.2, s32[4]{0:T(128)S(1)} %copy-done.2, bf16[2,4,8,512]{3,2,1,0:T(8,128)(2,1)S(1)} %inner_rows.1.refs_2_, ...), custom_call_target="tpu_custom_call" | custom-call | flops 4000000 | bytes 2000000 | tf_op jit(solution)/shard_map/own_products/pallas_call | solution.py:462
  10.4 0.0 collective-permute-done.4.refs_2_
  10.4 0.8 %near_products.1.refs_3_ = f32[4,8,8,512]{3,2,1,0:T(8,128)} custom-call(f32[4,4,8,512]{3,2,1,0:T(8,128)S(1)} %get-tuple-element.27.refs_0_, bf16[2,4,4,8,512]{4,3,2,1,0:T(8,128)(2,1)S(1)} %get-tuple-element.28.refs_1_, bf16[2,4,8,512]{3,2,1,0:T(8,128)(2,1)S(1)} %collective-permute-done.4.refs_2_), custom_call_target="tpu_custom_call" | custom-call | flops 1000000 | bytes 1000000 | tf_op jit(solution)/shard_map/near_products/pallas_call | solution.py:474
  11.2 0.9 %collective-permute-done.3.refs_2_ = bf16[2,4,8,512]{3,2,1,0:T(8,128)(2,1)S(1)} collective-permute-done((bf16[2,4,8,512]{3,2,1,0:T(8,128)(2,1)S(1)}, bf16[2,4,8,512]{3,2,1,0:T(8,128)(2,1)S(1)}, u32[]{:S(2)}, u32[]{:S(2)}) %collective-permute-start.3) | collective-permute-done | bytes 65568 | tf_op jit(solution)/shard_map/ppermute | solution.py:451
  12.1 0.8 %far_products.1 = f32[4,8,8,512]{3,2,1,0:T(8,128)} custom-call(f32[4,4,8,512]{3,2,1,0:T(8,128)S(1)} %get-tuple-element.25.refs_0_, bf16[2,4,4,8,512]{4,3,2,1,0:T(8,128)(2,1)S(1)} %get-tuple-element.26.refs_1_, bf16[2,4,8,512]{3,2,1,0:T(8,128)(2,1)S(1)} %collective-permute-done.3.refs_2_, ...), custom_call_target="tpu_custom_call", output_to_operand_aliasing={{}: (3, {})} | custom-call | flops 1000000 | bytes 1000000 | tf_op jit(solution)/shard_map/far_products/pallas_call | solution.py:484
  (1 shorter events, 0.0 us)
Async XLA Ops:
  0.0 3.9 %copy-start = (f32[2,8,8,512]{3,2,1,0:T(8,128)S(1)}, f32[2,8,8,512]{3,2,1,0:T(8,128)}, u32[]{:S(2)}) copy-start(f32[2,8,8,512]{3,2,1,0:T(8,128)} %controls.9) | copy-start | bytes 786436
  0.9 6.5 %collective-permute-start.2 = (f32[17,8,256]{2,1,0:T(8,128)S(1)}, f32[17,8,256]{2,1,0:T(8,128)S(1)}, u32[]{:S(2)}, u32[]{:S(2)}) collective-permute-start(f32[17,8,256]{2,1,0:T(8,128)S(1)} %get-tuple-element.24), channel_id=1, source_target_pairs={{2,4},{3,5},{6,8},{7,9},{10,12},{11,13},{14,16},{15,17},{18,20},{1... | collective-permute-start | bytes 417800 | tf_op jit(solution)/shard_map/ppermute | solution.py:47
  4.0 1.5 %collective-permute-start.1 = (f32[5,8,512]{2,1,0:T(8,128)S(1)}, f32[5,8,512]{2,1,0:T(8,128)S(1)}, u32[]{:S(2)}, u32[]{:S(2)}) collective-permute-start(f32[5,8,512]{2,1,0:T(8,128)S(1)} %get-tuple-element.19), channel_id=1, source_target_pairs={{0,2},{4,6},{8,10},{12,14},{16,18},{20,22},{24,26},{28,30},{2,0},{... | collective-permute-start | bytes 245768 | tf_op jit(solution)/shard_map/ppermute | solution.py:39
  4.1 1.3 %collective-permute-start = (f32[4,8,512]{2,1,0:T(8,128)S(1)}, f32[4,8,512]{2,1,0:T(8,128)S(1)}, u32[]{:S(2)}, u32[]{:S(2)}) collective-permute-start(f32[4,8,512]{2,1,0:T(8,128)S(1)} %get-tuple-element.18), channel_id=1, source_target_pairs={{0,2},{4,6},{8,10},{12,14},{16,18},{20,22},{24,26},{28,30},{2,0},{... | collective-permute-start | bytes 196616 | tf_op jit(solution)/shard_map/ppermute | solution.py:39
  5.8 3.6 %copy-start.1 = (bf16[1,4,4,8,8,512]{5,4,3,2,1,0:T(8,128)(2,1)S(1)}, bf16[1,4,4,8,8,512]{5,4,3,2,1,0:T(8,128)(2,1)}, u32[]{:S(2)}) copy-start(bf16[1,4,4,8,8,512]{5,4,3,2,1,0:T(8,128)(2,1)} %param.6) | copy-start | bytes 3145732
  5.8 4.5 %collective-permute-start.4 = (bf16[2,4,8,512]{3,2,1,0:T(8,128)(2,1)S(1)}, bf16[2,4,8,512]{3,2,1,0:T(8,128)(2,1)S(1)}, u32[]{:S(2)}, u32[]{:S(2)}) collective-permute-start(bf16[2,4,8,512]{3,2,1,0:T(8,128)(2,1)S(1)} %inner_rows.1.refs_2_), channel_id=1, source_target_pairs={{0,1},{1,0},{2,3},{3,2},{4,5},{5,4},{6,7},{7,6},{8,9},{9,8},{10,11... | collective-permute-start | bytes 196616 | tf_op jit(solution)/shard_map/ppermute | solution.py:451
  7.8 1.7 %copy-start.2 = (s32[4]{0:T(128)S(1)}, s32[4]{0:T(128)}, u32[]{:S(2)}) copy-start(s32[4]{0:T(128)} %refs_1_.1) | copy-start | bytes 52
  7.8 4.3 %collective-permute-start.3 = (bf16[2,4,8,512]{3,2,1,0:T(8,128)(2,1)S(1)}, bf16[2,4,8,512]{3,2,1,0:T(8,128)(2,1)S(1)}, u32[]{:S(2)}, u32[]{:S(2)}) collective-permute-start(bf16[2,4,8,512]{3,2,1,0:T(8,128)(2,1)S(1)} %outer_rows.1.refs_3_), channel_id=1, source_target_pairs={{0,1},{1,0},{2,3},{3,2},{4,5},{5,4},{6,7},{7,6},{8,9},{9,8},{10,11... | collective-permute-start | bytes 196616 | tf_op jit(solution)/shard_map/ppermute | solution.py:451

commit v5 on v4

--- a/solution.py
+++ b/solution.py
@@ -1,3 +1,4 @@
+import functools
 import math
 
 import jax
@@ -22,6 +23,13 @@
     return j + odd * (2 * SWEEPS - 1 - 2 * j)
 
 
+OUTER, INNER = 0, 1
+
+
+def row_of(side, odd, k):
+    return own_row(odd, k if side == OUTER else 2 * SWEEPS - 1 - k)
+
+
 def half_row(odd, j):
     return j % SWEEPS + odd * (SWEEPS - 1 - 2 * (j % SWEEPS))
 
@@ -47,47 +55,107 @@
     return lax.ppermute(value, ("tile", "tm"), flat + [(b, a) for a, b in flat])
 
 
-def half_codes(odd, code):
-    half = code.shape[1] // 2
-    left, right = code[:, :half], code[:, half:]
-    top = lax.broadcasted_iota(jnp.int32, left.shape, 0) < SWEEPS
-    even = jnp.where(top, left, pltpu.roll(right, SWEEPS, 0))
-    return jnp.where(odd == 1, jnp.where(top, pltpu.roll(left, SWEEPS, 0), right), even)
-
-
-def pack_kernel(controls, mask, diffusivity, across, codes, table, rows, sems):
+FRACTION = (20, 18, 14, 12)
+
+
+def to_fixed(value, bits):
+    return jnp.round(value * float(2**bits)).astype(jnp.int32) + (8 << bits)
+
+
+def from_fixed(value, bits):
+    return (value - (8 << bits)).astype(jnp.float32) * float(0.5**bits)
+
+
+def word_count(slots):
+    return 2 * slots + (slots + 1) // 2
+
+
+def encode(slots, read, code, packet):
+    words, last = [], []
+    for slot in range(slots):
+        one, two, three, four = (to_fixed(read(slot, k), FRACTION[k]) for k in range(SWEEPS))
+        words += [one | (two << 24), (two >> 8) | (three << 14)]
+        last.append(four)
+    words += [sum(value << (16 * i) for i, value in enumerate(last[at : at + 2])) for at in range(0, slots, 2)]
+    width = packet.shape[2]
+    parts = words[0].shape[1] // width
+    for index, word in enumerate(words):
+        for part in range(parts):
+            packet[index * parts + part] = word[:, part * width : (part + 1) * width]
+    for k in range(SWEEPS):
+        value = code(k)
+        for part in range(parts // 2):
+            low = value[:, part * width : (part + 1) * width]
+            high = value[:, (part + parts // 2) * width : (part + parts // 2 + 1) * width]
+            packet[len(words) * parts, pl.ds(k * (parts // 2) + part, 1), :] = low | (high << 16)
+
+
+def decode(packet, slots, slot, k):
+    count = word_count(slots)
+    parts = (packet.shape[0] - 1) // count
+
+    def word(index):
+        return jnp.concatenate([packet[index * parts + part] for part in range(parts)], axis=1)
+
+    def right(value, bits):
+        return lax.shift_right_logical(value, jnp.int32(bits))
+
+    if k == 0:
+        value = word(2 * slot) & 0xFFFFFF
+    elif k == 1:
+        value = right(word(2 * slot), 24) | ((word(2 * slot + 1) & 0x3FFF) << 8)
+    elif k == 2:
+        value = right(word(2 * slot + 1), 14)
+    else:
+        value = word(2 * slots + slot // 2)
+        value = right(value, 16) if slot % 2 else value & 0xFFFF
+    return from_fixed(value, FRACTION[k])
+
+
+def decode_codes(packet, slots, k):
+    count = word_count(slots)
+    half = (packet.shape[0] - 1) // count // 2
+    words = [packet[packet.shape[0] - 1, pl.ds(k * half + part, 1), :] for part in range(half)]
+    return jnp.concatenate([word & 0xFFFF for word in words] + [word >> 16 for word in words], axis=1)
+
+
+def pack_kernel(controls, mask, diffusivity, packet, codes, table, rows, sems):
     odd = parity()
-    slots, columns = controls.shape[0], controls.shape[3]
-    half, count = columns // 2, slots * SWEEPS
+    slots = controls.shape[0]
     copies = [
-        pltpu.make_async_copy(mask, rows, sems.at[0]),
+        pltpu.make_async_copy(mask, codes, sems.at[0]),
         pltpu.make_async_copy(diffusivity, table, sems.at[1]),
     ]
     for slot in range(slots):
-        for side in range(2):
+        for part in range(2):
+            at = SWEEPS // 2 * part
             copies.append(
                 pltpu.make_async_copy(
-                    controls.at[slot, pl.ds(outer_start(odd), SWEEPS), :, pl.ds(side * half, half)],
-                    across.at[pl.ds(side * count + slot * SWEEPS, SWEEPS)],
+                    controls.at[slot, pl.ds(outer_start(odd) + at, SWEEPS // 2)],
+                    rows.at[slot, pl.ds(at, SWEEPS // 2)],
                     sems.at[len(copies)],
                 )
             )
     for copy in copies[2:] + copies[:2]:
         copy.start()
-    copies[0].wait()
-    code = rows[...].astype(jnp.float32) + 1.0
-    codes[...] = code
-    across[2 * count] = half_codes(odd, code)
-    for copy in copies[1:]:
+    for copy in copies:
         copy.wait()
-
-
-def within_kernel(controls, codes, first, second):
+    encode(
+        slots,
+        lambda slot, k: rows[slot, half_row(odd, k)],
+        lambda k: codes[pl.ds(row_of(OUTER, odd, k), 1), :] + 1,
+        packet,
+    )
+
+
+def within_kernel(controls, codes, packet):
     odd = parity()
-    for slot, piece in enumerate((first, second)):
-        for row in range(SWEEPS):
-            piece[row] = controls[slot, inner_start(odd) + row]
-    second[SWEEPS] = codes[...]
+    encode(
+        controls.shape[0],
+        lambda slot, k: controls[slot, row_of(INNER, odd, k)],
+        lambda k: codes[pl.ds(row_of(INNER, odd, k), 1), :] + 1,
+        packet,
+    )
 
 
 def by_level(table, kind, shape):
@@ -99,7 +167,7 @@
 
 
 def kappa_of(code, sea, land):
-    return jnp.where(jnp.broadcast_to(code, sea.shape) == 2.0, land, sea)
+    return jnp.where(jnp.broadcast_to(code, sea.shape) == 2, land, sea)
 
 
 def along_row(kappa):
@@ -119,11 +187,6 @@
 
 FACE, EAST, WEST, CENTRE, KAPPA, COEFS = 0, 4, 8, 12, 16, 17
 PART, VALUE, KEPT = 0, SWEEPS, 2 * SWEEPS - 1
-OUTER, INNER = 0, 1
-
-
-def row_of(side, odd, k):
-    return own_row(odd, k if side == OUTER else 2 * SWEEPS - 1 - k)
 
 
 def middle_kernel(controls, codes, table, kept, coef, halves, face, centre, east, west, field):
@@ -137,7 +200,7 @@
 
     previous = lost = None
     for j in range(total):
-        kappa = kappa_of(codes[pl.ds(own_row(odd, j), 1), :], sea, land)
+        kappa = kappa_of(codes[pl.ds(own_row(odd, j), 1), :] + 1, sea, land)
         e, w, loss = along_row(kappa)
         east[j], west[j] = e, w
         if j:
@@ -250,41 +313,25 @@
                 before[slot], here[slot] = here[slot], after
 
 
-def inner_kernel(controls, first, second, kept, coef, halves, weights, *scratch):
+def side_kernel(side, controls, packet, kept, coef, halves, *refs):
     odd = parity()
-
-    def place(k):
-        return -1 - k + odd * (SWEEPS + 1 + 2 * k)
-
-    def far(slot, k):
-        return (first, second)[slot][place(k)]
-
-    def far_kappa(k):
-        return kappa_of(second[SWEEPS, pl.ds(place(k) + SWEEPS * odd, 1), :], halves[0], halves[1])
-
-    side_rows(INNER, odd, controls, far, far_kappa, None, kept, coef, weights, *scratch)
-
-
-def outer_kernel(controls, packet, kept, coef, halves, weights, *scratch):
-    odd = parity()
-    tile, tiles = lax.axis_index("tile"), lax.axis_size("tile")
-    count = controls.shape[0] * SWEEPS
-    edge = jnp.where(odd == 1, tile == tiles - 1, tile == 0)
-    inside = jnp.where(edge, 0.0, 1.0).astype(jnp.float32)
-
-    def place(k):
-        return SWEEPS + k - odd * (2 * k + SWEEPS + 1)
-
-    def far(slot, k):
-        at = SWEEPS * slot + place(k)
-        return jnp.concatenate([packet[at], packet[count + at]], axis=1)
-
-    def far_kappa(k):
-        left = packet[2 * count, pl.ds(place(k), 1), :]
-        right = packet[2 * count, pl.ds(place(k) + SWEEPS, 1), :]
-        return kappa_of(jnp.concatenate([left, right], axis=1), halves[0], halves[1])
-
-    side_rows(OUTER, odd, controls, far, far_kappa, inside, kept, coef, weights, *scratch)
+    slots = controls.shape[0]
+    inside = None
+    if side == OUTER:
+        tile, tiles = lax.axis_index("tile"), lax.axis_size("tile")
+        edge = jnp.where(odd == 1, tile == tiles - 1, tile == 0)
+        inside = jnp.where(edge, 0.0, 1.0).astype(jnp.float32)
+    side_rows(
+        side,
+        odd,
+        controls,
+        lambda slot, k: decode(packet, slots, slot, -1 - k),
+        lambda k: kappa_of(decode_codes(packet, slots, -1 - k), halves[0], halves[1]),
+        inside,
+        kept,
+        coef,
+        *refs,
+    )
 
 
 def products(pert, weight, total):
@@ -391,28 +438,28 @@
     f32, bf16 = jnp.float32, jnp.bfloat16
     dma = pltpu.SemaphoreType.DMA
 
-    packet = pltpu.VMEM((2 * slots * SWEEPS + 1, levels, columns // 2), f32)
+    packet = pltpu.VMEM((4 * word_count(slots) + 1, levels, columns // 4), jnp.int32)
     mine = near(controls)
     my_across, codes, table = pl.pallas_call(
         pack_kernel,
-        out_shape=(packet, pltpu.VMEM((height, columns), f32), pltpu.VMEM((2, levels), f32)),
+        out_shape=(packet, pltpu.VMEM((height, columns), jnp.int32), pltpu.VMEM((2, levels), f32)),
         in_specs=[ANY, ANY, ANY],
         out_specs=(VMEM, VMEM, VMEM),
-        scratch_shapes=[pltpu.VMEM((height, columns), land_mask.dtype), dma((2 * slots + 2,))],
+        scratch_shapes=[pltpu.VMEM((slots, SWEEPS, *row), f32), dma((2 * slots + 2,))],
         compiler_params=PARAMS,
         name="pack",
     )(far(controls), far(land_mask), far(diffusivity))
     across = swap_across(my_across)
     my_within = pl.pallas_call(
         within_kernel,
-        out_shape=(pltpu.VMEM((SWEEPS, *row), f32), pltpu.VMEM((SWEEPS + 1, *row), f32)),
+        out_shape=packet,
         in_specs=[VMEM, VMEM],
-        out_specs=(VMEM, VMEM),
+        out_specs=VMEM,
         compiler_params=PARAMS,
         cost_estimate=cost(1, 1),
         name="pack_within",
     )(mine, near(codes))
-    within = [swap_within(value) for value in my_within]
+    within = swap_within(my_within)
 
     kept, coef, halves = pl.pallas_call(
         middle_kernel,
@@ -431,20 +478,20 @@
     )(mine, near(codes), near(table))
     shared = (near(kept), near(coef), near(halves))
 
-    def side(kernel, arrived, name):
+    def side(which, arrived, name):
         return pl.pallas_call(
-            kernel,
+            functools.partial(side_kernel, which),
             out_shape=pltpu.VMEM((slots, SWEEPS, *row), bf16),
-            in_specs=[VMEM] * (4 + len(arrived)),
+            in_specs=[VMEM] * 5,
             out_specs=VMEM,
             scratch_shapes=[pltpu.VMEM((SWEEPS + 1, *row), f32)] * 4
             + [pltpu.VMEM((SWEEPS - 1, slots, 2 * SWEEPS, *row), f32)],
             compiler_params=PARAMS,
             cost_estimate=cost(1, 1),
             name=name,
-        )(mine, *map(near, arrived), *shared)
-
-    inner = side(inner_kernel, within, "inner_rows")
+        )(mine, near(arrived), *shared)
+
+    inner = side(INNER, within, "inner_rows")
 
     def shift(value):
         return [
@@ -453,7 +500,7 @@
         ]
 
     inner_arrived = shift(inner)
-    outer = side(outer_kernel, [across], "outer_rows")
+    outer = side(OUTER, across, "outer_rows")
     outer_arrived = shift(outer)
 
     arrivals = count - 1

time: 13.1 us -> 12.5 us (0.954)
  starting transfers between devices: 6.82 us -> 5.78 us
  waiting for transfers between devices: 1.2 us -> 1.41 us
  Pallas kernels: 4.78 us -> 4.93 us
    ppermute x1, waiting for transfers between devices: 0.01 us -> 0.74 us  [swap_across(): return lax.ppermute(value, ('tile', 'tm'), flat + [(b, a) for a, b in flat])]
    ppermute x2, starting transfers between devices: 3.21 us -> 2.67 us  [shift(): lax.ppermute(value, 'tm', [(i, (i + step) % count) for i in range(count)])]
    ppermute x1, starting transfers between devices: 3.03 us -> 2.59 us  [swap_across(): return lax.ppermute(value, ('tile', 'tm'), flat + [(b, a) for a, b in flat])]
    ppermute x2, waiting for transfers between devices: 0.94 us -> 0.67 us  [shift(): lax.ppermute(value, 'tm', [(i, (i + step) % count) for i in range(count)])]
    ppermute x2 -> x1, waiting for transfers between devices: 0.26 us -> 0.01 us  [swap_within(): return lax.ppermute(value, 'tile', pairs + [(b, a) for a, b in pairs])]
    ppermute x2 -> x1, starting transfers between devices: 0.58 us -> 0.52 us  [swap_within(): return lax.ppermute(value, 'tile', pairs + [(b, a) for a, b in pairs])]
  transfers between devices with their start and end apart: 5 -> 4, of which waited for: 2 -> 2; matrix products, arithmetic and copies ran while one was open for 0% -> 0% of each run, Pallas kernels for 24% -> 26%
where the time goes in v5:
time: 12.5 us; the launch traced here: 12.3 us
  starting transfers between devices  5.78 us (46%)
  Pallas kernels  4.93 us (39%)
  waiting for transfers between devices  1.41 us (11%)
    ppermute x2, starting transfers between devices, shift(): lax.ppermute(value, 'tm', [(i, (i + step) % count) for i in range(count)])  2.67 us
    ppermute x1, starting transfers between devices, swap_across(): return lax.ppermute(value, ('tile', 'tm'), flat + [(b, a) for a, b in flat])  2.59 us
    pallas_call x1, Pallas kernels, on_device(): pl.pallas_call(pack_kernel, out_shape=(packet, pltpu.VMEM((height, column...  0.93 us
    pallas_call x1, Pallas kernels, on_device(): pl.pallas_call(lambda *refs: own_kernel(factor, *refs), out_shape=(part,...  0.88 us
    pallas_call x2, Pallas kernels, side(): pl.pallas_call(functools.partial(side_kernel, which), out_shape=pltpu.VME...  0.84 us
    pallas_call x1, Pallas kernels, on_device(): pl.pallas_call(lambda *refs: near_kernel(factor, *refs), out_shape=result...  0.79 us
    pallas_call x1, Pallas kernels, on_device(): pl.pallas_call(lambda *refs: far_kernel(factor, *refs), out_shape=result,...  0.79 us
    ppermute x1, waiting for transfers between devices, swap_across(): return lax.ppermute(value, ('tile', 'tm'), flat + [(b, a) for a, b in flat])  0.74 us
  transfers between devices with their start and end apart: 4, of which 2 were waited for; matrix products, arithmetic and copies ran while one was open for 0% of the time, Pallas kernels for 26%

profile of v5, /device:TPU:0, one launch (start us, length us, event | category | flops | bytes accessed | tf_op | source)
XLA Modules:
  0.0 12.3 jit_solution(17727716771766783496)
XLA Ops:
  0.0 0.0 copy-start
  0.0 0.9 %pack.1 = (s32[21,8,128]{2,1,0:T(8,128)S(1)}, s32[8,512]{1,0:T(8,128)S(1)}, f32[2,8]{1,0:T(2,128)S(1)}) custom-call(f32[2,8,8,512]{3,2,1,0:T(8,128)} %controls.9, s32[8,512]{1,0:T(8,128)} %mask.1, f32[2,8]{1,0:T(2,128)} %diffusivity.1), custom_call_target="tpu_custom_call" | custom-call | tf_op jit(solution)/shard_map/pack/pallas_call | solution.py:443
  0.9 0.1 copy-done
  1.1 0.5 %collective-permute-start = (s32[21,8,128]{2,1,0:T(8,128)S(1)}, s32[21,8,128]{2,1,0:T(8,128)S(1)}, u32[]{:S(2)}, u32[]{:S(2)}) collective-permute-start(s32[21,8,128]{2,1,0:T(8,128)S(1)} %pack_within.1), channel_id=1, source_target_pairs={{0,2},{4,6},{8,10},{12,14},{16,18},{20,22},{24,26},{28,30},{2,0},{... | collective-permute-start | bytes 258056 | tf_op jit(solution)/shard_map/ppermute | solution.py:47
  1.6 2.6 %collective-permute-start.1 = (s32[21,8,128]{2,1,0:T(8,128)S(1)}, s32[21,8,128]{2,1,0:T(8,128)S(1)}, u32[]{:S(2)}, u32[]{:S(2)}) collective-permute-start(s32[21,8,128]{2,1,0:T(8,128)S(1)} %get-tuple-element.20), channel_id=1, source_target_pairs={{2,4},{3,5},{6,8},{7,9},{10,12},{11,13},{14,16},{15,17},{18,20},{1... | collective-permute-start | bytes 258056 | tf_op jit(solution)/shard_map/ppermute | solution.py:55
  4.2 0.7 %middle.1 = (f32[2,2,7,8,512]{4,3,2,1,0:T(8,128)S(1)}, f32[2,17,8,512]{3,2,1,0:T(8,128)S(1)}, f32[2,8,512]{2,1,0:T(8,128)S(1)}) custom-call(f32[2,8,8,512]{3,2,1,0:T(8,128)S(1)} %copy-done, s32[8,512]{1,0:T(8,128)S(1)} %get-tuple-element.15.codes, f32[2,8]{1,0:T(2,128)S(1)} %get-tuple-element.16.table), custom_call_target="tpu_custom_call" | custom-call | flops 1 | bytes 1 | tf_op jit(solution)/shard_map/middle/pallas_call | solution.py:464
  4.9 0.0 collective-permute-done.packet
  4.9 0.4 %inner_rows.1.refs_2_ = bf16[2,4,8,512]{3,2,1,0:T(8,128)(2,1)S(1)} custom-call(f32[2,8,8,512]{3,2,1,0:T(8,128)S(1)} %copy-done, s32[21,8,128]{2,1,0:T(8,128)S(1)} %collective-permute-done.packet, f32[2,2,7,8,512]{4,3,2,1,0:T(8,128)S(1)} %get-tuple-element.17.kept, f32[2,17,8,512]{3,2,1,0:T(8,128)S(1)} %get-tuple-element.18.coef, ...), custom_call_target="tpu_custom_call" | custom-call | flops 1 | bytes 1 | tf_op jit(solution)/shard_map/inner_rows/pallas_call | solution.py:482
  5.3 0.0 copy-start.1
  5.3 0.6 %collective-permute-start.3 = (bf16[2,4,8,512]{3,2,1,0:T(8,128)(2,1)S(1)}, bf16[2,4,8,512]{3,2,1,0:T(8,128)(2,1)S(1)}, u32[]{:S(2)}, u32[]{:S(2)}) collective-permute-start(bf16[2,4,8,512]{3,2,1,0:T(8,128)(2,1)S(1)} %inner_rows.1.refs_2_), channel_id=1, source_target_pairs={{0,1},{1,0},{2,3},{3,2},{4,5},{5,4},{6,7},{7,6},{8,9},{9,8},{10,11... | collective-permute-start | bytes 196616 | tf_op jit(solution)/shard_map/ppermute | solution.py:498
  5.9 0.7 %collective-permute-done.1.packet = s32[21,8,128]{2,1,0:T(8,128)S(1)} collective-permute-done((s32[21,8,128]{2,1,0:T(8,128)S(1)}, s32[21,8,128]{2,1,0:T(8,128)S(1)}, u32[]{:S(2)}, u32[]{:S(2)}) %collective-permute-start.1) | collective-permute-done | bytes 86048 | tf_op jit(solution)/shard_map/ppermute | solution.py:55
  6.7 0.4 %outer_rows.1.refs_3_ = bf16[2,4,8,512]{3,2,1,0:T(8,128)(2,1)S(1)} custom-call(f32[2,8,8,512]{3,2,1,0:T(8,128)S(1)} %copy-done, s32[21,8,128]{2,1,0:T(8,128)S(1)} %collective-permute-done.1.packet, f32[2,2,7,8,512]{4,3,2,1,0:T(8,128)S(1)} %get-tuple-element.17.kept, f32[2,17,8,512]{3,2,1,0:T(8,128)S(1)} %get-tuple-element.18.coef, ...), custom_call_target="tpu_custom_call" | custom-call | flops 1 | bytes 1 | tf_op jit(solution)/shard_map/outer_rows/pallas_call | solution.py:482
  7.1 0.0 copy-start.2
  7.1 2.1 %collective-permute-start.2 = (bf16[2,4,8,512]{3,2,1,0:T(8,128)(2,1)S(1)}, bf16[2,4,8,512]{3,2,1,0:T(8,128)(2,1)S(1)}, u32[]{:S(2)}, u32[]{:S(2)}) collective-permute-start(bf16[2,4,8,512]{3,2,1,0:T(8,128)(2,1)S(1)} %outer_rows.1.refs_3_), channel_id=1, source_target_pairs={{0,1},{1,0},{2,3},{3,2},{4,5},{5,4},{6,7},{7,6},{8,9},{9,8},{10,11... | collective-permute-start | bytes 196616 | tf_op jit(solution)/shard_map/ppermute | solution.py:498
  9.2 0.0 copy-done.1
  9.2 0.0 copy-done.2
  9.2 0.9 %own_products.1 = (f32[4,4,8,512]{3,2,1,0:T(8,128)S(1)}, f32[4,4,8,512]{3,2,1,0:T(8,128)S(1)}, bf16[2,4,4,8,512]{4,3,2,1,0:T(8,128)(2,1)S(1)}, bf16[2,4,4,8,512]{4,3,2,1,0:T(8,128)(2,1)S(1)}) custom-call(bf16[4,4,8,8,512]{4,3,2,1,0:T(8,128)(2,1)S(1)} %bitcast.2, s32[4]{0:T(128)S(1)} %copy-done.2, bf16[2,4,8,512]{3,2,1,0:T(8,128)(2,1)S(1)} %inner_rows.1.refs_2_, ...), custom_call_target="tpu_custom_call" | custom-call | flops 4000000 | bytes 2000000 | tf_op jit(solution)/shard_map/own_products/pallas_call | solution.py:509
  10.1 0.0 collective-permute-done.3.refs_2_
  10.1 0.8 %near_products.1.refs_3_ = f32[4,8,8,512]{3,2,1,0:T(8,128)} custom-call(f32[4,4,8,512]{3,2,1,0:T(8,128)S(1)} %get-tuple-element.23.refs_0_, bf16[2,4,4,8,512]{4,3,2,1,0:T(8,128)(2,1)S(1)} %get-tuple-element.24.refs_1_, bf16[2,4,8,512]{3,2,1,0:T(8,128)(2,1)S(1)} %collective-permute-done.3.refs_2_), custom_call_target="tpu_custom_call" | custom-call | flops 1000000 | bytes 1000000 | tf_op jit(solution)/shard_map/near_products/pallas_call | solution.py:521
  10.9 0.7 %collective-permute-done.2.refs_2_ = bf16[2,4,8,512]{3,2,1,0:T(8,128)(2,1)S(1)} collective-permute-done((bf16[2,4,8,512]{3,2,1,0:T(8,128)(2,1)S(1)}, bf16[2,4,8,512]{3,2,1,0:T(8,128)(2,1)S(1)}, u32[]{:S(2)}, u32[]{:S(2)}) %collective-permute-start.2) | collective-permute-done | bytes 65568 | tf_op jit(solution)/shard_map/ppermute | solution.py:498
  11.5 0.8 %far_products.1 = f32[4,8,8,512]{3,2,1,0:T(8,128)} custom-call(f32[4,4,8,512]{3,2,1,0:T(8,128)S(1)} %get-tuple-element.21.refs_0_, bf16[2,4,4,8,512]{4,3,2,1,0:T(8,128)(2,1)S(1)} %get-tuple-element.22.refs_1_, bf16[2,4,8,512]{3,2,1,0:T(8,128)(2,1)S(1)} %collective-permute-done.2.refs_2_, ...), custom_call_target="tpu_custom_call", output_to_operand_aliasing={{}: (3, {})} | custom-call | flops 1000000 | bytes 1000000 | tf_op jit(solution)/shard_map/far_products/pallas_call | solution.py:531
  (1 shorter events, 0.0 us)
Async XLA Ops:
  0.0 1.0 %copy-start = (f32[2,8,8,512]{3,2,1,0:T(8,128)S(1)}, f32[2,8,8,512]{3,2,1,0:T(8,128)}, u32[]{:S(2)}) copy-start(f32[2,8,8,512]{3,2,1,0:T(8,128)} %controls.9) | copy-start | bytes 786436
  1.1 3.8 %collective-permute-start = (s32[21,8,128]{2,1,0:T(8,128)S(1)}, s32[21,8,128]{2,1,0:T(8,128)S(1)}, u32[]{:S(2)}, u32[]{:S(2)}) collective-permute-start(s32[21,8,128]{2,1,0:T(8,128)S(1)} %pack_within.1), channel_id=1, source_target_pairs={{0,2},{4,6},{8,10},{12,14},{16,18},{20,22},{24,26},{28,30},{2,0},{... | collective-permute-start | bytes 258056 | tf_op jit(solution)/shard_map/ppermute | solution.py:47
  1.6 5.1 %collective-permute-start.1 = (s32[21,8,128]{2,1,0:T(8,128)S(1)}, s32[21,8,128]{2,1,0:T(8,128)S(1)}, u32[]{:S(2)}, u32[]{:S(2)}) collective-permute-start(s32[21,8,128]{2,1,0:T(8,128)S(1)} %get-tuple-element.20), channel_id=1, source_target_pairs={{2,4},{3,5},{6,8},{7,9},{10,12},{11,13},{14,16},{15,17},{18,20},{1... | collective-permute-start | bytes 258056 | tf_op jit(solution)/shard_map/ppermute | solution.py:55
  5.3 3.9 %copy-start.1 = (bf16[1,4,4,8,8,512]{5,4,3,2,1,0:T(8,128)(2,1)S(1)}, bf16[1,4,4,8,8,512]{5,4,3,2,1,0:T(8,128)(2,1)}, u32[]{:S(2)}) copy-start(bf16[1,4,4,8,8,512]{5,4,3,2,1,0:T(8,128)(2,1)} %param.6) | copy-start | bytes 3145732
  5.3 4.7 %collective-permute-start.3 = (bf16[2,4,8,512]{3,2,1,0:T(8,128)(2,1)S(1)}, bf16[2,4,8,512]{3,2,1,0:T(8,128)(2,1)S(1)}, u32[]{:S(2)}, u32[]{:S(2)}) collective-permute-start(bf16[2,4,8,512]{3,2,1,0:T(8,128)(2,1)S(1)} %inner_rows.1.refs_2_), channel_id=1, source_target_pairs={{0,1},{1,0},{2,3},{3,2},{4,5},{5,4},{6,7},{7,6},{8,9},{9,8},{10,11... | collective-permute-start | bytes 196616 | tf_op jit(solution)/shard_map/ppermute | solution.py:498
  7.1 2.1 %copy-start.2 = (s32[4]{0:T(128)S(1)}, s32[4]{0:T(128)}, u32[]{:S(2)}) copy-start(s32[4]{0:T(128)} %refs_1_.1) | copy-start | bytes 52
  7.1 4.5 %collective-permute-start.2 = (bf16[2,4,8,512]{3,2,1,0:T(8,128)(2,1)S(1)}, bf16[2,4,8,512]{3,2,1,0:T(8,128)(2,1)S(1)}, u32[]{:S(2)}, u32[]{:S(2)}) collective-permute-start(bf16[2,4,8,512]{3,2,1,0:T(8,128)(2,1)S(1)} %outer_rows.1.refs_3_), channel_id=1, source_target_pairs={{0,1},{1,0},{2,3},{3,2},{4,5},{5,4},{6,7},{7,6},{8,9},{9,8},{10,11... | collective-permute-start | bytes 196616 | tf_op jit(solution)/shard_map/ppermute | solution.py:498

commit v6 on v5

--- a/solution.py
+++ b/solution.py
@@ -119,43 +119,32 @@
     return jnp.concatenate([word & 0xFFFF for word in words] + [word >> 16 for word in words], axis=1)
 
 
-def pack_kernel(controls, mask, diffusivity, packet, codes, table, rows, sems):
+def pack_kernel(controls, mask, diffusivity, across, within, mine, codes, table, sems):
     odd = parity()
     slots = controls.shape[0]
     copies = [
         pltpu.make_async_copy(mask, codes, sems.at[0]),
         pltpu.make_async_copy(diffusivity, table, sems.at[1]),
     ]
-    for slot in range(slots):
-        for part in range(2):
-            at = SWEEPS // 2 * part
-            copies.append(
-                pltpu.make_async_copy(
-                    controls.at[slot, pl.ds(outer_start(odd) + at, SWEEPS // 2)],
-                    rows.at[slot, pl.ds(at, SWEEPS // 2)],
-                    sems.at[len(copies)],
+    for start in (outer_start(odd), inner_start(odd)):
+        for slot in range(slots):
+            for part in range(2):
+                rows = pl.ds(start + SWEEPS // 2 * part, SWEEPS // 2)
+                copies.append(
+                    pltpu.make_async_copy(controls.at[slot, rows], mine.at[slot, rows], sems.at[len(copies)])
                 )
-            )
-    for copy in copies[2:] + copies[:2]:
+    own, outer, inner = copies[:2], copies[2 : 2 + 2 * slots], copies[2 + 2 * slots :]
+    for copy in outer + own + inner:
         copy.start()
-    for copy in copies:
-        copy.wait()
-    encode(
-        slots,
-        lambda slot, k: rows[slot, half_row(odd, k)],
-        lambda k: codes[pl.ds(row_of(OUTER, odd, k), 1), :] + 1,
-        packet,
-    )
-
-
-def within_kernel(controls, codes, packet):
-    odd = parity()
-    encode(
-        controls.shape[0],
-        lambda slot, k: controls[slot, row_of(INNER, odd, k)],
-        lambda k: codes[pl.ds(row_of(INNER, odd, k), 1), :] + 1,
-        packet,
-    )
+    for side, packet, arriving in ((OUTER, across, outer + own), (INNER, within, inner)):
+        for copy in arriving:
+            copy.wait()
+        encode(
+            slots,
+            lambda slot, k, side=side: mine[slot, row_of(side, odd, k)],
+            lambda k, side=side: codes[pl.ds(row_of(side, odd, k), 1), :] + 1,
+            packet,
+        )
 
 
 def by_level(table, kind, shape):
@@ -439,27 +428,24 @@
     dma = pltpu.SemaphoreType.DMA
 
     packet = pltpu.VMEM((4 * word_count(slots) + 1, levels, columns // 4), jnp.int32)
-    mine = near(controls)
-    my_across, codes, table = pl.pallas_call(
+    my_across, my_within, mine, codes, table = pl.pallas_call(
         pack_kernel,
-        out_shape=(packet, pltpu.VMEM((height, columns), jnp.int32), pltpu.VMEM((2, levels), f32)),
+        out_shape=(
+            packet,
+            packet,
+            pltpu.VMEM(controls.shape, f32),
+            pltpu.VMEM((height, columns), jnp.int32),
+            pltpu.VMEM((2, levels), f32),
+        ),
         in_specs=[ANY, ANY, ANY],
-        out_specs=(VMEM, VMEM, VMEM),
-        scratch_shapes=[pltpu.VMEM((slots, SWEEPS, *row), f32), dma((2 * slots + 2,))],
+        out_specs=(VMEM,) * 5,
+        scratch_shapes=[dma((2 * 2 * slots + 2,))],
         compiler_params=PARAMS,
         name="pack",
     )(far(controls), far(land_mask), far(diffusivity))
     across = swap_across(my_across)
-    my_within = pl.pallas_call(
-        within_kernel,
-        out_shape=packet,
-        in_specs=[VMEM, VMEM],
-        out_specs=VMEM,
-        compiler_params=PARAMS,
-        cost_estimate=cost(1, 1),
-        name="pack_within",
-    )(mine, near(codes))
     within = swap_within(my_within)
+    mine = near(mine)
 
     kept, coef, halves = pl.pallas_call(
         middle_kernel,

time: 12.5 us -> 12.5 us (level)
    pallas_call x2 -> x1, Pallas kernels: 0.96 us -> 1.02 us  [on_device(): pl.pallas_call(pack_kernel, out_shape=(packet, packet, pltpu.VMEM(control...]
where the time goes in v6:
time: 12.5 us; the launch traced here: 12.3 us
  starting transfers between devices  5.78 us (46%)
  Pallas kernels  4.99 us (40%)
  waiting for transfers between devices  1.41 us (11%)
    ppermute x2, starting transfers between devices, shift(): lax.ppermute(value, 'tm', [(i, (i + step) % count) for i in range(count)])  2.67 us
    ppermute x1, starting transfers between devices, swap_across(): return lax.ppermute(value, ('tile', 'tm'), flat + [(b, a) for a, b in flat])  2.59 us
    pallas_call x1, Pallas kernels, on_device(): pl.pallas_call(pack_kernel, out_shape=(packet, packet, pltpu.VMEM(control...  1.02 us
    pallas_call x1, Pallas kernels, on_device(): pl.pallas_call(lambda *refs: own_kernel(factor, *refs), out_shape=(part,...  0.88 us
    pallas_call x2, Pallas kernels, side(): pl.pallas_call(functools.partial(side_kernel, which), out_shape=pltpu.VME...  0.84 us
    pallas_call x1, Pallas kernels, on_device(): pl.pallas_call(lambda *refs: near_kernel(factor, *refs), out_shape=result...  0.79 us
    pallas_call x1, Pallas kernels, on_device(): pl.pallas_call(lambda *refs: far_kernel(factor, *refs), out_shape=result,...  0.79 us
    ppermute x1, waiting for transfers between devices, swap_across(): return lax.ppermute(value, ('tile', 'tm'), flat + [(b, a) for a, b in flat])  0.74 us
  transfers between devices with their start and end apart: 4, of which 2 were waited for; matrix products, arithmetic and copies ran while one was open for 0% of the time, Pallas kernels for 26%

profile of v6, /device:TPU:0, one launch (start us, length us, event | category | flops | bytes accessed | tf_op | source)
XLA Modules:
  0.0 12.3 jit_solution(5722705939279198246)
XLA Ops:
  0.0 1.0 %pack.1 = (s32[21,8,128]{2,1,0:T(8,128)S(1)}, s32[21,8,128]{2,1,0:T(8,128)S(1)}, f32[2,8,8,512]{3,2,1,0:T(8,128)S(1)}, s32[8,512]{1,0:T(8,128)S(1)}, f32[2,8]{1,0:T(2,128)S(1)}) custom-call(f32[2,8,8,512]{3,2,1,0:T(8,128)} %controls.1, s32[8,512]{1,0:T(8,128)} %mask.1, f32[2,8]{1,0:T(2,128)} %diffusivity.1), custom_call_target="tpu_custom_call" | custom-call | tf_op jit(solution)/shard_map/pack/pallas_call | solution.py:431
  1.0 0.5 %collective-permute-start = (s32[21,8,128]{2,1,0:T(8,128)S(1)}, s32[21,8,128]{2,1,0:T(8,128)S(1)}, u32[]{:S(2)}, u32[]{:S(2)}) collective-permute-start(s32[21,8,128]{2,1,0:T(8,128)S(1)} %get-tuple-element.18), channel_id=1, source_target_pairs={{0,2},{4,6},{8,10},{12,14},{16,18},{20,22},{24,26},{28,30},{2,0},{... | collective-permute-start | bytes 258056 | tf_op jit(solution)/shard_map/ppermute | solution.py:47
  1.5 2.6 %collective-permute-start.1 = (s32[21,8,128]{2,1,0:T(8,128)S(1)}, s32[21,8,128]{2,1,0:T(8,128)S(1)}, u32[]{:S(2)}, u32[]{:S(2)}) collective-permute-start(s32[21,8,128]{2,1,0:T(8,128)S(1)} %get-tuple-element.24), channel_id=1, source_target_pairs={{2,4},{3,5},{6,8},{7,9},{10,12},{11,13},{14,16},{15,17},{18,20},{1... | collective-permute-start | bytes 258056 | tf_op jit(solution)/shard_map/ppermute | solution.py:55
  4.1 0.7 %middle.1 = (f32[2,2,7,8,512]{4,3,2,1,0:T(8,128)S(1)}, f32[2,17,8,512]{3,2,1,0:T(8,128)S(1)}, f32[2,8,512]{2,1,0:T(8,128)S(1)}) custom-call(f32[2,8,8,512]{3,2,1,0:T(8,128)S(1)} %get-tuple-element.17.controls, s32[8,512]{1,0:T(8,128)S(1)} %get-tuple-element.19.codes, f32[2,8]{1,0:T(2,128)S(1)} %get-tuple-element.20.table), custom_call_target="tpu_custom_call" | custom-call | flops 1 | bytes 1 | tf_op jit(solution)/shard_map/middle/pallas_call | solution.py:450
  4.8 0.0 collective-permute-done.packet
  4.8 0.4 %inner_rows.1.refs_2_ = bf16[2,4,8,512]{3,2,1,0:T(8,128)(2,1)S(1)} custom-call(f32[2,8,8,512]{3,2,1,0:T(8,128)S(1)} %get-tuple-element.17.controls, s32[21,8,128]{2,1,0:T(8,128)S(1)} %collective-permute-done.packet, f32[2,2,7,8,512]{4,3,2,1,0:T(8,128)S(1)} %get-tuple-element.21.kept, f32[2,17,8,512]{3,2,1,0:T(8,128)S(1)} %get-tuple-element.22.coef, ...), custom_call_target="tpu_custom_call" | custom-call | flops 1 | bytes 1 | tf_op jit(solution)/shard_map/inner_rows/pallas_call | solution.py:468
  5.3 0.0 copy-start
  5.3 0.6 %collective-permute-start.3 = (bf16[2,4,8,512]{3,2,1,0:T(8,128)(2,1)S(1)}, bf16[2,4,8,512]{3,2,1,0:T(8,128)(2,1)S(1)}, u32[]{:S(2)}, u32[]{:S(2)}) collective-permute-start(bf16[2,4,8,512]{3,2,1,0:T(8,128)(2,1)S(1)} %inner_rows.1.refs_2_), channel_id=1, source_target_pairs={{0,1},{1,0},{2,3},{3,2},{4,5},{5,4},{6,7},{7,6},{8,9},{9,8},{10,11... | collective-permute-start | bytes 196616 | tf_op jit(solution)/shard_map/ppermute | solution.py:484
  5.9 0.7 %collective-permute-done.1.packet = s32[21,8,128]{2,1,0:T(8,128)S(1)} collective-permute-done((s32[21,8,128]{2,1,0:T(8,128)S(1)}, s32[21,8,128]{2,1,0:T(8,128)S(1)}, u32[]{:S(2)}, u32[]{:S(2)}) %collective-permute-start.1) | collective-permute-done | bytes 86048 | tf_op jit(solution)/shard_map/ppermute | solution.py:55
  6.6 0.4 %outer_rows.1.refs_3_ = bf16[2,4,8,512]{3,2,1,0:T(8,128)(2,1)S(1)} custom-call(f32[2,8,8,512]{3,2,1,0:T(8,128)S(1)} %get-tuple-element.17.controls, s32[21,8,128]{2,1,0:T(8,128)S(1)} %collective-permute-done.1.packet, f32[2,2,7,8,512]{4,3,2,1,0:T(8,128)S(1)} %get-tuple-element.21.kept, f32[2,17,8,512]{3,2,1,0:T(8,128)S(1)} %get-tuple-element.22.coef, ...), custom_call_target="tpu_custom_call" | custom-call | flops 1 | bytes 1 | tf_op jit(solution)/shard_map/outer_rows/pallas_call | solution.py:468
  7.0 0.0 copy-start.1
  7.0 2.1 %collective-permute-start.2 = (bf16[2,4,8,512]{3,2,1,0:T(8,128)(2,1)S(1)}, bf16[2,4,8,512]{3,2,1,0:T(8,128)(2,1)S(1)}, u32[]{:S(2)}, u32[]{:S(2)}) collective-permute-start(bf16[2,4,8,512]{3,2,1,0:T(8,128)(2,1)S(1)} %outer_rows.1.refs_3_), channel_id=1, source_target_pairs={{0,1},{1,0},{2,3},{3,2},{4,5},{5,4},{6,7},{7,6},{8,9},{9,8},{10,11... | collective-permute-start | bytes 196616 | tf_op jit(solution)/shard_map/ppermute | solution.py:484
  9.1 0.0 copy-done
  9.1 0.0 copy-done.1
  9.1 0.9 %own_products.1 = (f32[4,4,8,512]{3,2,1,0:T(8,128)S(1)}, f32[4,4,8,512]{3,2,1,0:T(8,128)S(1)}, bf16[2,4,4,8,512]{4,3,2,1,0:T(8,128)(2,1)S(1)}, bf16[2,4,4,8,512]{4,3,2,1,0:T(8,128)(2,1)S(1)}) custom-call(bf16[4,4,8,8,512]{4,3,2,1,0:T(8,128)(2,1)S(1)} %bitcast.2, s32[4]{0:T(128)S(1)} %copy-done.1, bf16[2,4,8,512]{3,2,1,0:T(8,128)(2,1)S(1)} %inner_rows.1.refs_2_, ...), custom_call_target="tpu_custom_call" | custom-call | flops 4000000 | bytes 2000000 | tf_op jit(solution)/shard_map/own_products/pallas_call | solution.py:495
  10.0 0.0 collective-permute-done.3.refs_2_
  10.0 0.8 %near_products.1.refs_3_ = f32[4,8,8,512]{3,2,1,0:T(8,128)} custom-call(f32[4,4,8,512]{3,2,1,0:T(8,128)S(1)} %get-tuple-element.27.refs_0_, bf16[2,4,4,8,512]{4,3,2,1,0:T(8,128)(2,1)S(1)} %get-tuple-element.28.refs_1_, bf16[2,4,8,512]{3,2,1,0:T(8,128)(2,1)S(1)} %collective-permute-done.3.refs_2_), custom_call_target="tpu_custom_call" | custom-call | flops 1000000 | bytes 1000000 | tf_op jit(solution)/shard_map/near_products/pallas_call | solution.py:507
  10.8 0.7 %collective-permute-done.2.refs_2_ = bf16[2,4,8,512]{3,2,1,0:T(8,128)(2,1)S(1)} collective-permute-done((bf16[2,4,8,512]{3,2,1,0:T(8,128)(2,1)S(1)}, bf16[2,4,8,512]{3,2,1,0:T(8,128)(2,1)S(1)}, u32[]{:S(2)}, u32[]{:S(2)}) %collective-permute-start.2) | collective-permute-done | bytes 65568 | tf_op jit(solution)/shard_map/ppermute | solution.py:484
  11.5 0.8 %far_products.1 = f32[4,8,8,512]{3,2,1,0:T(8,128)} custom-call(f32[4,4,8,512]{3,2,1,0:T(8,128)S(1)} %get-tuple-element.25.refs_0_, bf16[2,4,4,8,512]{4,3,2,1,0:T(8,128)(2,1)S(1)} %get-tuple-element.26.refs_1_, bf16[2,4,8,512]{3,2,1,0:T(8,128)(2,1)S(1)} %collective-permute-done.2.refs_2_, ...), custom_call_target="tpu_custom_call", output_to_operand_aliasing={{}: (3, {})} | custom-call | flops 1000000 | bytes 1000000 | tf_op jit(solution)/shard_map/far_products/pallas_call | solution.py:517
Async XLA Ops:
  1.0 3.8 %collective-permute-start = (s32[21,8,128]{2,1,0:T(8,128)S(1)}, s32[21,8,128]{2,1,0:T(8,128)S(1)}, u32[]{:S(2)}, u32[]{:S(2)}) collective-permute-start(s32[21,8,128]{2,1,0:T(8,128)S(1)} %get-tuple-element.18), channel_id=1, source_target_pairs={{0,2},{4,6},{8,10},{12,14},{16,18},{20,22},{24,26},{28,30},{2,0},{... | collective-permute-start | bytes 258056 | tf_op jit(solution)/shard_map/ppermute | solution.py:47
  1.5 5.1 %collective-permute-start.1 = (s32[21,8,128]{2,1,0:T(8,128)S(1)}, s32[21,8,128]{2,1,0:T(8,128)S(1)}, u32[]{:S(2)}, u32[]{:S(2)}) collective-permute-start(s32[21,8,128]{2,1,0:T(8,128)S(1)} %get-tuple-element.24), channel_id=1, source_target_pairs={{2,4},{3,5},{6,8},{7,9},{10,12},{11,13},{14,16},{15,17},{18,20},{1... | collective-permute-start | bytes 258056 | tf_op jit(solution)/shard_map/ppermute | solution.py:55
  5.3 3.9 %copy-start = (bf16[1,4,4,8,8,512]{5,4,3,2,1,0:T(8,128)(2,1)S(1)}, bf16[1,4,4,8,8,512]{5,4,3,2,1,0:T(8,128)(2,1)}, u32[]{:S(2)}) copy-start(bf16[1,4,4,8,8,512]{5,4,3,2,1,0:T(8,128)(2,1)} %param.6) | copy-start | bytes 3145732
  5.3 4.7 %collective-permute-start.3 = (bf16[2,4,8,512]{3,2,1,0:T(8,128)(2,1)S(1)}, bf16[2,4,8,512]{3,2,1,0:T(8,128)(2,1)S(1)}, u32[]{:S(2)}, u32[]{:S(2)}) collective-permute-start(bf16[2,4,8,512]{3,2,1,0:T(8,128)(2,1)S(1)} %inner_rows.1.refs_2_), channel_id=1, source_target_pairs={{0,1},{1,0},{2,3},{3,2},{4,5},{5,4},{6,7},{7,6},{8,9},{9,8},{10,11... | collective-permute-start | bytes 196616 | tf_op jit(solution)/shard_map/ppermute | solution.py:484
  7.0 2.1 %copy-start.1 = (s32[4]{0:T(128)S(1)}, s32[4]{0:T(128)}, u32[]{:S(2)}) copy-start(s32[4]{0:T(128)} %refs_1_.1) | copy-start | bytes 52
  7.0 4.5 %collective-permute-start.2 = (bf16[2,4,8,512]{3,2,1,0:T(8,128)(2,1)S(1)}, bf16[2,4,8,512]{3,2,1,0:T(8,128)(2,1)S(1)}, u32[]{:S(2)}, u32[]{:S(2)}) collective-permute-start(bf16[2,4,8,512]{3,2,1,0:T(8,128)(2,1)S(1)} %outer_rows.1.refs_3_), channel_id=1, source_target_pairs={{0,1},{1,0},{2,3},{3,2},{4,5},{5,4},{6,7},{7,6},{8,9},{9,8},{10,11... | collective-permute-start | bytes 196616 | tf_op jit(solution)/shard_map/ppermute | solution.py:484

commit v7 on v6

--- a/solution.py
+++ b/solution.py
@@ -55,7 +55,7 @@
     return lax.ppermute(value, ("tile", "tm"), flat + [(b, a) for a, b in flat])
 
 
-FRACTION = (20, 18, 14, 12)
+FRACTION = (16, 16, 12, 12)
 
 
 def to_fixed(value, bits):
@@ -66,56 +66,68 @@
     return (value - (8 << bits)).astype(jnp.float32) * float(0.5**bits)
 
 
-def word_count(slots):
-    return 2 * slots + (slots + 1) // 2
+QUARTERS = 4
+PAIR_UNITS = 2 * QUARTERS + QUARTERS // 2
+
+
+def unit_count(slots):
+    return QUARTERS * slots + PAIR_UNITS * ((slots + 1) // 2) + 1
 
 
 def encode(slots, read, code, packet):
-    words, last = [], []
+    width = packet.shape[2]
+
+    def quarters(value):
+        return [value[:, part * width : (part + 1) * width] for part in range(QUARTERS)]
+
+    def halves_together(value):
+        parts = quarters(value)
+        return [low | (high << 16) for low, high in zip(parts[: QUARTERS // 2], parts[QUARTERS // 2 :])]
+
+    units, pairs = [], []
     for slot in range(slots):
         one, two, three, four = (to_fixed(read(slot, k), FRACTION[k]) for k in range(SWEEPS))
-        words += [one | (two << 24), (two >> 8) | (three << 14)]
-        last.append(four)
-    words += [sum(value << (16 * i) for i, value in enumerate(last[at : at + 2])) for at in range(0, slots, 2)]
-    width = packet.shape[2]
-    parts = words[0].shape[1] // width
-    for index, word in enumerate(words):
-        for part in range(parts):
-            packet[index * parts + part] = word[:, part * width : (part + 1) * width]
+        units += quarters(one | (two << 20))
+        rest = two >> 12
+        if slot % 2:
+            before = pairs.pop()
+            pairs.append((before[0] | (three << 16), before[1] | (four << 16), before[2] | (rest << 8)))
+        else:
+            pairs.append((three, four, rest))
+    for three, four, rest in pairs:
+        units += quarters(three) + quarters(four) + halves_together(rest)
+    for index, unit in enumerate(units):
+        packet[index] = unit
     for k in range(SWEEPS):
-        value = code(k)
-        for part in range(parts // 2):
-            low = value[:, part * width : (part + 1) * width]
-            high = value[:, (part + parts // 2) * width : (part + parts // 2 + 1) * width]
-            packet[len(words) * parts, pl.ds(k * (parts // 2) + part, 1), :] = low | (high << 16)
+        for part, unit in enumerate(halves_together(code(k))):
+            packet[len(units), pl.ds(k * (QUARTERS // 2) + part, 1), :] = unit
 
 
 def decode(packet, slots, slot, k):
-    count = word_count(slots)
-    parts = (packet.shape[0] - 1) // count
-
-    def word(index):
-        return jnp.concatenate([packet[index * parts + part] for part in range(parts)], axis=1)
+    base = QUARTERS * slots + PAIR_UNITS * (slot // 2)
+
+    def words(start, count=QUARTERS):
+        return jnp.concatenate([packet[start + part] for part in range(count)], axis=1)
 
     def right(value, bits):
         return lax.shift_right_logical(value, jnp.int32(bits))
 
     if k == 0:
-        value = word(2 * slot) & 0xFFFFFF
+        value = words(QUARTERS * slot) & 0xFFFFF
     elif k == 1:
-        value = right(word(2 * slot), 24) | ((word(2 * slot + 1) & 0x3FFF) << 8)
-    elif k == 2:
-        value = right(word(2 * slot + 1), 14)
+        folded = words(base + 2 * QUARTERS, QUARTERS // 2)
+        rest = jnp.concatenate([folded, right(folded, 16)], axis=1)
+        rest = right(rest, 8) & 0xFF if slot % 2 else rest & 0xFF
+        value = right(words(QUARTERS * slot), 20) | (rest << 12)
     else:
-        value = word(2 * slots + slot // 2)
+        value = words(base + QUARTERS * (k - 2))
         value = right(value, 16) if slot % 2 else value & 0xFFFF
     return from_fixed(value, FRACTION[k])
 
 
 def decode_codes(packet, slots, k):
-    count = word_count(slots)
-    half = (packet.shape[0] - 1) // count // 2
-    words = [packet[packet.shape[0] - 1, pl.ds(k * half + part, 1), :] for part in range(half)]
+    half = QUARTERS // 2
+    words = [packet[unit_count(slots) - 1, pl.ds(k * half + part, 1), :] for part in range(half)]
     return jnp.concatenate([word & 0xFFFF for word in words] + [word >> 16 for word in words], axis=1)
 
 
@@ -427,7 +439,7 @@
     f32, bf16 = jnp.float32, jnp.bfloat16
     dma = pltpu.SemaphoreType.DMA
 
-    packet = pltpu.VMEM((4 * word_count(slots) + 1, levels, columns // 4), jnp.int32)
+    packet = pltpu.VMEM((unit_count(slots), levels, columns // QUARTERS), jnp.int32)
     my_across, my_within, mine, codes, table = pl.pallas_call(
         pack_kernel,
         out_shape=(

time: 12.5 us -> 12.4 us (level)
  no operation moved by 1% of the time
where the time goes in v7:
time: 12.4 us; the launch traced here: 12.2 us
  starting transfers between devices  5.77 us (47%)
  Pallas kernels  4.98 us (40%)
  waiting for transfers between devices  1.34 us (11%)
    ppermute x2, starting transfers between devices, shift(): lax.ppermute(value, 'tm', [(i, (i + step) % count) for i in range(count)])  2.66 us
    ppermute x1, starting transfers between devices, swap_across(): return lax.ppermute(value, ('tile', 'tm'), flat + [(b, a) for a, b in flat])  2.59 us
    pallas_call x1, Pallas kernels, on_device(): pl.pallas_call(pack_kernel, out_shape=(packet, packet, pltpu.VMEM(control...  1.02 us
    pallas_call x1, Pallas kernels, on_device(): pl.pallas_call(lambda *refs: own_kernel(factor, *refs), out_shape=(part,...  0.87 us
    pallas_call x2, Pallas kernels, side(): pl.pallas_call(functools.partial(side_kernel, which), out_shape=pltpu.VME...  0.84 us
    pallas_call x1, Pallas kernels, on_device(): pl.pallas_call(lambda *refs: near_kernel(factor, *refs), out_shape=result...  0.79 us
    pallas_call x1, Pallas kernels, on_device(): pl.pallas_call(lambda *refs: far_kernel(factor, *refs), out_shape=result,...  0.79 us
    ppermute x2, waiting for transfers between devices, shift(): lax.ppermute(value, 'tm', [(i, (i + step) % count) for i in range(count)])  0.68 us
  transfers between devices with their start and end apart: 4, of which 2 were waited for; matrix products, arithmetic and copies ran while one was open for 0% of the time, Pallas kernels for 26%

profile of v7, /device:TPU:0, one launch (start us, length us, event | category | flops | bytes accessed | tf_op | source)
XLA Modules:
  0.0 12.2 jit_solution(4067733304884596283)
XLA Ops:
  0.0 1.0 %pack.1 = (s32[19,8,128]{2,1,0:T(8,128)S(1)}, s32[19,8,128]{2,1,0:T(8,128)S(1)}, f32[2,8,8,512]{3,2,1,0:T(8,128)S(1)}, s32[8,512]{1,0:T(8,128)S(1)}, f32[2,8]{1,0:T(2,128)S(1)}) custom-call(f32[2,8,8,512]{3,2,1,0:T(8,128)} %controls.1, s32[8,512]{1,0:T(8,128)} %mask.1, f32[2,8]{1,0:T(2,128)} %diffusivity.1), custom_call_target="tpu_custom_call" | custom-call | tf_op jit(solution)/shard_map/pack/pallas_call | solution.py:443
  1.0 0.5 %collective-permute-start = (s32[19,8,128]{2,1,0:T(8,128)S(1)}, s32[19,8,128]{2,1,0:T(8,128)S(1)}, u32[]{:S(2)}, u32[]{:S(2)}) collective-permute-start(s32[19,8,128]{2,1,0:T(8,128)S(1)} %get-tuple-element.18), channel_id=1, source_target_pairs={{0,2},{4,6},{8,10},{12,14},{16,18},{20,22},{24,26},{28,30},{2,0},{... | collective-permute-start | bytes 233480 | tf_op jit(solution)/shard_map/ppermute | solution.py:47
  1.5 2.6 %collective-permute-start.1 = (s32[19,8,128]{2,1,0:T(8,128)S(1)}, s32[19,8,128]{2,1,0:T(8,128)S(1)}, u32[]{:S(2)}, u32[]{:S(2)}) collective-permute-start(s32[19,8,128]{2,1,0:T(8,128)S(1)} %get-tuple-element.24), channel_id=1, source_target_pairs={{2,4},{3,5},{6,8},{7,9},{10,12},{11,13},{14,16},{15,17},{18,20},{1... | collective-permute-start | bytes 233480 | tf_op jit(solution)/shard_map/ppermute | solution.py:55
  4.1 0.7 %middle.1 = (f32[2,2,7,8,512]{4,3,2,1,0:T(8,128)S(1)}, f32[2,17,8,512]{3,2,1,0:T(8,128)S(1)}, f32[2,8,512]{2,1,0:T(8,128)S(1)}) custom-call(f32[2,8,8,512]{3,2,1,0:T(8,128)S(1)} %get-tuple-element.17.controls, s32[8,512]{1,0:T(8,128)S(1)} %get-tuple-element.19.codes, f32[2,8]{1,0:T(2,128)S(1)} %get-tuple-element.20.table), custom_call_target="tpu_custom_call" | custom-call | flops 1 | bytes 1 | tf_op jit(solution)/shard_map/middle/pallas_call | solution.py:462
  4.8 0.0 collective-permute-done.packet
  4.8 0.4 %inner_rows.1.refs_2_ = bf16[2,4,8,512]{3,2,1,0:T(8,128)(2,1)S(1)} custom-call(f32[2,8,8,512]{3,2,1,0:T(8,128)S(1)} %get-tuple-element.17.controls, s32[19,8,128]{2,1,0:T(8,128)S(1)} %collective-permute-done.packet, f32[2,2,7,8,512]{4,3,2,1,0:T(8,128)S(1)} %get-tuple-element.21.kept, f32[2,17,8,512]{3,2,1,0:T(8,128)S(1)} %get-tuple-element.22.coef, ...), custom_call_target="tpu_custom_call" | custom-call | flops 1 | bytes 1 | tf_op jit(solution)/shard_map/inner_rows/pallas_call | solution.py:480
  5.3 0.0 copy-start
  5.3 0.6 %collective-permute-start.3 = (bf16[2,4,8,512]{3,2,1,0:T(8,128)(2,1)S(1)}, bf16[2,4,8,512]{3,2,1,0:T(8,128)(2,1)S(1)}, u32[]{:S(2)}, u32[]{:S(2)}) collective-permute-start(bf16[2,4,8,512]{3,2,1,0:T(8,128)(2,1)S(1)} %inner_rows.1.refs_2_), channel_id=1, source_target_pairs={{0,1},{1,0},{2,3},{3,2},{4,5},{5,4},{6,7},{7,6},{8,9},{9,8},{10,11... | collective-permute-start | bytes 196616 | tf_op jit(solution)/shard_map/ppermute | solution.py:496
  5.8 0.7 %collective-permute-done.1.packet = s32[19,8,128]{2,1,0:T(8,128)S(1)} collective-permute-done((s32[19,8,128]{2,1,0:T(8,128)S(1)}, s32[19,8,128]{2,1,0:T(8,128)S(1)}, u32[]{:S(2)}, u32[]{:S(2)}) %collective-permute-start.1) | collective-permute-done | bytes 77856 | tf_op jit(solution)/shard_map/ppermute | solution.py:55
  6.5 0.4 %outer_rows.1.refs_3_ = bf16[2,4,8,512]{3,2,1,0:T(8,128)(2,1)S(1)} custom-call(f32[2,8,8,512]{3,2,1,0:T(8,128)S(1)} %get-tuple-element.17.controls, s32[19,8,128]{2,1,0:T(8,128)S(1)} %collective-permute-done.1.packet, f32[2,2,7,8,512]{4,3,2,1,0:T(8,128)S(1)} %get-tuple-element.21.kept, f32[2,17,8,512]{3,2,1,0:T(8,128)S(1)} %get-tuple-element.22.coef, ...), custom_call_target="tpu_custom_call" | custom-call | flops 1 | bytes 1 | tf_op jit(solution)/shard_map/outer_rows/pallas_call | solution.py:480
  6.9 0.0 copy-start.1
  6.9 2.1 %collective-permute-start.2 = (bf16[2,4,8,512]{3,2,1,0:T(8,128)(2,1)S(1)}, bf16[2,4,8,512]{3,2,1,0:T(8,128)(2,1)S(1)}, u32[]{:S(2)}, u32[]{:S(2)}) collective-permute-start(bf16[2,4,8,512]{3,2,1,0:T(8,128)(2,1)S(1)} %outer_rows.1.refs_3_), channel_id=1, source_target_pairs={{0,1},{1,0},{2,3},{3,2},{4,5},{5,4},{6,7},{7,6},{8,9},{9,8},{10,11... | collective-permute-start | bytes 196616 | tf_op jit(solution)/shard_map/ppermute | solution.py:496
  9.0 0.0 copy-done
  9.0 0.0 copy-done.1
  9.0 0.9 %own_products.1 = (f32[4,4,8,512]{3,2,1,0:T(8,128)S(1)}, f32[4,4,8,512]{3,2,1,0:T(8,128)S(1)}, bf16[2,4,4,8,512]{4,3,2,1,0:T(8,128)(2,1)S(1)}, bf16[2,4,4,8,512]{4,3,2,1,0:T(8,128)(2,1)S(1)}) custom-call(bf16[4,4,8,8,512]{4,3,2,1,0:T(8,128)(2,1)S(1)} %bitcast.2, s32[4]{0:T(128)S(1)} %copy-done.1, bf16[2,4,8,512]{3,2,1,0:T(8,128)(2,1)S(1)} %inner_rows.1.refs_2_, ...), custom_call_target="tpu_custom_call" | custom-call | flops 4000000 | bytes 2000000 | tf_op jit(solution)/shard_map/own_products/pallas_call | solution.py:507
  9.9 0.0 collective-permute-done.3.refs_2_
  9.9 0.8 %near_products.1.refs_3_ = f32[4,8,8,512]{3,2,1,0:T(8,128)} custom-call(f32[4,4,8,512]{3,2,1,0:T(8,128)S(1)} %get-tuple-element.27.refs_0_, bf16[2,4,4,8,512]{4,3,2,1,0:T(8,128)(2,1)S(1)} %get-tuple-element.28.refs_1_, bf16[2,4,8,512]{3,2,1,0:T(8,128)(2,1)S(1)} %collective-permute-done.3.refs_2_), custom_call_target="tpu_custom_call" | custom-call | flops 1000000 | bytes 1000000 | tf_op jit(solution)/shard_map/near_products/pallas_call | solution.py:519
  10.7 0.7 %collective-permute-done.2.refs_2_ = bf16[2,4,8,512]{3,2,1,0:T(8,128)(2,1)S(1)} collective-permute-done((bf16[2,4,8,512]{3,2,1,0:T(8,128)(2,1)S(1)}, bf16[2,4,8,512]{3,2,1,0:T(8,128)(2,1)S(1)}, u32[]{:S(2)}, u32[]{:S(2)}) %collective-permute-start.2) | collective-permute-done | bytes 65568 | tf_op jit(solution)/shard_map/ppermute | solution.py:496
  11.4 0.8 %far_products.1 = f32[4,8,8,512]{3,2,1,0:T(8,128)} custom-call(f32[4,4,8,512]{3,2,1,0:T(8,128)S(1)} %get-tuple-element.25.refs_0_, bf16[2,4,4,8,512]{4,3,2,1,0:T(8,128)(2,1)S(1)} %get-tuple-element.26.refs_1_, bf16[2,4,8,512]{3,2,1,0:T(8,128)(2,1)S(1)} %collective-permute-done.2.refs_2_, ...), custom_call_target="tpu_custom_call", output_to_operand_aliasing={{}: (3, {})} | custom-call | flops 1000000 | bytes 1000000 | tf_op jit(solution)/shard_map/far_products/pallas_call | solution.py:529
Async XLA Ops:
  1.0 3.8 %collective-permute-start = (s32[19,8,128]{2,1,0:T(8,128)S(1)}, s32[19,8,128]{2,1,0:T(8,128)S(1)}, u32[]{:S(2)}, u32[]{:S(2)}) collective-permute-start(s32[19,8,128]{2,1,0:T(8,128)S(1)} %get-tuple-element.18), channel_id=1, source_target_pairs={{0,2},{4,6},{8,10},{12,14},{16,18},{20,22},{24,26},{28,30},{2,0},{... | collective-permute-start | bytes 233480 | tf_op jit(solution)/shard_map/ppermute | solution.py:47
  1.5 5.0 %collective-permute-start.1 = (s32[19,8,128]{2,1,0:T(8,128)S(1)}, s32[19,8,128]{2,1,0:T(8,128)S(1)}, u32[]{:S(2)}, u32[]{:S(2)}) collective-permute-start(s32[19,8,128]{2,1,0:T(8,128)S(1)} %get-tuple-element.24), channel_id=1, source_target_pairs={{2,4},{3,5},{6,8},{7,9},{10,12},{11,13},{14,16},{15,17},{18,20},{1... | collective-permute-start | bytes 233480 | tf_op jit(solution)/shard_map/ppermute | solution.py:55
  5.3 3.8 %copy-start = (bf16[1,4,4,8,8,512]{5,4,3,2,1,0:T(8,128)(2,1)S(1)}, bf16[1,4,4,8,8,512]{5,4,3,2,1,0:T(8,128)(2,1)}, u32[]{:S(2)}) copy-start(bf16[1,4,4,8,8,512]{5,4,3,2,1,0:T(8,128)(2,1)} %param.6) | copy-start | bytes 3145732
  5.3 4.6 %collective-permute-start.3 = (bf16[2,4,8,512]{3,2,1,0:T(8,128)(2,1)S(1)}, bf16[2,4,8,512]{3,2,1,0:T(8,128)(2,1)S(1)}, u32[]{:S(2)}, u32[]{:S(2)}) collective-permute-start(bf16[2,4,8,512]{3,2,1,0:T(8,128)(2,1)S(1)} %inner_rows.1.refs_2_), channel_id=1, source_target_pairs={{0,1},{1,0},{2,3},{3,2},{4,5},{5,4},{6,7},{7,6},{8,9},{9,8},{10,11... | collective-permute-start | bytes 196616 | tf_op jit(solution)/shard_map/ppermute | solution.py:496
  6.9 2.1 %copy-start.1 = (s32[4]{0:T(128)S(1)}, s32[4]{0:T(128)}, u32[]{:S(2)}) copy-start(s32[4]{0:T(128)} %refs_1_.1) | copy-start | bytes 52
  6.9 4.5 %collective-permute-start.2 = (bf16[2,4,8,512]{3,2,1,0:T(8,128)(2,1)S(1)}, bf16[2,4,8,512]{3,2,1,0:T(8,128)(2,1)S(1)}, u32[]{:S(2)}, u32[]{:S(2)}) collective-permute-start(bf16[2,4,8,512]{3,2,1,0:T(8,128)(2,1)S(1)} %outer_rows.1.refs_3_), channel_id=1, source_target_pairs={{0,1},{1,0},{2,3},{3,2},{4,5},{5,4},{6,7},{7,6},{8,9},{9,8},{10,11... | collective-permute-start | bytes 196616 | tf_op jit(solution)/shard_map/ppermute | solution.py:496

commit v8 on v7

--- a/solution.py
+++ b/solution.py
@@ -148,23 +148,28 @@
     own, outer, inner = copies[:2], copies[2 : 2 + 2 * slots], copies[2 + 2 * slots :]
     for copy in outer + own + inner:
         copy.start()
-    for side, packet, arriving in ((OUTER, across, outer + own), (INNER, within, inner)):
-        for copy in arriving:
-            copy.wait()
-        encode(
-            slots,
-            lambda slot, k, side=side: mine[slot, row_of(side, odd, k)],
-            lambda k, side=side: codes[pl.ds(row_of(side, odd, k), 1), :] + 1,
-            packet,
-        )
+
+    def read(side, arriving, slot, k):
+        if k == 0:
+            for copy in arriving[2 * slot : 2 * slot + 2]:
+                copy.wait()
+        return mine[slot, row_of(side, odd, k)]
+
+    def code(side, k):
+        if side == OUTER and k == 0:
+            for copy in own:
+                copy.wait()
+        return codes[pl.ds(row_of(side, odd, k), 1), :] + 1
+
+    for side, packet, arriving in ((OUTER, across, outer), (INNER, within, inner)):
+        encode(slots, functools.partial(read, side, arriving), functools.partial(code, side), packet)
 
 
 def by_level(table, kind, shape):
-    level = lax.broadcasted_iota(jnp.int32, shape, 0)
-    value = jnp.broadcast_to(table[kind : kind + 1, 0:1], shape)
-    for index in range(1, shape[0]):
-        value = jnp.where(level == index, table[kind : kind + 1, index : index + 1], value)
-    return value
+    levels = shape[0]
+    square = jnp.broadcast_to(table[kind : kind + 1, :], (levels, levels))
+    diagonal = lax.broadcasted_iota(jnp.int32, square.shape, 0) == lax.broadcasted_iota(jnp.int32, square.shape, 1)
+    return jnp.broadcast_to(jnp.sum(jnp.where(diagonal, square, 0.0), axis=1, keepdims=True), shape)
 
 
 def kappa_of(code, sea, land):
@@ -190,7 +195,7 @@
 PART, VALUE, KEPT = 0, SWEEPS, 2 * SWEEPS - 1
 
 
-def middle_kernel(controls, codes, table, kept, coef, halves, face, centre, east, west, field):
+def middle_kernel(controls, codes, table, kept, coef, halves, shifted, face, centre, east, west, field):
     odd = parity()
     slots, _, levels, columns = controls.shape
     shape = (levels, columns)
@@ -199,10 +204,18 @@
         halves[kind] = 0.5 * by_level(table, kind, shape)
     sea, land = halves[0], halves[1]
 
+    lane = lax.broadcasted_iota(jnp.int32, shape, 1)
+    first_lane, last_lane = lane == 0, lane == columns - 1
+    shifted[0] = pltpu.roll(codes[...], columns - 1, 1)
+    shifted[1] = pltpu.roll(codes[...], 1, 1)
     previous = lost = None
     for j in range(total):
-        kappa = kappa_of(codes[pl.ds(own_row(odd, j), 1), :] + 1, sea, land)
-        e, w, loss = along_row(kappa)
+        place = pl.ds(own_row(odd, j), 1)
+        kappa = kappa_of(codes[place, :] + 1, sea, land)
+        to_east = kappa + jnp.where(last_lane, 0.0, kappa_of(shifted[0, place, :] + 1, sea, land))
+        to_west = kappa + jnp.where(first_lane, 0.0, kappa_of(shifted[1, place, :] + 1, sea, land))
+        loss = to_east + to_west
+        e, w = jnp.where(last_lane, 0.0, to_east), jnp.where(first_lane, 0.0, to_west)
         east[j], west[j] = e, w
         if j:
             face[j] = previous + kappa
@@ -382,28 +395,29 @@
         copy.wait()
 
 
-def add_others(factor, part, others, arrived, row):
-    variables = part.shape[0]
-    total = [part[v, row] for v in range(variables)]
+def add_others(factor, part, others, arrived, row, variables):
+    total = [part[v, row] for v in variables]
     for index, weights in enumerate(arrived):
         slots = weights.shape[0]
         for slot in range(slots):
             weight = weights[slot, row].astype(jnp.float32) * factor
             place = index * slots + slot
-            total = products([others[place, v, row] for v in range(variables)], weight, total)
+            total = products([others[place, v, row] for v in variables], weight, total)
     return total
 
 
 def add_and_write(factor, start, part, others, arrived, out, ready, sems):
-    for row in range(SWEEPS):
-        for v, total in enumerate(add_others(factor, part, others, arrived, row)):
-            ready[v, row] = total
-    writes = [
-        pltpu.make_async_copy(ready.at[v], out.at[v, pl.ds(start, SWEEPS)], sems.at[v])
-        for v in range(part.shape[0])
-    ]
-    for copy in writes:
-        copy.start()
+    count = part.shape[0]
+    half = (count + 1) // 2
+    writes = []
+    for first in range(0, count, half):
+        variables = range(first, min(first + half, count))
+        for row in range(SWEEPS):
+            for v, total in zip(variables, add_others(factor, part, others, arrived, row, variables)):
+                ready[v, row] = total
+        for v in variables:
+            writes.append(pltpu.make_async_copy(ready.at[v], out.at[v, pl.ds(start, SWEEPS)], sems.at[v]))
+            writes[-1].start()
     for copy in writes:
         copy.wait()
 
@@ -468,7 +482,8 @@
         ),
         in_specs=[VMEM] * 3,
         out_specs=(VMEM,) * 3,
-        scratch_shapes=[pltpu.VMEM((height, *row), f32)] * 4
+        scratch_shapes=[pltpu.VMEM((2, height, columns), jnp.int32)]
+        + [pltpu.VMEM((height, *row), f32)] * 4
         + [pltpu.VMEM((SWEEPS - 1, slots, height, *row), f32)],
         compiler_params=PARAMS,
         cost_estimate=cost(1, 1),

time: 12.4 us -> 12.3 us (level)
  Pallas kernels: 4.98 us -> 4.78 us
  starting transfers between devices: 5.77 us -> 5.91 us
    ppermute x2, starting transfers between devices: 2.66 us -> 2.8 us  [shift(): lax.ppermute(value, 'tm', [(i, (i + step) % count) for i in range(count)])]
    pallas_call x1, Pallas kernels: 0.66 us -> 0.53 us  [on_device(): pl.pallas_call(middle_kernel, out_shape=(pltpu.VMEM((2, slots, KEPT, *row...]
  transfers between devices with their start and end apart: 4 -> 4, of which waited for: 2 -> 2; matrix products, arithmetic and copies ran while one was open for 0% -> 0% of each run, Pallas kernels for 26% -> 25%
where the time goes in v8:
time: 12.3 us; the launch traced here: 12.2 us
  starting transfers between devices  5.91 us (48%)
  Pallas kernels  4.78 us (39%)
  waiting for transfers between devices  1.37 us (11%)
    ppermute x2, starting transfers between devices, shift(): lax.ppermute(value, 'tm', [(i, (i + step) % count) for i in range(count)])  2.8 us
    ppermute x1, starting transfers between devices, swap_across(): return lax.ppermute(value, ('tile', 'tm'), flat + [(b, a) for a, b in flat])  2.59 us
    pallas_call x1, Pallas kernels, on_device(): pl.pallas_call(pack_kernel, out_shape=(packet, packet, pltpu.VMEM(control...  1.01 us
    pallas_call x1, Pallas kernels, on_device(): pl.pallas_call(lambda *refs: own_kernel(factor, *refs), out_shape=(part,...  0.87 us
    pallas_call x2, Pallas kernels, side(): pl.pallas_call(functools.partial(side_kernel, which), out_shape=pltpu.VME...  0.84 us
    pallas_call x1, Pallas kernels, on_device(): pl.pallas_call(lambda *refs: near_kernel(factor, *refs), out_shape=result...  0.77 us
    pallas_call x1, Pallas kernels, on_device(): pl.pallas_call(lambda *refs: far_kernel(factor, *refs), out_shape=result,...  0.77 us
    ppermute x2, waiting for transfers between devices, shift(): lax.ppermute(value, 'tm', [(i, (i + step) % count) for i in range(count)])  0.7 us
  transfers between devices with their start and end apart: 4, of which 2 were waited for; matrix products, arithmetic and copies ran while one was open for 0% of the time, Pallas kernels for 25%

profile of v8, /device:TPU:0, one launch (start us, length us, event | category | flops | bytes accessed | tf_op | source)
XLA Modules:
  0.0 12.2 jit_solution(1094194089225281945)
XLA Ops:
  0.0 1.0 %pack.1 = (s32[19,8,128]{2,1,0:T(8,128)S(1)}, s32[19,8,128]{2,1,0:T(8,128)S(1)}, f32[2,8,8,512]{3,2,1,0:T(8,128)S(1)}, s32[8,512]{1,0:T(8,128)S(1)}, f32[2,8]{1,0:T(2,128)S(1)}) custom-call(f32[2,8,8,512]{3,2,1,0:T(8,128)} %controls.1, s32[8,512]{1,0:T(8,128)} %mask.1, f32[2,8]{1,0:T(2,128)} %diffusivity.1), custom_call_target="tpu_custom_call" | custom-call | tf_op jit(solution)/shard_map/pack/pallas_call | solution.py:457
  1.0 0.5 %collective-permute-start = (s32[19,8,128]{2,1,0:T(8,128)S(1)}, s32[19,8,128]{2,1,0:T(8,128)S(1)}, u32[]{:S(2)}, u32[]{:S(2)}) collective-permute-start(s32[19,8,128]{2,1,0:T(8,128)S(1)} %get-tuple-element.18), channel_id=1, source_target_pairs={{0,2},{4,6},{8,10},{12,14},{16,18},{20,22},{24,26},{28,30},{2,0},{... | collective-permute-start | bytes 233480 | tf_op jit(solution)/shard_map/ppermute | solution.py:47
  1.5 2.6 %collective-permute-start.1 = (s32[19,8,128]{2,1,0:T(8,128)S(1)}, s32[19,8,128]{2,1,0:T(8,128)S(1)}, u32[]{:S(2)}, u32[]{:S(2)}) collective-permute-start(s32[19,8,128]{2,1,0:T(8,128)S(1)} %get-tuple-element.24), channel_id=1, source_target_pairs={{2,4},{3,5},{6,8},{7,9},{10,12},{11,13},{14,16},{15,17},{18,20},{1... | collective-permute-start | bytes 233480 | tf_op jit(solution)/shard_map/ppermute | solution.py:55
  4.1 0.5 %middle.1 = (f32[2,2,7,8,512]{4,3,2,1,0:T(8,128)S(1)}, f32[2,17,8,512]{3,2,1,0:T(8,128)S(1)}, f32[2,8,512]{2,1,0:T(8,128)S(1)}) custom-call(f32[2,8,8,512]{3,2,1,0:T(8,128)S(1)} %get-tuple-element.17.controls, s32[8,512]{1,0:T(8,128)S(1)} %get-tuple-element.19.codes, f32[2,8]{1,0:T(2,128)S(1)} %get-tuple-element.20.table), custom_call_target="tpu_custom_call" | custom-call | flops 1 | bytes 1 | tf_op jit(solution)/shard_map/middle/pallas_call | solution.py:476
  4.7 0.0 collective-permute-done.packet
  4.7 0.4 %inner_rows.1.refs_2_ = bf16[2,4,8,512]{3,2,1,0:T(8,128)(2,1)S(1)} custom-call(f32[2,8,8,512]{3,2,1,0:T(8,128)S(1)} %get-tuple-element.17.controls, s32[19,8,128]{2,1,0:T(8,128)S(1)} %collective-permute-done.packet, f32[2,2,7,8,512]{4,3,2,1,0:T(8,128)S(1)} %get-tuple-element.21.kept, f32[2,17,8,512]{3,2,1,0:T(8,128)S(1)} %get-tuple-element.22.coef, ...), custom_call_target="tpu_custom_call" | custom-call | flops 1 | bytes 1 | tf_op jit(solution)/shard_map/inner_rows/pallas_call | solution.py:495
  5.1 0.0 copy-start
  5.1 0.7 %collective-permute-start.3 = (bf16[2,4,8,512]{3,2,1,0:T(8,128)(2,1)S(1)}, bf16[2,4,8,512]{3,2,1,0:T(8,128)(2,1)S(1)}, u32[]{:S(2)}, u32[]{:S(2)}) collective-permute-start(bf16[2,4,8,512]{3,2,1,0:T(8,128)(2,1)S(1)} %inner_rows.1.refs_2_), channel_id=1, source_target_pairs={{0,1},{1,0},{2,3},{3,2},{4,5},{5,4},{6,7},{7,6},{8,9},{9,8},{10,11... | collective-permute-start | bytes 196616 | tf_op jit(solution)/shard_map/ppermute | solution.py:511
  5.8 0.7 %collective-permute-done.1.packet = s32[19,8,128]{2,1,0:T(8,128)S(1)} collective-permute-done((s32[19,8,128]{2,1,0:T(8,128)S(1)}, s32[19,8,128]{2,1,0:T(8,128)S(1)}, u32[]{:S(2)}, u32[]{:S(2)}) %collective-permute-start.1) | collective-permute-done | bytes 77856 | tf_op jit(solution)/shard_map/ppermute | solution.py:55
  6.5 0.4 %outer_rows.1.refs_3_ = bf16[2,4,8,512]{3,2,1,0:T(8,128)(2,1)S(1)} custom-call(f32[2,8,8,512]{3,2,1,0:T(8,128)S(1)} %get-tuple-element.17.controls, s32[19,8,128]{2,1,0:T(8,128)S(1)} %collective-permute-done.1.packet, f32[2,2,7,8,512]{4,3,2,1,0:T(8,128)S(1)} %get-tuple-element.21.kept, f32[2,17,8,512]{3,2,1,0:T(8,128)S(1)} %get-tuple-element.22.coef, ...), custom_call_target="tpu_custom_call" | custom-call | flops 1 | bytes 1 | tf_op jit(solution)/shard_map/outer_rows/pallas_call | solution.py:495
  6.9 0.0 copy-start.1
  6.9 2.1 %collective-permute-start.2 = (bf16[2,4,8,512]{3,2,1,0:T(8,128)(2,1)S(1)}, bf16[2,4,8,512]{3,2,1,0:T(8,128)(2,1)S(1)}, u32[]{:S(2)}, u32[]{:S(2)}) collective-permute-start(bf16[2,4,8,512]{3,2,1,0:T(8,128)(2,1)S(1)} %outer_rows.1.refs_3_), channel_id=1, source_target_pairs={{0,1},{1,0},{2,3},{3,2},{4,5},{5,4},{6,7},{7,6},{8,9},{9,8},{10,11... | collective-permute-start | bytes 196616 | tf_op jit(solution)/shard_map/ppermute | solution.py:511
  9.0 0.0 copy-done
  9.0 0.0 copy-done.1
  9.0 0.9 %own_products.1 = (f32[4,4,8,512]{3,2,1,0:T(8,128)S(1)}, f32[4,4,8,512]{3,2,1,0:T(8,128)S(1)}, bf16[2,4,4,8,512]{4,3,2,1,0:T(8,128)(2,1)S(1)}, bf16[2,4,4,8,512]{4,3,2,1,0:T(8,128)(2,1)S(1)}) custom-call(bf16[4,4,8,8,512]{4,3,2,1,0:T(8,128)(2,1)S(1)} %bitcast.2, s32[4]{0:T(128)S(1)} %copy-done.1, bf16[2,4,8,512]{3,2,1,0:T(8,128)(2,1)S(1)} %inner_rows.1.refs_2_, ...), custom_call_target="tpu_custom_call" | custom-call | flops 4000000 | bytes 2000000 | tf_op jit(solution)/shard_map/own_products/pallas_call | solution.py:522
  9.9 0.0 collective-permute-done.3.refs_2_
  9.9 0.8 %near_products.1.refs_3_ = f32[4,8,8,512]{3,2,1,0:T(8,128)} custom-call(f32[4,4,8,512]{3,2,1,0:T(8,128)S(1)} %get-tuple-element.27.refs_0_, bf16[2,4,4,8,512]{4,3,2,1,0:T(8,128)(2,1)S(1)} %get-tuple-element.28.refs_1_, bf16[2,4,8,512]{3,2,1,0:T(8,128)(2,1)S(1)} %collective-permute-done.3.refs_2_), custom_call_target="tpu_custom_call" | custom-call | flops 1000000 | bytes 1000000 | tf_op jit(solution)/shard_map/near_products/pallas_call | solution.py:534
  10.7 0.7 %collective-permute-done.2.refs_2_ = bf16[2,4,8,512]{3,2,1,0:T(8,128)(2,1)S(1)} collective-permute-done((bf16[2,4,8,512]{3,2,1,0:T(8,128)(2,1)S(1)}, bf16[2,4,8,512]{3,2,1,0:T(8,128)(2,1)S(1)}, u32[]{:S(2)}, u32[]{:S(2)}) %collective-permute-start.2) | collective-permute-done | bytes 65568 | tf_op jit(solution)/shard_map/ppermute | solution.py:511
  11.4 0.8 %far_products.1 = f32[4,8,8,512]{3,2,1,0:T(8,128)} custom-call(f32[4,4,8,512]{3,2,1,0:T(8,128)S(1)} %get-tuple-element.25.refs_0_, bf16[2,4,4,8,512]{4,3,2,1,0:T(8,128)(2,1)S(1)} %get-tuple-element.26.refs_1_, bf16[2,4,8,512]{3,2,1,0:T(8,128)(2,1)S(1)} %collective-permute-done.2.refs_2_, ...), custom_call_target="tpu_custom_call", output_to_operand_aliasing={{}: (3, {})} | custom-call | flops 1000000 | bytes 1000000 | tf_op jit(solution)/shard_map/far_products/pallas_call | solution.py:544
Async XLA Ops:
  1.0 3.6 %collective-permute-start = (s32[19,8,128]{2,1,0:T(8,128)S(1)}, s32[19,8,128]{2,1,0:T(8,128)S(1)}, u32[]{:S(2)}, u32[]{:S(2)}) collective-permute-start(s32[19,8,128]{2,1,0:T(8,128)S(1)} %get-tuple-element.18), channel_id=1, source_target_pairs={{0,2},{4,6},{8,10},{12,14},{16,18},{20,22},{24,26},{28,30},{2,0},{... | collective-permute-start | bytes 233480 | tf_op jit(solution)/shard_map/ppermute | solution.py:47
  1.5 5.0 %collective-permute-start.1 = (s32[19,8,128]{2,1,0:T(8,128)S(1)}, s32[19,8,128]{2,1,0:T(8,128)S(1)}, u32[]{:S(2)}, u32[]{:S(2)}) collective-permute-start(s32[19,8,128]{2,1,0:T(8,128)S(1)} %get-tuple-element.24), channel_id=1, source_target_pairs={{2,4},{3,5},{6,8},{7,9},{10,12},{11,13},{14,16},{15,17},{18,20},{1... | collective-permute-start | bytes 233480 | tf_op jit(solution)/shard_map/ppermute | solution.py:55
  5.1 3.9 %copy-start = (bf16[1,4,4,8,8,512]{5,4,3,2,1,0:T(8,128)(2,1)S(1)}, bf16[1,4,4,8,8,512]{5,4,3,2,1,0:T(8,128)(2,1)}, u32[]{:S(2)}) copy-start(bf16[1,4,4,8,8,512]{5,4,3,2,1,0:T(8,128)(2,1)} %param.6) | copy-start | bytes 3145732
  5.1 4.8 %collective-permute-start.3 = (bf16[2,4,8,512]{3,2,1,0:T(8,128)(2,1)S(1)}, bf16[2,4,8,512]{3,2,1,0:T(8,128)(2,1)S(1)}, u32[]{:S(2)}, u32[]{:S(2)}) collective-permute-start(bf16[2,4,8,512]{3,2,1,0:T(8,128)(2,1)S(1)} %inner_rows.1.refs_2_), channel_id=1, source_target_pairs={{0,1},{1,0},{2,3},{3,2},{4,5},{5,4},{6,7},{7,6},{8,9},{9,8},{10,11... | collective-permute-start | bytes 196616 | tf_op jit(solution)/shard_map/ppermute | solution.py:511
  6.9 2.1 %copy-start.1 = (s32[4]{0:T(128)S(1)}, s32[4]{0:T(128)}, u32[]{:S(2)}) copy-start(s32[4]{0:T(128)} %refs_1_.1) | copy-start | bytes 52
  6.9 4.5 %collective-permute-start.2 = (bf16[2,4,8,512]{3,2,1,0:T(8,128)(2,1)S(1)}, bf16[2,4,8,512]{3,2,1,0:T(8,128)(2,1)S(1)}, u32[]{:S(2)}, u32[]{:S(2)}) collective-permute-start(bf16[2,4,8,512]{3,2,1,0:T(8,128)(2,1)S(1)} %outer_rows.1.refs_3_), channel_id=1, source_target_pairs={{0,1},{1,0},{2,3},{3,2},{4,5},{5,4},{6,7},{7,6},{8,9},{9,8},{10,11... | collective-permute-start | bytes 196616 | tf_op jit(solution)/shard_map/ppermute | solution.py:511

commit v9 on v8

--- a/solution.py
+++ b/solution.py
@@ -267,58 +267,64 @@
                 before[slot], here[slot] = here[slot], after
 
 
-def side_rows(side, odd, controls, far, far_kappa, inside, kept, coef, weights, face, centre, east, west, field):
+def edge_here(odd):
+    tile, tiles = lax.axis_index("tile"), lax.axis_size("tile")
+    return jnp.where(odd == 1, tile == tiles - 1, tile == 0)
+
+
+def side_rows(side, odd, controls, neighbour, kept, coef, weights, face, centre, east, west, field):
     slots = controls.shape[0]
-
-    def masked(value):
-        return value if inside is None else value * inside
-
-    previous = masked(far_kappa(-SWEEPS))
-    lost = None
-    for k in range(1 - SWEEPS, 1):
-        i = k + SWEEPS
-        kappa = masked(far_kappa(k)) if k else coef[side, KAPPA]
-        step = previous + kappa
-        face[i] = step
-        if lost is not None:
-            centre[i - 1] = 1.0 - (lost + step)
-        if k:
-            e, w, loss = along_row(kappa)
-            east[i], west[i] = e, w
-            lost = loss + step
-        else:
-            centre[i] = coef[side, CENTRE] - step
-        previous = kappa
-    first = face[SWEEPS]
-    first_inside = masked(first)
+    if neighbour is None:
+        face[SWEEPS] = coef[side, KAPPA]
+    else:
+        far, far_kappa = neighbour
+        previous = far_kappa(-SWEEPS)
+        lost = None
+        for k in range(1 - SWEEPS, 1):
+            i = k + SWEEPS
+            kappa = far_kappa(k) if k else coef[side, KAPPA]
+            step = previous + kappa
+            face[i] = step
+            if lost is not None:
+                centre[i - 1] = 1.0 - (lost + step)
+            if k:
+                e, w, loss = along_row(kappa)
+                east[i], west[i] = e, w
+                lost = loss + step
+            previous = kappa
+    centre[SWEEPS] = coef[side, CENTRE] - face[SWEEPS]
 
     def value(slot, sweep, k):
         if sweep == 0:
-            return masked(far(slot, k)) if k < 0 else controls[slot, row_of(side, odd, k)]
+            return far(slot, k) if k < 0 else controls[slot, row_of(side, odd, k)]
         if k == sweep:
             return kept[side, slot, VALUE + sweep - 1]
         return field[sweep - 1, slot, k + SWEEPS]
 
     for sweep in range(1, SWEEPS + 1):
-        low = sweep - SWEEPS
-        before = [value(slot, sweep - 1, low - 1) for slot in range(slots)]
+        low = 0 if neighbour is None else sweep - SWEEPS
+        before = [None if neighbour is None else value(slot, sweep - 1, low - 1) for slot in range(slots)]
         here = [value(slot, sweep - 1, low) for slot in range(slots)]
         for k in range(low, sweep):
             i = k + SWEEPS
-            below = face[i] if k < 0 else first if k == 0 else coef[side, FACE + k]
+            below = face[i] if k <= 0 else coef[side, FACE + k]
             if k < sweep - 1:
-                above = face[i + 1] if k < -1 else first_inside if k == -1 else coef[side, FACE + k + 1]
+                above = face[i + 1] if k < 0 else coef[side, FACE + k + 1]
                 c = centre[i] if k <= 0 else coef[side, CENTRE + k]
                 e, w = (east[i], west[i]) if k < 0 else (coef[side, EAST + k], coef[side, WEST + k])
             for slot in range(slots):
                 after = None
                 if k < sweep - 1:
                     after = value(slot, sweep - 1, k + 1)
-                    result = sideways(c, e, w, here[slot]) + above * after + below * before[slot]
-                elif k == 0:
-                    result = kept[side, slot, PART] + below * (before[slot] - here[slot])
+                    result = sideways(c, e, w, here[slot]) + above * after
+                    if before[slot] is not None:
+                        result = result + below * before[slot]
                 else:
-                    result = kept[side, slot, PART + sweep - 1] + below * before[slot]
+                    result = kept[side, slot, PART + sweep - 1]
+                    if before[slot] is not None:
+                        result = result + below * before[slot]
+                    if k == 0:
+                        result = result - below * here[slot]
                 if sweep == SWEEPS:
                     place = half_row(odd, k if side == OUTER else 2 * SWEEPS - 1 - k)
                     weights[slot, place] = result.astype(weights.dtype)
@@ -327,25 +333,30 @@
                 before[slot], here[slot] = here[slot], after
 
 
-def side_kernel(side, controls, packet, kept, coef, halves, *refs):
-    odd = parity()
-    slots = controls.shape[0]
-    inside = None
-    if side == OUTER:
-        tile, tiles = lax.axis_index("tile"), lax.axis_size("tile")
-        edge = jnp.where(odd == 1, tile == tiles - 1, tile == 0)
-        inside = jnp.where(edge, 0.0, 1.0).astype(jnp.float32)
-    side_rows(
-        side,
-        odd,
-        controls,
+def neighbour_of(packet, slots, halves):
+    return (
         lambda slot, k: decode(packet, slots, slot, -1 - k),
         lambda k: kappa_of(decode_codes(packet, slots, -1 - k), halves[0], halves[1]),
-        inside,
-        kept,
-        coef,
-        *refs,
     )
+
+
+def inner_kernel(controls, packet, kept, coef, halves, weights, *scratch):
+    neighbour = neighbour_of(packet, controls.shape[0], halves)
+    side_rows(INNER, parity(), controls, neighbour, kept, coef, weights, *scratch)
+
+
+def outer_kernel(controls, packet, kept, coef, halves, weights, *scratch):
+    odd = parity()
+    edge = edge_here(odd)
+
+    @pl.when(edge)
+    def _():
+        side_rows(OUTER, odd, controls, None, kept, coef, weights, *scratch)
+
+    @pl.when(jnp.logical_not(edge))
+    def _():
+        neighbour = neighbour_of(packet, controls.shape[0], halves)
+        side_rows(OUTER, odd, controls, neighbour, kept, coef, weights, *scratch)
 
 
 def products(pert, weight, total):
@@ -473,6 +484,10 @@
     within = swap_within(my_within)
     mine = near(mine)
 
+    half = pltpu.VMEM((slots, SWEEPS, *row), bf16)
+    middle_scratch = [pltpu.VMEM((2, height, columns), jnp.int32)]
+    middle_scratch += [pltpu.VMEM((height, *row), f32)] * 4
+    middle_scratch += [pltpu.VMEM((SWEEPS - 1, slots, height, *row), f32)]
     kept, coef, halves = pl.pallas_call(
         middle_kernel,
         out_shape=(
@@ -482,29 +497,27 @@
         ),
         in_specs=[VMEM] * 3,
         out_specs=(VMEM,) * 3,
-        scratch_shapes=[pltpu.VMEM((2, height, columns), jnp.int32)]
-        + [pltpu.VMEM((height, *row), f32)] * 4
-        + [pltpu.VMEM((SWEEPS - 1, slots, height, *row), f32)],
+        scratch_shapes=middle_scratch,
         compiler_params=PARAMS,
         cost_estimate=cost(1, 1),
         name="middle",
     )(mine, near(codes), near(table))
     shared = (near(kept), near(coef), near(halves))
 
-    def side(which, arrived, name):
+    def side(kernel, name, *operands):
         return pl.pallas_call(
-            functools.partial(side_kernel, which),
-            out_shape=pltpu.VMEM((slots, SWEEPS, *row), bf16),
-            in_specs=[VMEM] * 5,
+            kernel,
+            out_shape=half,
+            in_specs=[VMEM] * len(operands),
             out_specs=VMEM,
             scratch_shapes=[pltpu.VMEM((SWEEPS + 1, *row), f32)] * 4
             + [pltpu.VMEM((SWEEPS - 1, slots, 2 * SWEEPS, *row), f32)],
             compiler_params=PARAMS,
             cost_estimate=cost(1, 1),
             name=name,
-        )(mine, near(arrived), *shared)
-
-    inner = side(INNER, within, "inner_rows")
+        )(*operands)
+
+    inner = side(inner_kernel, "inner_rows", mine, near(within), *shared)
 
     def shift(value):
         return [
@@ -513,7 +526,7 @@
         ]
 
     inner_arrived = shift(inner)
-    outer = side(OUTER, across, "outer_rows")
+    outer = side(outer_kernel, "outer_rows", mine, near(across), *shared)
     outer_arrived = shift(outer)
 
     arrivals = count - 1

time: 12.3 us -> 12.3 us (level)
  Pallas kernels: 4.78 us -> 4.64 us
  waiting for transfers between devices: 1.37 us -> 1.5 us
    pallas_call x2, Pallas kernels: 0.84 us -> 0.7 us  [side(): pl.pallas_call(kernel, out_shape=half, in_specs=[VMEM] * len(operands), o...]
    ppermute x2, waiting for transfers between devices: 0.7 us -> 0.83 us  [shift(): lax.ppermute(value, 'tm', [(i, (i + step) % count) for i in range(count)])]
  transfers between devices with their start and end apart: 4 -> 4, of which waited for: 2 -> 2; matrix products, arithmetic and copies ran while one was open for 0% -> 0% of each run, Pallas kernels for 25% -> 24%
where the time goes in v9:
time: 12.3 us; the launch traced here: 12.1 us
  starting transfers between devices  5.91 us (48%)
  Pallas kernels  4.64 us (38%)
  waiting for transfers between devices  1.5 us (12%)
    ppermute x2, starting transfers between devices, shift(): lax.ppermute(value, 'tm', [(i, (i + step) % count) for i in range(count)])  2.8 us
    ppermute x1, starting transfers between devices, swap_across(): return lax.ppermute(value, ('tile', 'tm'), flat + [(b, a) for a, b in flat])  2.59 us
    pallas_call x1, Pallas kernels, on_device(): pl.pallas_call(pack_kernel, out_shape=(packet, packet, pltpu.VMEM(control...  1.01 us
    pallas_call x1, Pallas kernels, on_device(): pl.pallas_call(lambda *refs: own_kernel(factor, *refs), out_shape=(part,...  0.87 us
    ppermute x2, waiting for transfers between devices, shift(): lax.ppermute(value, 'tm', [(i, (i + step) % count) for i in range(count)])  0.83 us
    pallas_call x1, Pallas kernels, on_device(): pl.pallas_call(lambda *refs: near_kernel(factor, *refs), out_shape=result...  0.77 us
    pallas_call x1, Pallas kernels, on_device(): pl.pallas_call(lambda *refs: far_kernel(factor, *refs), out_shape=result,...  0.77 us
    pallas_call x2, Pallas kernels, side(): pl.pallas_call(kernel, out_shape=half, in_specs=[VMEM] * len(operands), o...  0.7 us
  transfers between devices with their start and end apart: 4, of which 2 were waited for; matrix products, arithmetic and copies ran while one was open for 0% of the time, Pallas kernels for 24%

profile of v9, /device:TPU:0, one launch (start us, length us, event | category | flops | bytes accessed | tf_op | source)
XLA Modules:
  0.0 12.1 jit_solution(13061820572255032367)
XLA Ops:
  0.0 1.0 %pack.1 = (s32[19,8,128]{2,1,0:T(8,128)S(1)}, s32[19,8,128]{2,1,0:T(8,128)S(1)}, f32[2,8,8,512]{3,2,1,0:T(8,128)S(1)}, s32[8,512]{1,0:T(8,128)S(1)}, f32[2,8]{1,0:T(2,128)S(1)}) custom-call(f32[2,8,8,512]{3,2,1,0:T(8,128)} %controls.1, s32[8,512]{1,0:T(8,128)} %mask.1, f32[2,8]{1,0:T(2,128)} %diffusivity.1), custom_call_target="tpu_custom_call" | custom-call | tf_op jit(solution)/shard_map/pack/pallas_call | solution.py:468
  1.0 0.5 %collective-permute-start = (s32[19,8,128]{2,1,0:T(8,128)S(1)}, s32[19,8,128]{2,1,0:T(8,128)S(1)}, u32[]{:S(2)}, u32[]{:S(2)}) collective-permute-start(s32[19,8,128]{2,1,0:T(8,128)S(1)} %get-tuple-element.18), channel_id=1, source_target_pairs={{0,2},{4,6},{8,10},{12,14},{16,18},{20,22},{24,26},{28,30},{2,0},{... | collective-permute-start | bytes 233480 | tf_op jit(solution)/shard_map/ppermute | solution.py:47
  1.5 2.6 %collective-permute-start.1 = (s32[19,8,128]{2,1,0:T(8,128)S(1)}, s32[19,8,128]{2,1,0:T(8,128)S(1)}, u32[]{:S(2)}, u32[]{:S(2)}) collective-permute-start(s32[19,8,128]{2,1,0:T(8,128)S(1)} %get-tuple-element.24), channel_id=1, source_target_pairs={{2,4},{3,5},{6,8},{7,9},{10,12},{11,13},{14,16},{15,17},{18,20},{1... | collective-permute-start | bytes 233480 | tf_op jit(solution)/shard_map/ppermute | solution.py:55
  4.1 0.5 %middle.1 = (f32[2,2,7,8,512]{4,3,2,1,0:T(8,128)S(1)}, f32[2,17,8,512]{3,2,1,0:T(8,128)S(1)}, f32[2,8,512]{2,1,0:T(8,128)S(1)}) custom-call(f32[2,8,8,512]{3,2,1,0:T(8,128)S(1)} %get-tuple-element.17.controls, s32[8,512]{1,0:T(8,128)S(1)} %get-tuple-element.19.codes, f32[2,8]{1,0:T(2,128)S(1)} %get-tuple-element.20.table), custom_call_target="tpu_custom_call" | custom-call | flops 1 | bytes 1 | tf_op jit(solution)/shard_map/middle/pallas_call | solution.py:491
  4.7 0.0 collective-permute-done.packet
  4.7 0.4 %inner_rows.1.refs_2_ = bf16[2,4,8,512]{3,2,1,0:T(8,128)(2,1)S(1)} custom-call(f32[2,8,8,512]{3,2,1,0:T(8,128)S(1)} %get-tuple-element.17.controls, s32[19,8,128]{2,1,0:T(8,128)S(1)} %collective-permute-done.packet, f32[2,2,7,8,512]{4,3,2,1,0:T(8,128)S(1)} %get-tuple-element.21.kept, f32[2,17,8,512]{3,2,1,0:T(8,128)S(1)} %get-tuple-element.22.coef, ...), custom_call_target="tpu_custom_call" | custom-call | flops 1 | bytes 1 | tf_op jit(solution)/shard_map/inner_rows/pallas_call | solution.py:508
  5.1 0.0 copy-start
  5.1 0.7 %collective-permute-start.3 = (bf16[2,4,8,512]{3,2,1,0:T(8,128)(2,1)S(1)}, bf16[2,4,8,512]{3,2,1,0:T(8,128)(2,1)S(1)}, u32[]{:S(2)}, u32[]{:S(2)}) collective-permute-start(bf16[2,4,8,512]{3,2,1,0:T(8,128)(2,1)S(1)} %inner_rows.1.refs_2_), channel_id=1, source_target_pairs={{0,1},{1,0},{2,3},{3,2},{4,5},{5,4},{6,7},{7,6},{8,9},{9,8},{10,11... | collective-permute-start | bytes 196616 | tf_op jit(solution)/shard_map/ppermute | solution.py:524
  5.8 0.7 %collective-permute-done.1.packet = s32[19,8,128]{2,1,0:T(8,128)S(1)} collective-permute-done((s32[19,8,128]{2,1,0:T(8,128)S(1)}, s32[19,8,128]{2,1,0:T(8,128)S(1)}, u32[]{:S(2)}, u32[]{:S(2)}) %collective-permute-start.1) | collective-permute-done | bytes 77856 | tf_op jit(solution)/shard_map/ppermute | solution.py:55
  6.5 0.3 %outer_rows.1.refs_3_ = bf16[2,4,8,512]{3,2,1,0:T(8,128)(2,1)S(1)} custom-call(f32[2,8,8,512]{3,2,1,0:T(8,128)S(1)} %get-tuple-element.17.controls, s32[19,8,128]{2,1,0:T(8,128)S(1)} %collective-permute-done.1.packet, f32[2,2,7,8,512]{4,3,2,1,0:T(8,128)S(1)} %get-tuple-element.21.kept, f32[2,17,8,512]{3,2,1,0:T(8,128)S(1)} %get-tuple-element.22.coef, ...), custom_call_target="tpu_custom_call" | custom-call | flops 1 | bytes 1 | tf_op jit(solution)/shard_map/outer_rows/pallas_call | solution.py:508
  6.8 0.0 copy-start.1
  6.8 2.1 %collective-permute-start.2 = (bf16[2,4,8,512]{3,2,1,0:T(8,128)(2,1)S(1)}, bf16[2,4,8,512]{3,2,1,0:T(8,128)(2,1)S(1)}, u32[]{:S(2)}, u32[]{:S(2)}) collective-permute-start(bf16[2,4,8,512]{3,2,1,0:T(8,128)(2,1)S(1)} %outer_rows.1.refs_3_), channel_id=1, source_target_pairs={{0,1},{1,0},{2,3},{3,2},{4,5},{5,4},{6,7},{7,6},{8,9},{9,8},{10,11... | collective-permute-start | bytes 196616 | tf_op jit(solution)/shard_map/ppermute | solution.py:524
  8.9 0.0 copy-done
  8.9 0.0 copy-done.1
  8.9 0.9 %own_products.1 = (f32[4,4,8,512]{3,2,1,0:T(8,128)S(1)}, f32[4,4,8,512]{3,2,1,0:T(8,128)S(1)}, bf16[2,4,4,8,512]{4,3,2,1,0:T(8,128)(2,1)S(1)}, bf16[2,4,4,8,512]{4,3,2,1,0:T(8,128)(2,1)S(1)}) custom-call(bf16[4,4,8,8,512]{4,3,2,1,0:T(8,128)(2,1)S(1)} %bitcast.2, s32[4]{0:T(128)S(1)} %copy-done.1, bf16[2,4,8,512]{3,2,1,0:T(8,128)(2,1)S(1)} %inner_rows.1.refs_2_, ...), custom_call_target="tpu_custom_call" | custom-call | flops 4000000 | bytes 2000000 | tf_op jit(solution)/shard_map/own_products/pallas_call | solution.py:535
  9.8 0.0 collective-permute-done.3.refs_2_
  9.8 0.8 %near_products.1.refs_3_ = f32[4,8,8,512]{3,2,1,0:T(8,128)} custom-call(f32[4,4,8,512]{3,2,1,0:T(8,128)S(1)} %get-tuple-element.27.refs_0_, bf16[2,4,4,8,512]{4,3,2,1,0:T(8,128)(2,1)S(1)} %get-tuple-element.28.refs_1_, bf16[2,4,8,512]{3,2,1,0:T(8,128)(2,1)S(1)} %collective-permute-done.3.refs_2_), custom_call_target="tpu_custom_call" | custom-call | flops 1000000 | bytes 1000000 | tf_op jit(solution)/shard_map/near_products/pallas_call | solution.py:547
  10.5 0.8 %collective-permute-done.2.refs_2_ = bf16[2,4,8,512]{3,2,1,0:T(8,128)(2,1)S(1)} collective-permute-done((bf16[2,4,8,512]{3,2,1,0:T(8,128)(2,1)S(1)}, bf16[2,4,8,512]{3,2,1,0:T(8,128)(2,1)S(1)}, u32[]{:S(2)}, u32[]{:S(2)}) %collective-permute-start.2) | collective-permute-done | bytes 65568 | tf_op jit(solution)/shard_map/ppermute | solution.py:524
  11.4 0.8 %far_products.1 = f32[4,8,8,512]{3,2,1,0:T(8,128)} custom-call(f32[4,4,8,512]{3,2,1,0:T(8,128)S(1)} %get-tuple-element.25.refs_0_, bf16[2,4,4,8,512]{4,3,2,1,0:T(8,128)(2,1)S(1)} %get-tuple-element.26.refs_1_, bf16[2,4,8,512]{3,2,1,0:T(8,128)(2,1)S(1)} %collective-permute-done.2.refs_2_, ...), custom_call_target="tpu_custom_call", output_to_operand_aliasing={{}: (3, {})} | custom-call | flops 1000000 | bytes 1000000 | tf_op jit(solution)/shard_map/far_products/pallas_call | solution.py:557
Async XLA Ops:
  1.0 3.6 %collective-permute-start = (s32[19,8,128]{2,1,0:T(8,128)S(1)}, s32[19,8,128]{2,1,0:T(8,128)S(1)}, u32[]{:S(2)}, u32[]{:S(2)}) collective-permute-start(s32[19,8,128]{2,1,0:T(8,128)S(1)} %get-tuple-element.18), channel_id=1, source_target_pairs={{0,2},{4,6},{8,10},{12,14},{16,18},{20,22},{24,26},{28,30},{2,0},{... | collective-permute-start | bytes 233480 | tf_op jit(solution)/shard_map/ppermute | solution.py:47
  1.5 5.0 %collective-permute-start.1 = (s32[19,8,128]{2,1,0:T(8,128)S(1)}, s32[19,8,128]{2,1,0:T(8,128)S(1)}, u32[]{:S(2)}, u32[]{:S(2)}) collective-permute-start(s32[19,8,128]{2,1,0:T(8,128)S(1)} %get-tuple-element.24), channel_id=1, source_target_pairs={{2,4},{3,5},{6,8},{7,9},{10,12},{11,13},{14,16},{15,17},{18,20},{1... | collective-permute-start | bytes 233480 | tf_op jit(solution)/shard_map/ppermute | solution.py:55
  5.1 3.8 %copy-start = (bf16[1,4,4,8,8,512]{5,4,3,2,1,0:T(8,128)(2,1)S(1)}, bf16[1,4,4,8,8,512]{5,4,3,2,1,0:T(8,128)(2,1)}, u32[]{:S(2)}) copy-start(bf16[1,4,4,8,8,512]{5,4,3,2,1,0:T(8,128)(2,1)} %param.6) | copy-start | bytes 3145732
  5.1 4.6 %collective-permute-start.3 = (bf16[2,4,8,512]{3,2,1,0:T(8,128)(2,1)S(1)}, bf16[2,4,8,512]{3,2,1,0:T(8,128)(2,1)S(1)}, u32[]{:S(2)}, u32[]{:S(2)}) collective-permute-start(bf16[2,4,8,512]{3,2,1,0:T(8,128)(2,1)S(1)} %inner_rows.1.refs_2_), channel_id=1, source_target_pairs={{0,1},{1,0},{2,3},{3,2},{4,5},{5,4},{6,7},{7,6},{8,9},{9,8},{10,11... | collective-permute-start | bytes 196616 | tf_op jit(solution)/shard_map/ppermute | solution.py:524
  6.8 2.1 %copy-start.1 = (s32[4]{0:T(128)S(1)}, s32[4]{0:T(128)}, u32[]{:S(2)}) copy-start(s32[4]{0:T(128)} %refs_1_.1) | copy-start | bytes 52
  6.8 4.6 %collective-permute-start.2 = (bf16[2,4,8,512]{3,2,1,0:T(8,128)(2,1)S(1)}, bf16[2,4,8,512]{3,2,1,0:T(8,128)(2,1)S(1)}, u32[]{:S(2)}, u32[]{:S(2)}) collective-permute-start(bf16[2,4,8,512]{3,2,1,0:T(8,128)(2,1)S(1)} %outer_rows.1.refs_3_), channel_id=1, source_target_pairs={{0,1},{1,0},{2,3},{3,2},{4,5},{5,4},{6,7},{7,6},{8,9},{9,8},{10,11... | collective-permute-start | bytes 196616 | tf_op jit(solution)/shard_map/ppermute | solution.py:524

commit v10 on v9

--- a/solution.py
+++ b/solution.py
@@ -131,7 +131,9 @@
     return jnp.concatenate([word & 0xFFFF for word in words] + [word >> 16 for word in words], axis=1)
 
 
-def pack_kernel(controls, mask, diffusivity, across, within, mine, codes, table, sems):
+def pack_kernel(
+    controls, mask, diffusivity, across, within, mine, codes, table, kept, coef, halves, sems, *scratch
+):
     odd = parity()
     slots = controls.shape[0]
     copies = [
@@ -164,6 +166,10 @@
     for side, packet, arriving in ((OUTER, across, outer), (INNER, within, inner)):
         encode(slots, functools.partial(read, side, arriving), functools.partial(code, side), packet)
 
+    @pl.when(starts_first())
+    def _():
+        own_rows(mine, codes, table, kept, coef, halves, *scratch)
+
 
 def by_level(table, kind, shape):
     levels = shape[0]
@@ -195,7 +201,19 @@
 PART, VALUE, KEPT = 0, SWEEPS, 2 * SWEEPS - 1
 
 
-def middle_kernel(controls, codes, table, kept, coef, halves, shifted, face, centre, east, west, field):
+def starts_first():
+    return jnp.logical_and(lax.axis_index("tile") == 0, lax.axis_index("tm") == 0)
+
+
+def middle_kernel(controls, codes, table, *refs):
+    kept, coef, halves = refs[3:6]
+
+    @pl.when(jnp.logical_not(starts_first()))
+    def _():
+        own_rows(controls, codes, table, kept, coef, halves, *refs[6:])
+
+
+def own_rows(controls, codes, table, kept, coef, halves, shifted, face, centre, east, west, field):
     odd = parity()
     slots, _, levels, columns = controls.shape
     shape = (levels, columns)
@@ -465,7 +483,15 @@
     dma = pltpu.SemaphoreType.DMA
 
     packet = pltpu.VMEM((unit_count(slots), levels, columns // QUARTERS), jnp.int32)
-    my_across, my_within, mine, codes, table = pl.pallas_call(
+    middle_scratch = [pltpu.VMEM((2, height, columns), jnp.int32)]
+    middle_scratch += [pltpu.VMEM((height, *row), f32)] * 4
+    middle_scratch += [pltpu.VMEM((SWEEPS - 1, slots, height, *row), f32)]
+    middle_out = (
+        pltpu.VMEM((2, slots, KEPT, *row), f32),
+        pltpu.VMEM((2, COEFS, *row), f32),
+        pltpu.VMEM((2, *row), f32),
+    )
+    my_across, my_within, mine, codes, table, *middle = pl.pallas_call(
         pack_kernel,
         out_shape=(
             packet,
@@ -473,10 +499,11 @@
             pltpu.VMEM(controls.shape, f32),
             pltpu.VMEM((height, columns), jnp.int32),
             pltpu.VMEM((2, levels), f32),
+            *middle_out,
         ),
         in_specs=[ANY, ANY, ANY],
-        out_specs=(VMEM,) * 5,
-        scratch_shapes=[dma((2 * 2 * slots + 2,))],
+        out_specs=(VMEM,) * 8,
+        scratch_shapes=[dma((4 * slots + 2,)), *middle_scratch],
         compiler_params=PARAMS,
         name="pack",
     )(far(controls), far(land_mask), far(diffusivity))
@@ -485,23 +512,17 @@
     mine = near(mine)
 
     half = pltpu.VMEM((slots, SWEEPS, *row), bf16)
-    middle_scratch = [pltpu.VMEM((2, height, columns), jnp.int32)]
-    middle_scratch += [pltpu.VMEM((height, *row), f32)] * 4
-    middle_scratch += [pltpu.VMEM((SWEEPS - 1, slots, height, *row), f32)]
     kept, coef, halves = pl.pallas_call(
         middle_kernel,
-        out_shape=(
-            pltpu.VMEM((2, slots, KEPT, *row), f32),
-            pltpu.VMEM((2, COEFS, *row), f32),
-            pltpu.VMEM((2, *row), f32),
-        ),
-        in_specs=[VMEM] * 3,
+        out_shape=middle_out,
+        in_specs=[VMEM] * 6,
         out_specs=(VMEM,) * 3,
         scratch_shapes=middle_scratch,
+        input_output_aliases={3: 0, 4: 1, 5: 2},
         compiler_params=PARAMS,
         cost_estimate=cost(1, 1),
         name="middle",
-    )(mine, near(codes), near(table))
+    )(mine, near(codes), near(table), *map(near, middle))
     shared = (near(kept), near(coef), near(halves))
 
     def side(kernel, name, *operands):

time: 12.3 us -> 12.3 us (level)
    ppermute x2, starting transfers between devices: 2.8 us -> 3.34 us  [shift(): lax.ppermute(value, 'tm', [(i, (i + step) % count) for i in range(count)])]
    pallas_call x1, Pallas kernels: 0.53 us -> 0.01 us  [on_device(): pl.pallas_call(middle_kernel, out_shape=middle_out, in_specs=[VMEM] * 6,...]
    pallas_call x1, Pallas kernels: 1.01 us -> 1.53 us  [on_device(): pl.pallas_call(pack_kernel, out_shape=(packet, packet, pltpu.VMEM(control...]
    ppermute x1, starting transfers between devices: 0.52 us -> 0.07 us  [swap_within(): return lax.ppermute(value, 'tile', pairs + [(b, a) for a, b in pairs])]
  transfers between devices with their start and end apart: 4 -> 4, of which waited for: 2 -> 2; matrix products, arithmetic and copies ran while one was open for 0% -> 0% of each run, Pallas kernels for 24% -> 19%
where the time goes in v10:
time: 12.3 us; the launch traced here: 12.1 us
  starting transfers between devices  5.92 us (48%)
  Pallas kernels  4.64 us (38%)
  waiting for transfers between devices  1.49 us (12%)
    ppermute x2, starting transfers between devices, shift(): lax.ppermute(value, 'tm', [(i, (i + step) % count) for i in range(count)])  3.34 us
    ppermute x1, starting transfers between devices, swap_across(): return lax.ppermute(value, ('tile', 'tm'), flat + [(b, a) for a, b in flat])  2.51 us
    pallas_call x1, Pallas kernels, on_device(): pl.pallas_call(pack_kernel, out_shape=(packet, packet, pltpu.VMEM(control...  1.53 us
    pallas_call x1, Pallas kernels, on_device(): pl.pallas_call(lambda *refs: own_kernel(factor, *refs), out_shape=(part,...  0.88 us
    ppermute x2, waiting for transfers between devices, shift(): lax.ppermute(value, 'tm', [(i, (i + step) % count) for i in range(count)])  0.83 us
    pallas_call x1, Pallas kernels, on_device(): pl.pallas_call(lambda *refs: near_kernel(factor, *refs), out_shape=result...  0.77 us
    pallas_call x1, Pallas kernels, on_device(): pl.pallas_call(lambda *refs: far_kernel(factor, *refs), out_shape=result,...  0.77 us
    pallas_call x2, Pallas kernels, side(): pl.pallas_call(kernel, out_shape=half, in_specs=[VMEM] * len(operands), o...  0.7 us
  transfers between devices with their start and end apart: 4, of which 2 were waited for; matrix products, arithmetic and copies ran while one was open for 0% of the time, Pallas kernels for 19%

profile of v10, /device:TPU:0, one launch (start us, length us, event | category | flops | bytes accessed | tf_op | source)
XLA Modules:
  0.0 12.1 jit_solution(6140660778094494959)
XLA Ops:
  0.0 1.5 %pack.1 = (s32[19,8,128]{2,1,0:T(8,128)S(1)}, s32[19,8,128]{2,1,0:T(8,128)S(1)}, f32[2,8,8,512]{3,2,1,0:T(8,128)S(1)}, s32[8,512]{1,0:T(8,128)S(1)}, f32[2,8]{1,...) custom-call(f32[2,8,8,512]{3,2,1,0:T(8,128)} %controls.1, ...), custom_call_target="tpu_custom_call" | custom-call | tf_op jit(solution)/shard_map/pack/pallas_call | solution.py:494
  1.5 0.1 collective-permute-start
  1.6 2.5 %collective-permute-start.1 = (s32[19,8,128]{2,1,0:T(8,128)S(1)}, s32[19,8,128]{2,1,0:T(8,128)S(1)}, u32[]{:S(2)}, u32[]{:S(2)}) collective-permute-start(s32[19,8,128]{2,1,0:T(8,128)S(1)} %get-tuple-element.30), channel_id=1, source_target_pairs={{2,4},{3,5},{6,8},{7,9},{10,12},{11,13},{14,16},{15,17},{18,20},{1... | collective-permute-start | bytes 233480 | tf_op jit(solution)/shard_map/ppermute | solution.py:55
  4.1 0.0 collective-permute-done.packet
  4.1 0.4 %inner_rows.1.refs_2_ = bf16[2,4,8,512]{3,2,1,0:T(8,128)(2,1)S(1)} custom-call(f32[2,8,8,512]{3,2,1,0:T(8,128)S(1)} %get-tuple-element.20.controls, s32[19,8,128]{2,1,0:T(8,128)S(1)} %collective-permute-done.packet, f32[2,2,7,8,512]{4,3,2,1,0:T(8,128)S(1)} %get-tuple-element.27.kept, f32[2,17,8,512]{3,2,1,0:T(8,128)S(1)} %get-tuple-element.28.coef, ...), custom_call_target="tpu_custom_call" | custom-call | flops 1 | bytes 1 | tf_op jit(solution)/shard_map/inner_rows/pallas_call | solution.py:529
  4.6 0.0 copy-start
  4.6 1.3 %collective-permute-start.3 = (bf16[2,4,8,512]{3,2,1,0:T(8,128)(2,1)S(1)}, bf16[2,4,8,512]{3,2,1,0:T(8,128)(2,1)S(1)}, u32[]{:S(2)}, u32[]{:S(2)}) collective-permute-start(bf16[2,4,8,512]{3,2,1,0:T(8,128)(2,1)S(1)} %inner_rows.1.refs_2_), channel_id=1, source_target_pairs={{0,1},{1,0},{2,3},{3,2},{4,5},{5,4},{6,7},{7,6},{8,9},{9,8},{10,11... | collective-permute-start | bytes 196616 | tf_op jit(solution)/shard_map/ppermute | solution.py:545
  5.8 0.7 %collective-permute-done.1.packet = s32[19,8,128]{2,1,0:T(8,128)S(1)} collective-permute-done((s32[19,8,128]{2,1,0:T(8,128)S(1)}, s32[19,8,128]{2,1,0:T(8,128)S(1)}, u32[]{:S(2)}, u32[]{:S(2)}) %collective-permute-start.1) | collective-permute-done | bytes 77856 | tf_op jit(solution)/shard_map/ppermute | solution.py:55
  6.5 0.3 %outer_rows.1.refs_3_ = bf16[2,4,8,512]{3,2,1,0:T(8,128)(2,1)S(1)} custom-call(f32[2,8,8,512]{3,2,1,0:T(8,128)S(1)} %get-tuple-element.20.controls, s32[19,8,128]{2,1,0:T(8,128)S(1)} %collective-permute-done.1.packet, f32[2,2,7,8,512]{4,3,2,1,0:T(8,128)S(1)} %get-tuple-element.27.kept, f32[2,17,8,512]{3,2,1,0:T(8,128)S(1)} %get-tuple-element.28.coef, ...), custom_call_target="tpu_custom_call" | custom-call | flops 1 | bytes 1 | tf_op jit(solution)/shard_map/outer_rows/pallas_call | solution.py:529
  6.8 0.0 copy-start.1
  6.8 2.1 %collective-permute-start.2 = (bf16[2,4,8,512]{3,2,1,0:T(8,128)(2,1)S(1)}, bf16[2,4,8,512]{3,2,1,0:T(8,128)(2,1)S(1)}, u32[]{:S(2)}, u32[]{:S(2)}) collective-permute-start(bf16[2,4,8,512]{3,2,1,0:T(8,128)(2,1)S(1)} %outer_rows.1.refs_3_), channel_id=1, source_target_pairs={{0,1},{1,0},{2,3},{3,2},{4,5},{5,4},{6,7},{7,6},{8,9},{9,8},{10,11... | collective-permute-start | bytes 196616 | tf_op jit(solution)/shard_map/ppermute | solution.py:545
  8.9 0.0 copy-done
  8.9 0.0 copy-done.1
  8.9 0.9 %own_products.1 = (f32[4,4,8,512]{3,2,1,0:T(8,128)S(1)}, f32[4,4,8,512]{3,2,1,0:T(8,128)S(1)}, bf16[2,4,4,8,512]{4,3,2,1,0:T(8,128)(2,1)S(1)}, bf16[2,4,4,8,512]{4,3,2,1,0:T(8,128)(2,1)S(1)}) custom-call(bf16[4,4,8,8,512]{4,3,2,1,0:T(8,128)(2,1)S(1)} %bitcast.2, s32[4]{0:T(128)S(1)} %copy-done.1, bf16[2,4,8,512]{3,2,1,0:T(8,128)(2,1)S(1)} %inner_rows.1.refs_2_, ...), custom_call_target="tpu_custom_call" | custom-call | flops 4000000 | bytes 2000000 | tf_op jit(solution)/shard_map/own_products/pallas_call | solution.py:556
  9.8 0.0 collective-permute-done.3.refs_2_
  9.8 0.8 %near_products.1.refs_3_ = f32[4,8,8,512]{3,2,1,0:T(8,128)} custom-call(f32[4,4,8,512]{3,2,1,0:T(8,128)S(1)} %get-tuple-element.33.refs_0_, bf16[2,4,4,8,512]{4,3,2,1,0:T(8,128)(2,1)S(1)} %get-tuple-element.34.refs_1_, bf16[2,4,8,512]{3,2,1,0:T(8,128)(2,1)S(1)} %collective-permute-done.3.refs_2_), custom_call_target="tpu_custom_call" | custom-call | flops 1000000 | bytes 1000000 | tf_op jit(solution)/shard_map/near_products/pallas_call | solution.py:568
  10.6 0.8 %collective-permute-done.2.refs_2_ = bf16[2,4,8,512]{3,2,1,0:T(8,128)(2,1)S(1)} collective-permute-done((bf16[2,4,8,512]{3,2,1,0:T(8,128)(2,1)S(1)}, bf16[2,4,8,512]{3,2,1,0:T(8,128)(2,1)S(1)}, u32[]{:S(2)}, u32[]{:S(2)}) %collective-permute-start.2) | collective-permute-done | bytes 65568 | tf_op jit(solution)/shard_map/ppermute | solution.py:545
  11.4 0.8 %far_products.1 = f32[4,8,8,512]{3,2,1,0:T(8,128)} custom-call(f32[4,4,8,512]{3,2,1,0:T(8,128)S(1)} %get-tuple-element.31.refs_0_, bf16[2,4,4,8,512]{4,3,2,1,0:T(8,128)(2,1)S(1)} %get-tuple-element.32.refs_1_, bf16[2,4,8,512]{3,2,1,0:T(8,128)(2,1)S(1)} %collective-permute-done.2.refs_2_, ...), custom_call_target="tpu_custom_call", output_to_operand_aliasing={{}: (3, {})} | custom-call | flops 1000000 | bytes 1000000 | tf_op jit(solution)/shard_map/far_products/pallas_call | solution.py:578
  (1 shorter events, 0.0 us)
Async XLA Ops:
  1.5 2.6 %collective-permute-start = (s32[19,8,128]{2,1,0:T(8,128)S(1)}, s32[19,8,128]{2,1,0:T(8,128)S(1)}, u32[]{:S(2)}, u32[]{:S(2)}) collective-permute-start(s32[19,8,128]{2,1,0:T(8,128)S(1)} %get-tuple-element.21), channel_id=1, source_target_pairs={{0,2},{4,6},{8,10},{12,14},{16,18},{20,22},{24,26},{28,30},{2,0},{... | collective-permute-start | bytes 233480 | tf_op jit(solution)/shard_map/ppermute | solution.py:47
  1.6 4.9 %collective-permute-start.1 = (s32[19,8,128]{2,1,0:T(8,128)S(1)}, s32[19,8,128]{2,1,0:T(8,128)S(1)}, u32[]{:S(2)}, u32[]{:S(2)}) collective-permute-start(s32[19,8,128]{2,1,0:T(8,128)S(1)} %get-tuple-element.30), channel_id=1, source_target_pairs={{2,4},{3,5},{6,8},{7,9},{10,12},{11,13},{14,16},{15,17},{18,20},{1... | collective-permute-start | bytes 233480 | tf_op jit(solution)/shard_map/ppermute | solution.py:55
  4.6 4.3 %copy-start = (bf16[1,4,4,8,8,512]{5,4,3,2,1,0:T(8,128)(2,1)S(1)}, bf16[1,4,4,8,8,512]{5,4,3,2,1,0:T(8,128)(2,1)}, u32[]{:S(2)}) copy-start(bf16[1,4,4,8,8,512]{5,4,3,2,1,0:T(8,128)(2,1)} %param.6) | copy-start | bytes 3145732
  4.6 5.2 %collective-permute-start.3 = (bf16[2,4,8,512]{3,2,1,0:T(8,128)(2,1)S(1)}, bf16[2,4,8,512]{3,2,1,0:T(8,128)(2,1)S(1)}, u32[]{:S(2)}, u32[]{:S(2)}) collective-permute-start(bf16[2,4,8,512]{3,2,1,0:T(8,128)(2,1)S(1)} %inner_rows.1.refs_2_), channel_id=1, source_target_pairs={{0,1},{1,0},{2,3},{3,2},{4,5},{5,4},{6,7},{7,6},{8,9},{9,8},{10,11... | collective-permute-start | bytes 196616 | tf_op jit(solution)/shard_map/ppermute | solution.py:545
  6.8 2.1 %copy-start.1 = (s32[4]{0:T(128)S(1)}, s32[4]{0:T(128)}, u32[]{:S(2)}) copy-start(s32[4]{0:T(128)} %refs_1_.1) | copy-start | bytes 52
  6.8 4.6 %collective-permute-start.2 = (bf16[2,4,8,512]{3,2,1,0:T(8,128)(2,1)S(1)}, bf16[2,4,8,512]{3,2,1,0:T(8,128)(2,1)S(1)}, u32[]{:S(2)}, u32[]{:S(2)}) collective-permute-start(bf16[2,4,8,512]{3,2,1,0:T(8,128)(2,1)S(1)} %outer_rows.1.refs_3_), channel_id=1, source_target_pairs={{0,1},{1,0},{2,3},{3,2},{4,5},{5,4},{6,7},{7,6},{8,9},{9,8},{10,11... | collective-permute-start | bytes 196616 | tf_op jit(solution)/shard_map/ppermute | solution.py:545

commit v11 on v9

--- a/solution.py
+++ b/solution.py
@@ -146,7 +146,7 @@
                     pltpu.make_async_copy(controls.at[slot, rows], mine.at[slot, rows], sems.at[len(copies)])
                 )
     own, outer, inner = copies[:2], copies[2 : 2 + 2 * slots], copies[2 + 2 * slots :]
-    for copy in outer + own + inner:
+    for copy in own[:1] + outer + inner + own[1:]:
         copy.start()
 
     def read(side, arriving, slot, k):

time: 12.3 us -> 12.3 us (level)
  no operation moved by 1% of the time
where the time goes in v11:
time: 12.3 us; the launch traced here: 12.1 us
  starting transfers between devices  5.91 us (48%)
  Pallas kernels  4.63 us (38%)
  waiting for transfers between devices  1.5 us (12%)
    ppermute x2, starting transfers between devices, shift(): lax.ppermute(value, 'tm', [(i, (i + step) % count) for i in range(count)])  2.8 us
    ppermute x1, starting transfers between devices, swap_across(): return lax.ppermute(value, ('tile', 'tm'), flat + [(b, a) for a, b in flat])  2.59 us
    pallas_call x1, Pallas kernels, on_device(): pl.pallas_call(pack_kernel, out_shape=(packet, packet, pltpu.VMEM(control...  0.99 us
    pallas_call x1, Pallas kernels, on_device(): pl.pallas_call(lambda *refs: own_kernel(factor, *refs), out_shape=(part,...  0.87 us
    ppermute x2, waiting for transfers between devices, shift(): lax.ppermute(value, 'tm', [(i, (i + step) % count) for i in range(count)])  0.83 us
    pallas_call x1, Pallas kernels, on_device(): pl.pallas_call(lambda *refs: near_kernel(factor, *refs), out_shape=result...  0.77 us
    pallas_call x1, Pallas kernels, on_device(): pl.pallas_call(lambda *refs: far_kernel(factor, *refs), out_shape=result,...  0.77 us
    pallas_call x2, Pallas kernels, side(): pl.pallas_call(kernel, out_shape=half, in_specs=[VMEM] * len(operands), o...  0.7 us
  transfers between devices with their start and end apart: 4, of which 2 were waited for; matrix products, arithmetic and copies ran while one was open for 0% of the time, Pallas kernels for 24%

profile of v11, /device:TPU:0, one launch (start us, length us, event | category | flops | bytes accessed | tf_op | source)
XLA Modules:
  0.0 12.1 jit_solution(10814402622824462138)
XLA Ops:
  0.0 1.0 %pack.1 = (s32[19,8,128]{2,1,0:T(8,128)S(1)}, s32[19,8,128]{2,1,0:T(8,128)S(1)}, f32[2,8,8,512]{3,2,1,0:T(8,128)S(1)}, s32[8,512]{1,0:T(8,128)S(1)}, f32[2,8]{1,0:T(2,128)S(1)}) custom-call(f32[2,8,8,512]{3,2,1,0:T(8,128)} %controls.1, s32[8,512]{1,0:T(8,128)} %mask.1, f32[2,8]{1,0:T(2,128)} %diffusivity.1), custom_call_target="tpu_custom_call" | custom-call | tf_op jit(solution)/shard_map/pack/pallas_call | solution.py:468
  1.0 0.5 %collective-permute-start = (s32[19,8,128]{2,1,0:T(8,128)S(1)}, s32[19,8,128]{2,1,0:T(8,128)S(1)}, u32[]{:S(2)}, u32[]{:S(2)}) collective-permute-start(s32[19,8,128]{2,1,0:T(8,128)S(1)} %get-tuple-element.18), channel_id=1, source_target_pairs={{0,2},{4,6},{8,10},{12,14},{16,18},{20,22},{24,26},{28,30},{2,0},{... | collective-permute-start | bytes 233480 | tf_op jit(solution)/shard_map/ppermute | solution.py:47
  1.5 2.6 %collective-permute-start.1 = (s32[19,8,128]{2,1,0:T(8,128)S(1)}, s32[19,8,128]{2,1,0:T(8,128)S(1)}, u32[]{:S(2)}, u32[]{:S(2)}) collective-permute-start(s32[19,8,128]{2,1,0:T(8,128)S(1)} %get-tuple-element.24), channel_id=1, source_target_pairs={{2,4},{3,5},{6,8},{7,9},{10,12},{11,13},{14,16},{15,17},{18,20},{1... | collective-permute-start | bytes 233480 | tf_op jit(solution)/shard_map/ppermute | solution.py:55
  4.1 0.5 %middle.1 = (f32[2,2,7,8,512]{4,3,2,1,0:T(8,128)S(1)}, f32[2,17,8,512]{3,2,1,0:T(8,128)S(1)}, f32[2,8,512]{2,1,0:T(8,128)S(1)}) custom-call(f32[2,8,8,512]{3,2,1,0:T(8,128)S(1)} %get-tuple-element.17.controls, s32[8,512]{1,0:T(8,128)S(1)} %get-tuple-element.19.codes, f32[2,8]{1,0:T(2,128)S(1)} %get-tuple-element.20.table), custom_call_target="tpu_custom_call" | custom-call | flops 1 | bytes 1 | tf_op jit(solution)/shard_map/middle/pallas_call | solution.py:491
  4.6 0.0 collective-permute-done.packet
  4.7 0.4 %inner_rows.1.refs_2_ = bf16[2,4,8,512]{3,2,1,0:T(8,128)(2,1)S(1)} custom-call(f32[2,8,8,512]{3,2,1,0:T(8,128)S(1)} %get-tuple-element.17.controls, s32[19,8,128]{2,1,0:T(8,128)S(1)} %collective-permute-done.packet, f32[2,2,7,8,512]{4,3,2,1,0:T(8,128)S(1)} %get-tuple-element.21.kept, f32[2,17,8,512]{3,2,1,0:T(8,128)S(1)} %get-tuple-element.22.coef, ...), custom_call_target="tpu_custom_call" | custom-call | flops 1 | bytes 1 | tf_op jit(solution)/shard_map/inner_rows/pallas_call | solution.py:508
  5.1 0.0 copy-start
  5.1 0.7 %collective-permute-start.3 = (bf16[2,4,8,512]{3,2,1,0:T(8,128)(2,1)S(1)}, bf16[2,4,8,512]{3,2,1,0:T(8,128)(2,1)S(1)}, u32[]{:S(2)}, u32[]{:S(2)}) collective-permute-start(bf16[2,4,8,512]{3,2,1,0:T(8,128)(2,1)S(1)} %inner_rows.1.refs_2_), channel_id=1, source_target_pairs={{0,1},{1,0},{2,3},{3,2},{4,5},{5,4},{6,7},{7,6},{8,9},{9,8},{10,11... | collective-permute-start | bytes 196616 | tf_op jit(solution)/shard_map/ppermute | solution.py:524
  5.8 0.7 %collective-permute-done.1.packet = s32[19,8,128]{2,1,0:T(8,128)S(1)} collective-permute-done((s32[19,8,128]{2,1,0:T(8,128)S(1)}, s32[19,8,128]{2,1,0:T(8,128)S(1)}, u32[]{:S(2)}, u32[]{:S(2)}) %collective-permute-start.1) | collective-permute-done | bytes 77856 | tf_op jit(solution)/shard_map/ppermute | solution.py:55
  6.5 0.3 %outer_rows.1.refs_3_ = bf16[2,4,8,512]{3,2,1,0:T(8,128)(2,1)S(1)} custom-call(f32[2,8,8,512]{3,2,1,0:T(8,128)S(1)} %get-tuple-element.17.controls, s32[19,8,128]{2,1,0:T(8,128)S(1)} %collective-permute-done.1.packet, f32[2,2,7,8,512]{4,3,2,1,0:T(8,128)S(1)} %get-tuple-element.21.kept, f32[2,17,8,512]{3,2,1,0:T(8,128)S(1)} %get-tuple-element.22.coef, ...), custom_call_target="tpu_custom_call" | custom-call | flops 1 | bytes 1 | tf_op jit(solution)/shard_map/outer_rows/pallas_call | solution.py:508
  6.8 0.0 copy-start.1
  6.8 2.1 %collective-permute-start.2 = (bf16[2,4,8,512]{3,2,1,0:T(8,128)(2,1)S(1)}, bf16[2,4,8,512]{3,2,1,0:T(8,128)(2,1)S(1)}, u32[]{:S(2)}, u32[]{:S(2)}) collective-permute-start(bf16[2,4,8,512]{3,2,1,0:T(8,128)(2,1)S(1)} %outer_rows.1.refs_3_), channel_id=1, source_target_pairs={{0,1},{1,0},{2,3},{3,2},{4,5},{5,4},{6,7},{7,6},{8,9},{9,8},{10,11... | collective-permute-start | bytes 196616 | tf_op jit(solution)/shard_map/ppermute | solution.py:524
  8.9 0.0 copy-done
  8.9 0.0 copy-done.1
  8.9 0.9 %own_products.1 = (f32[4,4,8,512]{3,2,1,0:T(8,128)S(1)}, f32[4,4,8,512]{3,2,1,0:T(8,128)S(1)}, bf16[2,4,4,8,512]{4,3,2,1,0:T(8,128)(2,1)S(1)}, bf16[2,4,4,8,512]{4,3,2,1,0:T(8,128)(2,1)S(1)}) custom-call(bf16[4,4,8,8,512]{4,3,2,1,0:T(8,128)(2,1)S(1)} %bitcast.2, s32[4]{0:T(128)S(1)} %copy-done.1, bf16[2,4,8,512]{3,2,1,0:T(8,128)(2,1)S(1)} %inner_rows.1.refs_2_, ...), custom_call_target="tpu_custom_call" | custom-call | flops 4000000 | bytes 2000000 | tf_op jit(solution)/shard_map/own_products/pallas_call | solution.py:535
  9.7 0.0 collective-permute-done.3.refs_2_
  9.8 0.8 %near_products.1.refs_3_ = f32[4,8,8,512]{3,2,1,0:T(8,128)} custom-call(f32[4,4,8,512]{3,2,1,0:T(8,128)S(1)} %get-tuple-element.27.refs_0_, bf16[2,4,4,8,512]{4,3,2,1,0:T(8,128)(2,1)S(1)} %get-tuple-element.28.refs_1_, bf16[2,4,8,512]{3,2,1,0:T(8,128)(2,1)S(1)} %collective-permute-done.3.refs_2_), custom_call_target="tpu_custom_call" | custom-call | flops 1000000 | bytes 1000000 | tf_op jit(solution)/shard_map/near_products/pallas_call | solution.py:547
  10.5 0.8 %collective-permute-done.2.refs_2_ = bf16[2,4,8,512]{3,2,1,0:T(8,128)(2,1)S(1)} collective-permute-done((bf16[2,4,8,512]{3,2,1,0:T(8,128)(2,1)S(1)}, bf16[2,4,8,512]{3,2,1,0:T(8,128)(2,1)S(1)}, u32[]{:S(2)}, u32[]{:S(2)}) %collective-permute-start.2) | collective-permute-done | bytes 65568 | tf_op jit(solution)/shard_map/ppermute | solution.py:524
  11.4 0.8 %far_products.1 = f32[4,8,8,512]{3,2,1,0:T(8,128)} custom-call(f32[4,4,8,512]{3,2,1,0:T(8,128)S(1)} %get-tuple-element.25.refs_0_, bf16[2,4,4,8,512]{4,3,2,1,0:T(8,128)(2,1)S(1)} %get-tuple-element.26.refs_1_, bf16[2,4,8,512]{3,2,1,0:T(8,128)(2,1)S(1)} %collective-permute-done.2.refs_2_, ...), custom_call_target="tpu_custom_call", output_to_operand_aliasing={{}: (3, {})} | custom-call | flops 1000000 | bytes 1000000 | tf_op jit(solution)/shard_map/far_products/pallas_call | solution.py:557
Async XLA Ops:
  1.0 3.6 %collective-permute-start = (s32[19,8,128]{2,1,0:T(8,128)S(1)}, s32[19,8,128]{2,1,0:T(8,128)S(1)}, u32[]{:S(2)}, u32[]{:S(2)}) collective-permute-start(s32[19,8,128]{2,1,0:T(8,128)S(1)} %get-tuple-element.18), channel_id=1, source_target_pairs={{0,2},{4,6},{8,10},{12,14},{16,18},{20,22},{24,26},{28,30},{2,0},{... | collective-permute-start | bytes 233480 | tf_op jit(solution)/shard_map/ppermute | solution.py:47
  1.5 5.0 %collective-permute-start.1 = (s32[19,8,128]{2,1,0:T(8,128)S(1)}, s32[19,8,128]{2,1,0:T(8,128)S(1)}, u32[]{:S(2)}, u32[]{:S(2)}) collective-permute-start(s32[19,8,128]{2,1,0:T(8,128)S(1)} %get-tuple-element.24), channel_id=1, source_target_pairs={{2,4},{3,5},{6,8},{7,9},{10,12},{11,13},{14,16},{15,17},{18,20},{1... | collective-permute-start | bytes 233480 | tf_op jit(solution)/shard_map/ppermute | solution.py:55
  5.1 3.8 %copy-start = (bf16[1,4,4,8,8,512]{5,4,3,2,1,0:T(8,128)(2,1)S(1)}, bf16[1,4,4,8,8,512]{5,4,3,2,1,0:T(8,128)(2,1)}, u32[]{:S(2)}) copy-start(bf16[1,4,4,8,8,512]{5,4,3,2,1,0:T(8,128)(2,1)} %param.6) | copy-start | bytes 3145732
  5.1 4.6 %collective-permute-start.3 = (bf16[2,4,8,512]{3,2,1,0:T(8,128)(2,1)S(1)}, bf16[2,4,8,512]{3,2,1,0:T(8,128)(2,1)S(1)}, u32[]{:S(2)}, u32[]{:S(2)}) collective-permute-start(bf16[2,4,8,512]{3,2,1,0:T(8,128)(2,1)S(1)} %inner_rows.1.refs_2_), channel_id=1, source_target_pairs={{0,1},{1,0},{2,3},{3,2},{4,5},{5,4},{6,7},{7,6},{8,9},{9,8},{10,11... | collective-permute-start | bytes 196616 | tf_op jit(solution)/shard_map/ppermute | solution.py:524
  6.8 2.1 %copy-start.1 = (s32[4]{0:T(128)S(1)}, s32[4]{0:T(128)}, u32[]{:S(2)}) copy-start(s32[4]{0:T(128)} %refs_1_.1) | copy-start | bytes 52
  6.8 4.6 %collective-permute-start.2 = (bf16[2,4,8,512]{3,2,1,0:T(8,128)(2,1)S(1)}, bf16[2,4,8,512]{3,2,1,0:T(8,128)(2,1)S(1)}, u32[]{:S(2)}, u32[]{:S(2)}) collective-permute-start(bf16[2,4,8,512]{3,2,1,0:T(8,128)(2,1)S(1)} %outer_rows.1.refs_3_), channel_id=1, source_target_pairs={{0,1},{1,0},{2,3},{3,2},{4,5},{5,4},{6,7},{7,6},{8,9},{9,8},{10,11... | collective-permute-start | bytes 196616 | tf_op jit(solution)/shard_map/ppermute | solution.py:524

commit v12 on v10

--- a/solution.py
+++ b/solution.py
@@ -148,7 +148,7 @@
                     pltpu.make_async_copy(controls.at[slot, rows], mine.at[slot, rows], sems.at[len(copies)])
                 )
     own, outer, inner = copies[:2], copies[2 : 2 + 2 * slots], copies[2 + 2 * slots :]
-    for copy in outer + own + inner:
+    for copy in own[:1] + outer + inner + own[1:]:
         copy.start()
 
     def read(side, arriving, slot, k):

time: 12.3 us -> 12.3 us (level)
  no operation moved by 1% of the time
where the time goes in v12:
time: 12.3 us; the launch traced here: 12.1 us
  starting transfers between devices  5.92 us (48%)
  Pallas kernels  4.63 us (38%)
  waiting for transfers between devices  1.49 us (12%)
    ppermute x2, starting transfers between devices, shift(): lax.ppermute(value, 'tm', [(i, (i + step) % count) for i in range(count)])  3.34 us
    ppermute x1, starting transfers between devices, swap_across(): return lax.ppermute(value, ('tile', 'tm'), flat + [(b, a) for a, b in flat])  2.51 us
    pallas_call x1, Pallas kernels, on_device(): pl.pallas_call(pack_kernel, out_shape=(packet, packet, pltpu.VMEM(control...  1.52 us
    pallas_call x1, Pallas kernels, on_device(): pl.pallas_call(lambda *refs: own_kernel(factor, *refs), out_shape=(part,...  0.88 us
    ppermute x2, waiting for transfers between devices, shift(): lax.ppermute(value, 'tm', [(i, (i + step) % count) for i in range(count)])  0.83 us
    pallas_call x1, Pallas kernels, on_device(): pl.pallas_call(lambda *refs: near_kernel(factor, *refs), out_shape=result...  0.77 us
    pallas_call x1, Pallas kernels, on_device(): pl.pallas_call(lambda *refs: far_kernel(factor, *refs), out_shape=result,...  0.77 us
    pallas_call x2, Pallas kernels, side(): pl.pallas_call(kernel, out_shape=half, in_specs=[VMEM] * len(operands), o...  0.7 us
  transfers between devices with their start and end apart: 4, of which 2 were waited for; matrix products, arithmetic and copies ran while one was open for 0% of the time, Pallas kernels for 19%

profile of v12, /device:TPU:0, one launch (start us, length us, event | category | flops | bytes accessed | tf_op | source)
XLA Modules:
  0.0 12.1 jit_solution(3176977054742090691)
XLA Ops:
  0.0 1.5 %pack.1 = (s32[19,8,128]{2,1,0:T(8,128)S(1)}, s32[19,8,128]{2,1,0:T(8,128)S(1)}, f32[2,8,8,512]{3,2,1,0:T(8,128)S(1)}, s32[8,512]{1,0:T(8,128)S(1)}, f32[2,8]{1,...) custom-call(f32[2,8,8,512]{3,2,1,0:T(8,128)} %controls.1, ...), custom_call_target="tpu_custom_call" | custom-call | tf_op jit(solution)/shard_map/pack/pallas_call | solution.py:494
  1.5 0.1 collective-permute-start
  1.6 2.5 %collective-permute-start.1 = (s32[19,8,128]{2,1,0:T(8,128)S(1)}, s32[19,8,128]{2,1,0:T(8,128)S(1)}, u32[]{:S(2)}, u32[]{:S(2)}) collective-permute-start(s32[19,8,128]{2,1,0:T(8,128)S(1)} %get-tuple-element.30), channel_id=1, source_target_pairs={{2,4},{3,5},{6,8},{7,9},{10,12},{11,13},{14,16},{15,17},{18,20},{1... | collective-permute-start | bytes 233480 | tf_op jit(solution)/shard_map/ppermute | solution.py:55
  4.1 0.0 collective-permute-done.packet
  4.1 0.4 %inner_rows.1.refs_2_ = bf16[2,4,8,512]{3,2,1,0:T(8,128)(2,1)S(1)} custom-call(f32[2,8,8,512]{3,2,1,0:T(8,128)S(1)} %get-tuple-element.20.controls, s32[19,8,128]{2,1,0:T(8,128)S(1)} %collective-permute-done.packet, f32[2,2,7,8,512]{4,3,2,1,0:T(8,128)S(1)} %get-tuple-element.27.kept, f32[2,17,8,512]{3,2,1,0:T(8,128)S(1)} %get-tuple-element.28.coef, ...), custom_call_target="tpu_custom_call" | custom-call | flops 1 | bytes 1 | tf_op jit(solution)/shard_map/inner_rows/pallas_call | solution.py:529
  4.6 0.0 copy-start
  4.6 1.3 %collective-permute-start.3 = (bf16[2,4,8,512]{3,2,1,0:T(8,128)(2,1)S(1)}, bf16[2,4,8,512]{3,2,1,0:T(8,128)(2,1)S(1)}, u32[]{:S(2)}, u32[]{:S(2)}) collective-permute-start(bf16[2,4,8,512]{3,2,1,0:T(8,128)(2,1)S(1)} %inner_rows.1.refs_2_), channel_id=1, source_target_pairs={{0,1},{1,0},{2,3},{3,2},{4,5},{5,4},{6,7},{7,6},{8,9},{9,8},{10,11... | collective-permute-start | bytes 196616 | tf_op jit(solution)/shard_map/ppermute | solution.py:545
  5.8 0.7 %collective-permute-done.1.packet = s32[19,8,128]{2,1,0:T(8,128)S(1)} collective-permute-done((s32[19,8,128]{2,1,0:T(8,128)S(1)}, s32[19,8,128]{2,1,0:T(8,128)S(1)}, u32[]{:S(2)}, u32[]{:S(2)}) %collective-permute-start.1) | collective-permute-done | bytes 77856 | tf_op jit(solution)/shard_map/ppermute | solution.py:55
  6.5 0.3 %outer_rows.1.refs_3_ = bf16[2,4,8,512]{3,2,1,0:T(8,128)(2,1)S(1)} custom-call(f32[2,8,8,512]{3,2,1,0:T(8,128)S(1)} %get-tuple-element.20.controls, s32[19,8,128]{2,1,0:T(8,128)S(1)} %collective-permute-done.1.packet, f32[2,2,7,8,512]{4,3,2,1,0:T(8,128)S(1)} %get-tuple-element.27.kept, f32[2,17,8,512]{3,2,1,0:T(8,128)S(1)} %get-tuple-element.28.coef, ...), custom_call_target="tpu_custom_call" | custom-call | flops 1 | bytes 1 | tf_op jit(solution)/shard_map/outer_rows/pallas_call | solution.py:529
  6.8 0.0 copy-start.1
  6.8 2.1 %collective-permute-start.2 = (bf16[2,4,8,512]{3,2,1,0:T(8,128)(2,1)S(1)}, bf16[2,4,8,512]{3,2,1,0:T(8,128)(2,1)S(1)}, u32[]{:S(2)}, u32[]{:S(2)}) collective-permute-start(bf16[2,4,8,512]{3,2,1,0:T(8,128)(2,1)S(1)} %outer_rows.1.refs_3_), channel_id=1, source_target_pairs={{0,1},{1,0},{2,3},{3,2},{4,5},{5,4},{6,7},{7,6},{8,9},{9,8},{10,11... | collective-permute-start | bytes 196616 | tf_op jit(solution)/shard_map/ppermute | solution.py:545
  8.9 0.0 copy-done
  8.9 0.0 copy-done.1
  8.9 0.9 %own_products.1 = (f32[4,4,8,512]{3,2,1,0:T(8,128)S(1)}, f32[4,4,8,512]{3,2,1,0:T(8,128)S(1)}, bf16[2,4,4,8,512]{4,3,2,1,0:T(8,128)(2,1)S(1)}, bf16[2,4,4,8,512]{4,3,2,1,0:T(8,128)(2,1)S(1)}) custom-call(bf16[4,4,8,8,512]{4,3,2,1,0:T(8,128)(2,1)S(1)} %bitcast.2, s32[4]{0:T(128)S(1)} %copy-done.1, bf16[2,4,8,512]{3,2,1,0:T(8,128)(2,1)S(1)} %inner_rows.1.refs_2_, ...), custom_call_target="tpu_custom_call" | custom-call | flops 4000000 | bytes 2000000 | tf_op jit(solution)/shard_map/own_products/pallas_call | solution.py:556
  9.7 0.0 collective-permute-done.3.refs_2_
  9.8 0.8 %near_products.1.refs_3_ = f32[4,8,8,512]{3,2,1,0:T(8,128)} custom-call(f32[4,4,8,512]{3,2,1,0:T(8,128)S(1)} %get-tuple-element.33.refs_0_, bf16[2,4,4,8,512]{4,3,2,1,0:T(8,128)(2,1)S(1)} %get-tuple-element.34.refs_1_, bf16[2,4,8,512]{3,2,1,0:T(8,128)(2,1)S(1)} %collective-permute-done.3.refs_2_), custom_call_target="tpu_custom_call" | custom-call | flops 1000000 | bytes 1000000 | tf_op jit(solution)/shard_map/near_products/pallas_call | solution.py:568
  10.5 0.8 %collective-permute-done.2.refs_2_ = bf16[2,4,8,512]{3,2,1,0:T(8,128)(2,1)S(1)} collective-permute-done((bf16[2,4,8,512]{3,2,1,0:T(8,128)(2,1)S(1)}, bf16[2,4,8,512]{3,2,1,0:T(8,128)(2,1)S(1)}, u32[]{:S(2)}, u32[]{:S(2)}) %collective-permute-start.2) | collective-permute-done | bytes 65568 | tf_op jit(solution)/shard_map/ppermute | solution.py:545
  11.4 0.8 %far_products.1 = f32[4,8,8,512]{3,2,1,0:T(8,128)} custom-call(f32[4,4,8,512]{3,2,1,0:T(8,128)S(1)} %get-tuple-element.31.refs_0_, bf16[2,4,4,8,512]{4,3,2,1,0:T(8,128)(2,1)S(1)} %get-tuple-element.32.refs_1_, bf16[2,4,8,512]{3,2,1,0:T(8,128)(2,1)S(1)} %collective-permute-done.2.refs_2_, ...), custom_call_target="tpu_custom_call", output_to_operand_aliasing={{}: (3, {})} | custom-call | flops 1000000 | bytes 1000000 | tf_op jit(solution)/shard_map/far_products/pallas_call | solution.py:578
  (1 shorter events, 0.0 us)
Async XLA Ops:
  1.5 2.6 %collective-permute-start = (s32[19,8,128]{2,1,0:T(8,128)S(1)}, s32[19,8,128]{2,1,0:T(8,128)S(1)}, u32[]{:S(2)}, u32[]{:S(2)}) collective-permute-start(s32[19,8,128]{2,1,0:T(8,128)S(1)} %get-tuple-element.21), channel_id=1, source_target_pairs={{0,2},{4,6},{8,10},{12,14},{16,18},{20,22},{24,26},{28,30},{2,0},{... | collective-permute-start | bytes 233480 | tf_op jit(solution)/shard_map/ppermute | solution.py:47
  1.6 4.9 %collective-permute-start.1 = (s32[19,8,128]{2,1,0:T(8,128)S(1)}, s32[19,8,128]{2,1,0:T(8,128)S(1)}, u32[]{:S(2)}, u32[]{:S(2)}) collective-permute-start(s32[19,8,128]{2,1,0:T(8,128)S(1)} %get-tuple-element.30), channel_id=1, source_target_pairs={{2,4},{3,5},{6,8},{7,9},{10,12},{11,13},{14,16},{15,17},{18,20},{1... | collective-permute-start | bytes 233480 | tf_op jit(solution)/shard_map/ppermute | solution.py:55
  4.6 4.3 %copy-start = (bf16[1,4,4,8,8,512]{5,4,3,2,1,0:T(8,128)(2,1)S(1)}, bf16[1,4,4,8,8,512]{5,4,3,2,1,0:T(8,128)(2,1)}, u32[]{:S(2)}) copy-start(bf16[1,4,4,8,8,512]{5,4,3,2,1,0:T(8,128)(2,1)} %param.6) | copy-start | bytes 3145732
  4.6 5.2 %collective-permute-start.3 = (bf16[2,4,8,512]{3,2,1,0:T(8,128)(2,1)S(1)}, bf16[2,4,8,512]{3,2,1,0:T(8,128)(2,1)S(1)}, u32[]{:S(2)}, u32[]{:S(2)}) collective-permute-start(bf16[2,4,8,512]{3,2,1,0:T(8,128)(2,1)S(1)} %inner_rows.1.refs_2_), channel_id=1, source_target_pairs={{0,1},{1,0},{2,3},{3,2},{4,5},{5,4},{6,7},{7,6},{8,9},{9,8},{10,11... | collective-permute-start | bytes 196616 | tf_op jit(solution)/shard_map/ppermute | solution.py:545
  6.8 2.1 %copy-start.1 = (s32[4]{0:T(128)S(1)}, s32[4]{0:T(128)}, u32[]{:S(2)}) copy-start(s32[4]{0:T(128)} %refs_1_.1) | copy-start | bytes 52
  6.8 4.6 %collective-permute-start.2 = (bf16[2,4,8,512]{3,2,1,0:T(8,128)(2,1)S(1)}, bf16[2,4,8,512]{3,2,1,0:T(8,128)(2,1)S(1)}, u32[]{:S(2)}, u32[]{:S(2)}) collective-permute-start(bf16[2,4,8,512]{3,2,1,0:T(8,128)(2,1)S(1)} %outer_rows.1.refs_3_), channel_id=1, source_target_pairs={{0,1},{1,0},{2,3},{3,2},{4,5},{5,4},{6,7},{7,6},{8,9},{9,8},{10,11... | collective-permute-start | bytes 196616 | tf_op jit(solution)/shard_map/ppermute | solution.py:545

commit v13 on v11

--- a/solution.py
+++ b/solution.py
@@ -157,12 +157,12 @@
 
     def code(side, k):
         if side == OUTER and k == 0:
-            for copy in own:
-                copy.wait()
+            own[0].wait()
         return codes[pl.ds(row_of(side, odd, k), 1), :] + 1
 
     for side, packet, arriving in ((OUTER, across, outer), (INNER, within, inner)):
         encode(slots, functools.partial(read, side, arriving), functools.partial(code, side), packet)
+    own[1].wait()
 
 
 def by_level(table, kind, shape):

time: 12.3 us -> 12.3 us (level)
  no operation moved by 1% of the time
where the time goes in v13:
time: 12.3 us; the launch traced here: 12.1 us
  starting transfers between devices  5.91 us (48%)
  Pallas kernels  4.63 us (38%)
  waiting for transfers between devices  1.5 us (12%)
    ppermute x2, starting transfers between devices, shift(): lax.ppermute(value, 'tm', [(i, (i + step) % count) for i in range(count)])  2.8 us
    ppermute x1, starting transfers between devices, swap_across(): return lax.ppermute(value, ('tile', 'tm'), flat + [(b, a) for a, b in flat])  2.59 us
    pallas_call x1, Pallas kernels, on_device(): pl.pallas_call(pack_kernel, out_shape=(packet, packet, pltpu.VMEM(control...  0.99 us
    pallas_call x1, Pallas kernels, on_device(): pl.pallas_call(lambda *refs: own_kernel(factor, *refs), out_shape=(part,...  0.87 us
    ppermute x2, waiting for transfers between devices, shift(): lax.ppermute(value, 'tm', [(i, (i + step) % count) for i in range(count)])  0.83 us
    pallas_call x1, Pallas kernels, on_device(): pl.pallas_call(lambda *refs: near_kernel(factor, *refs), out_shape=result...  0.77 us
    pallas_call x1, Pallas kernels, on_device(): pl.pallas_call(lambda *refs: far_kernel(factor, *refs), out_shape=result,...  0.77 us
    pallas_call x2, Pallas kernels, side(): pl.pallas_call(kernel, out_shape=half, in_specs=[VMEM] * len(operands), o...  0.7 us
  transfers between devices with their start and end apart: 4, of which 2 were waited for; matrix products, arithmetic and copies ran while one was open for 0% of the time, Pallas kernels for 24%

profile of v13, /device:TPU:0, one launch (start us, length us, event | category | flops | bytes accessed | tf_op | source)
XLA Modules:
  0.0 12.1 jit_solution(14457993134945557677)
XLA Ops:
  0.0 1.0 %pack.1 = (s32[19,8,128]{2,1,0:T(8,128)S(1)}, s32[19,8,128]{2,1,0:T(8,128)S(1)}, f32[2,8,8,512]{3,2,1,0:T(8,128)S(1)}, s32[8,512]{1,0:T(8,128)S(1)}, f32[2,8]{1,0:T(2,128)S(1)}) custom-call(f32[2,8,8,512]{3,2,1,0:T(8,128)} %controls.1, s32[8,512]{1,0:T(8,128)} %mask.1, f32[2,8]{1,0:T(2,128)} %diffusivity.1), custom_call_target="tpu_custom_call" | custom-call | tf_op jit(solution)/shard_map/pack/pallas_call | solution.py:468
  1.0 0.5 %collective-permute-start = (s32[19,8,128]{2,1,0:T(8,128)S(1)}, s32[19,8,128]{2,1,0:T(8,128)S(1)}, u32[]{:S(2)}, u32[]{:S(2)}) collective-permute-start(s32[19,8,128]{2,1,0:T(8,128)S(1)} %get-tuple-element.18), channel_id=1, source_target_pairs={{0,2},{4,6},{8,10},{12,14},{16,18},{20,22},{24,26},{28,30},{2,0},{... | collective-permute-start | bytes 233480 | tf_op jit(solution)/shard_map/ppermute | solution.py:47
  1.5 2.6 %collective-permute-start.1 = (s32[19,8,128]{2,1,0:T(8,128)S(1)}, s32[19,8,128]{2,1,0:T(8,128)S(1)}, u32[]{:S(2)}, u32[]{:S(2)}) collective-permute-start(s32[19,8,128]{2,1,0:T(8,128)S(1)} %get-tuple-element.24), channel_id=1, source_target_pairs={{2,4},{3,5},{6,8},{7,9},{10,12},{11,13},{14,16},{15,17},{18,20},{1... | collective-permute-start | bytes 233480 | tf_op jit(solution)/shard_map/ppermute | solution.py:55
  4.1 0.5 %middle.1 = (f32[2,2,7,8,512]{4,3,2,1,0:T(8,128)S(1)}, f32[2,17,8,512]{3,2,1,0:T(8,128)S(1)}, f32[2,8,512]{2,1,0:T(8,128)S(1)}) custom-call(f32[2,8,8,512]{3,2,1,0:T(8,128)S(1)} %get-tuple-element.17.controls, s32[8,512]{1,0:T(8,128)S(1)} %get-tuple-element.19.codes, f32[2,8]{1,0:T(2,128)S(1)} %get-tuple-element.20.table), custom_call_target="tpu_custom_call" | custom-call | flops 1 | bytes 1 | tf_op jit(solution)/shard_map/middle/pallas_call | solution.py:491
  4.6 0.0 collective-permute-done.packet
  4.7 0.4 %inner_rows.1.refs_2_ = bf16[2,4,8,512]{3,2,1,0:T(8,128)(2,1)S(1)} custom-call(f32[2,8,8,512]{3,2,1,0:T(8,128)S(1)} %get-tuple-element.17.controls, s32[19,8,128]{2,1,0:T(8,128)S(1)} %collective-permute-done.packet, f32[2,2,7,8,512]{4,3,2,1,0:T(8,128)S(1)} %get-tuple-element.21.kept, f32[2,17,8,512]{3,2,1,0:T(8,128)S(1)} %get-tuple-element.22.coef, ...), custom_call_target="tpu_custom_call" | custom-call | flops 1 | bytes 1 | tf_op jit(solution)/shard_map/inner_rows/pallas_call | solution.py:508
  5.1 0.0 copy-start
  5.1 0.7 %collective-permute-start.3 = (bf16[2,4,8,512]{3,2,1,0:T(8,128)(2,1)S(1)}, bf16[2,4,8,512]{3,2,1,0:T(8,128)(2,1)S(1)}, u32[]{:S(2)}, u32[]{:S(2)}) collective-permute-start(bf16[2,4,8,512]{3,2,1,0:T(8,128)(2,1)S(1)} %inner_rows.1.refs_2_), channel_id=1, source_target_pairs={{0,1},{1,0},{2,3},{3,2},{4,5},{5,4},{6,7},{7,6},{8,9},{9,8},{10,11... | collective-permute-start | bytes 196616 | tf_op jit(solution)/shard_map/ppermute | solution.py:524
  5.8 0.7 %collective-permute-done.1.packet = s32[19,8,128]{2,1,0:T(8,128)S(1)} collective-permute-done((s32[19,8,128]{2,1,0:T(8,128)S(1)}, s32[19,8,128]{2,1,0:T(8,128)S(1)}, u32[]{:S(2)}, u32[]{:S(2)}) %collective-permute-start.1) | collective-permute-done | bytes 77856 | tf_op jit(solution)/shard_map/ppermute | solution.py:55
  6.5 0.3 %outer_rows.1.refs_3_ = bf16[2,4,8,512]{3,2,1,0:T(8,128)(2,1)S(1)} custom-call(f32[2,8,8,512]{3,2,1,0:T(8,128)S(1)} %get-tuple-element.17.controls, s32[19,8,128]{2,1,0:T(8,128)S(1)} %collective-permute-done.1.packet, f32[2,2,7,8,512]{4,3,2,1,0:T(8,128)S(1)} %get-tuple-element.21.kept, f32[2,17,8,512]{3,2,1,0:T(8,128)S(1)} %get-tuple-element.22.coef, ...), custom_call_target="tpu_custom_call" | custom-call | flops 1 | bytes 1 | tf_op jit(solution)/shard_map/outer_rows/pallas_call | solution.py:508
  6.8 0.0 copy-start.1
  6.8 2.1 %collective-permute-start.2 = (bf16[2,4,8,512]{3,2,1,0:T(8,128)(2,1)S(1)}, bf16[2,4,8,512]{3,2,1,0:T(8,128)(2,1)S(1)}, u32[]{:S(2)}, u32[]{:S(2)}) collective-permute-start(bf16[2,4,8,512]{3,2,1,0:T(8,128)(2,1)S(1)} %outer_rows.1.refs_3_), channel_id=1, source_target_pairs={{0,1},{1,0},{2,3},{3,2},{4,5},{5,4},{6,7},{7,6},{8,9},{9,8},{10,11... | collective-permute-start | bytes 196616 | tf_op jit(solution)/shard_map/ppermute | solution.py:524
  8.9 0.0 copy-done
  8.9 0.0 copy-done.1
  8.9 0.9 %own_products.1 = (f32[4,4,8,512]{3,2,1,0:T(8,128)S(1)}, f32[4,4,8,512]{3,2,1,0:T(8,128)S(1)}, bf16[2,4,4,8,512]{4,3,2,1,0:T(8,128)(2,1)S(1)}, bf16[2,4,4,8,512]{4,3,2,1,0:T(8,128)(2,1)S(1)}) custom-call(bf16[4,4,8,8,512]{4,3,2,1,0:T(8,128)(2,1)S(1)} %bitcast.2, s32[4]{0:T(128)S(1)} %copy-done.1, bf16[2,4,8,512]{3,2,1,0:T(8,128)(2,1)S(1)} %inner_rows.1.refs_2_, ...), custom_call_target="tpu_custom_call" | custom-call | flops 4000000 | bytes 2000000 | tf_op jit(solution)/shard_map/own_products/pallas_call | solution.py:535
  9.7 0.0 collective-permute-done.3.refs_2_
  9.8 0.8 %near_products.1.refs_3_ = f32[4,8,8,512]{3,2,1,0:T(8,128)} custom-call(f32[4,4,8,512]{3,2,1,0:T(8,128)S(1)} %get-tuple-element.27.refs_0_, bf16[2,4,4,8,512]{4,3,2,1,0:T(8,128)(2,1)S(1)} %get-tuple-element.28.refs_1_, bf16[2,4,8,512]{3,2,1,0:T(8,128)(2,1)S(1)} %collective-permute-done.3.refs_2_), custom_call_target="tpu_custom_call" | custom-call | flops 1000000 | bytes 1000000 | tf_op jit(solution)/shard_map/near_products/pallas_call | solution.py:547
  10.5 0.8 %collective-permute-done.2.refs_2_ = bf16[2,4,8,512]{3,2,1,0:T(8,128)(2,1)S(1)} collective-permute-done((bf16[2,4,8,512]{3,2,1,0:T(8,128)(2,1)S(1)}, bf16[2,4,8,512]{3,2,1,0:T(8,128)(2,1)S(1)}, u32[]{:S(2)}, u32[]{:S(2)}) %collective-permute-start.2) | collective-permute-done | bytes 65568 | tf_op jit(solution)/shard_map/ppermute | solution.py:524
  11.4 0.8 %far_products.1 = f32[4,8,8,512]{3,2,1,0:T(8,128)} custom-call(f32[4,4,8,512]{3,2,1,0:T(8,128)S(1)} %get-tuple-element.25.refs_0_, bf16[2,4,4,8,512]{4,3,2,1,0:T(8,128)(2,1)S(1)} %get-tuple-element.26.refs_1_, bf16[2,4,8,512]{3,2,1,0:T(8,128)(2,1)S(1)} %collective-permute-done.2.refs_2_, ...), custom_call_target="tpu_custom_call", output_to_operand_aliasing={{}: (3, {})} | custom-call | flops 1000000 | bytes 1000000 | tf_op jit(solution)/shard_map/far_products/pallas_call | solution.py:557
Async XLA Ops:
  1.0 3.6 %collective-permute-start = (s32[19,8,128]{2,1,0:T(8,128)S(1)}, s32[19,8,128]{2,1,0:T(8,128)S(1)}, u32[]{:S(2)}, u32[]{:S(2)}) collective-permute-start(s32[19,8,128]{2,1,0:T(8,128)S(1)} %get-tuple-element.18), channel_id=1, source_target_pairs={{0,2},{4,6},{8,10},{12,14},{16,18},{20,22},{24,26},{28,30},{2,0},{... | collective-permute-start | bytes 233480 | tf_op jit(solution)/shard_map/ppermute | solution.py:47
  1.5 5.0 %collective-permute-start.1 = (s32[19,8,128]{2,1,0:T(8,128)S(1)}, s32[19,8,128]{2,1,0:T(8,128)S(1)}, u32[]{:S(2)}, u32[]{:S(2)}) collective-permute-start(s32[19,8,128]{2,1,0:T(8,128)S(1)} %get-tuple-element.24), channel_id=1, source_target_pairs={{2,4},{3,5},{6,8},{7,9},{10,12},{11,13},{14,16},{15,17},{18,20},{1... | collective-permute-start | bytes 233480 | tf_op jit(solution)/shard_map/ppermute | solution.py:55
  5.1 3.8 %copy-start = (bf16[1,4,4,8,8,512]{5,4,3,2,1,0:T(8,128)(2,1)S(1)}, bf16[1,4,4,8,8,512]{5,4,3,2,1,0:T(8,128)(2,1)}, u32[]{:S(2)}) copy-start(bf16[1,4,4,8,8,512]{5,4,3,2,1,0:T(8,128)(2,1)} %param.6) | copy-start | bytes 3145732
  5.1 4.6 %collective-permute-start.3 = (bf16[2,4,8,512]{3,2,1,0:T(8,128)(2,1)S(1)}, bf16[2,4,8,512]{3,2,1,0:T(8,128)(2,1)S(1)}, u32[]{:S(2)}, u32[]{:S(2)}) collective-permute-start(bf16[2,4,8,512]{3,2,1,0:T(8,128)(2,1)S(1)} %inner_rows.1.refs_2_), channel_id=1, source_target_pairs={{0,1},{1,0},{2,3},{3,2},{4,5},{5,4},{6,7},{7,6},{8,9},{9,8},{10,11... | collective-permute-start | bytes 196616 | tf_op jit(solution)/shard_map/ppermute | solution.py:524
  6.8 2.1 %copy-start.1 = (s32[4]{0:T(128)S(1)}, s32[4]{0:T(128)}, u32[]{:S(2)}) copy-start(s32[4]{0:T(128)} %refs_1_.1) | copy-start | bytes 52
  6.8 4.6 %collective-permute-start.2 = (bf16[2,4,8,512]{3,2,1,0:T(8,128)(2,1)S(1)}, bf16[2,4,8,512]{3,2,1,0:T(8,128)(2,1)S(1)}, u32[]{:S(2)}, u32[]{:S(2)}) collective-permute-start(bf16[2,4,8,512]{3,2,1,0:T(8,128)(2,1)S(1)} %outer_rows.1.refs_3_), channel_id=1, source_target_pairs={{0,1},{1,0},{2,3},{3,2},{4,5},{5,4},{6,7},{7,6},{8,9},{9,8},{10,11... | collective-permute-start | bytes 196616 | tf_op jit(solution)/shard_map/ppermute | solution.py:524
